TPU v7x, 256 devices: a whole 4x4x8 slice. The times are simulated.
256 devices in a mesh: member: 16 (over z, x_hi), band: 16 (over x_lo, y, core).
Axes of the slice: x: 4 (x_hi: 2, x_lo: 2; x = x_hi * 2 + x_lo), y: 4, z: 8, core: 2. Of those that a mesh axis runs over, the one named last changes fastest.
Arguments:
- copy_fields: bfloat16 [16, 240, 384, 480], P('member', 'band'), may hold values from -6 to 6
- norm_gain: float32 [384], replicated, may hold values from 0.25 to 1.75
- mix_real: bfloat16 [384, 384], replicated, may hold values from -0.21875 to 0.21875
- mix_imag: bfloat16 [384, 384], replicated, may hold values from -0.21875 to 0.21875
- filter_bank: float32 [32, 240], replicated, may hold values from 0.5 to 1.5
- perturbation_draw_numbers: int32 [16], P('member'), may hold values from 0 to 31
- amplitudes: float32 [8], replicated, may hold values from 0.2 to 1
- desired_magnitude_slot: int32 [16], P('member'), may hold values from 0 to 7
Outputs:
- bred: bfloat16 [16, 240, 384, 480], P('member', 'band')
All inputs are finite; a program needn't handle non-finite values.
Results may differ from a plain program's by a relative error of at most 0.007.
Values may be sent and summed in bfloat16 or wider, within the bound.
No kernel may reach another device: no remote copies, remote signals or barrier semaphores. Data moves between devices by JAX's collectives and lax.ppermute only.
A program may use at most 128 MiB of HBM per device.

v0:
```python
import math

import jax
import jax.numpy as jnp
import numpy as np
from jax import lax
from jax.sharding import PartitionSpec as P

H = 240
W = 480
M = 240
L = 240


def broadcast(value, axis, source):
    kept = jnp.where(lax.axis_index(axis) == source, value, 0).astype(value.dtype)
    return lax.psum(kept, axis)


def legendre_table(degree_count, order_count, lat_count):
    colatitude = (np.arange(lat_count) + 0.5) * np.pi / lat_count
    cosines = np.cos(colatitude)
    sines = np.sin(colatitude)
    orders = np.arange(order_count)[:, None] * 1.0
    steps_up = np.arange(1, order_count) * 1.0
    log_factor = np.concatenate(
        [[0.0], np.cumsum(np.log((2.0 * steps_up - 1.0) / (2.0 * steps_up)))]
    )
    diagonal_start = np.exp(
        0.5 * np.log((2.0 * orders + 1.0) / 2.0)
        + 0.5 * log_factor[:, None]
        + orders * np.log(sines)[None, :]
    )
    result = np.zeros((order_count, degree_count, lat_count))
    previous = np.zeros(diagonal_start.shape)
    before_previous = np.zeros(diagonal_start.shape)
    for degree in range(degree_count):
        lower = degree - 1.0
        rising = np.sqrt(
            np.maximum(4.0 * degree * degree - 1.0, 1.0)
            / np.maximum(degree * degree - orders * orders, 1.0)
        )
        falling = np.sqrt(
            np.maximum(lower * lower - orders * orders, 0.0) / max(4.0 * lower * lower - 1.0, 1.0)
        )
        current = np.where(
            orders == degree,
            diagonal_start,
            np.where(
                degree > orders,
                rising * (cosines[None, :] * previous - falling * before_previous),
                0.0,
            ),
        )
        result[:, degree] = current
        before_previous = previous
        previous = current
    return result


def fourier_tables(lon_count, mode_order):
    longitude = 2.0 * np.pi * np.arange(lon_count)[:, None] / lon_count
    angles = longitude * (mode_order[None, :] * 1.0)
    forward_factor = math.sqrt(2.0 * math.pi) / lon_count
    forward_table = np.stack(
        [forward_factor * np.cos(angles), -forward_factor * np.sin(angles)], axis=1
    )
    inverse_factor = np.where(mode_order == 0, 1.0, 2.0) / math.sqrt(2.0 * math.pi)
    inverse_table = np.stack(
        [
            (inverse_factor[None, :] * np.cos(angles)).T,
            (-inverse_factor[None, :] * np.sin(angles)).T,
        ],
        axis=0,
    )
    return (forward_table, inverse_table)


def latitude_weights(lat_count):
    colatitude = (jnp.arange(lat_count, dtype=jnp.float32) + 0.5) * (math.pi / lat_count)
    return jnp.sin(colatitude) * (math.pi / lat_count)


def spectral_pass(legendre_part, fourier_part, gain_part, mixing_matrix):
    coeffs = jnp.einsum(
        "mlj,mjc->mlc", legendre_part, fourier_part, preferred_element_type=jnp.float32
    ).astype(jnp.bfloat16)
    mode_count, degree_count, channel_count = coeffs.shape
    mixed_values = jnp.dot(
        coeffs.reshape(mode_count * degree_count, channel_count),
        mixing_matrix,
        preferred_element_type=jnp.float32,
    )
    mixed_values = (
        mixed_values.reshape(mode_count, degree_count, channel_count) * gain_part[None, :, None]
    ).astype(jnp.bfloat16)
    return jnp.einsum(
        "mlj,mlc->mjc", legendre_part, mixed_values, preferred_element_type=jnp.float32
    ).astype(jnp.bfloat16)


def shards(
    copy_fields,
    norm_gain,
    mix_real,
    mix_imag,
    filter_bank,
    perturbation_draw_numbers,
    amplitudes,
    desired_magnitude_slot,
):
    band_count = lax.axis_size("band")
    band_index = lax.axis_index("band")
    lat_rows = copy_fields.shape[1]
    channels = copy_fields.shape[2]
    mode_rows = M // band_count
    mode_order = np.arange(M)
    forward_np, inverse_np = fourier_tables(W, mode_order)
    forward_table = jnp.asarray(forward_np, jnp.float32).astype(jnp.bfloat16)
    inverse_table = jnp.asarray(inverse_np, jnp.float32).astype(jnp.bfloat16)
    legendre_all = jnp.asarray(legendre_table(L, M, H)[mode_order], jnp.float32).astype(
        jnp.bfloat16
    )
    legendre_all = legendre_all.reshape(band_count, mode_rows, L, H)
    own_table = lax.dynamic_index_in_dim(legendre_all, band_index, 0, keepdims=False)
    global_rows = band_index * lat_rows + jnp.arange(lat_rows, dtype=jnp.int32)
    colatitude = (global_rows.astype(jnp.float32) + 0.5) * (math.pi / H)
    weights = jnp.sin(colatitude) * (math.pi / H)
    total_weight = jnp.sum(latitude_weights(H)) * (channels * W)
    broadened_fields = copy_fields[0].astype(jnp.float32)
    average = jnp.mean(broadened_fields, axis=1, keepdims=True)
    variance = jnp.mean(jnp.square(broadened_fields - average), axis=1, keepdims=True)
    normed = (
        (broadened_fields - average) * lax.rsqrt(variance + 1e-05) * norm_gain[None, :, None]
    ).astype(jnp.bfloat16)
    fourier = jnp.einsum("jew,wrm->mjre", normed, forward_table, preferred_element_type=jnp.float32)
    fourier = (fourier * weights[None, :, None, None]).astype(jnp.bfloat16)
    moved = lax.all_to_all(fourier, "band", split_axis=0, concat_axis=1, tiled=True)
    moved = moved.reshape(mode_rows, H, 2 * channels)
    bank_rows = filter_bank.shape[0]
    seed_onehot = (jnp.arange(bank_rows, dtype=jnp.int32) == perturbation_draw_numbers[0]).astype(
        jnp.float32
    )
    degree_gain = jnp.dot(seed_onehot, filter_bank, precision=lax.Precision.HIGHEST)
    mixing_matrix = jnp.concatenate(
        [jnp.concatenate([mix_real, mix_imag], 1), jnp.concatenate([-mix_imag, mix_real], 1)], 0
    )
    returned = spectral_pass(own_table, moved, degree_gain, mixing_matrix)
    returned = returned.reshape(mode_rows, H, 2, channels)
    split_ensemble_copy = jax.nn.gelu(
        jnp.einsum(
            "mjre,rmw->jew",
            lax.all_to_all(returned, "band", split_axis=1, concat_axis=0, tiled=True),
            inverse_table,
            preferred_element_type=jnp.float32,
        )
    )
    predicted_field = (broadened_fields + split_ensemble_copy).astype(jnp.bfloat16)
    unperturbed_field = broadcast(predicted_field, "member", 0)
    copy_minus_unperturbed = lax.optimization_barrier(predicted_field).astype(
        jnp.float32
    ) - unperturbed_field.astype(jnp.float32)
    partial_sum = jnp.sum(weights[:, None, None] * copy_minus_unperturbed * copy_minus_unperturbed)
    spread_sum = lax.psum(partial_sum, "band")
    spread = spread_sum / total_weight
    level_count = amplitudes.shape[0]
    target = jnp.sum(
        jnp.where(
            jnp.arange(level_count, dtype=jnp.int32) == desired_magnitude_slot[0], amplitudes, 0.0
        )
    )
    rescale = target / jnp.sqrt(spread + 1e-06)
    bred = (unperturbed_field.astype(jnp.float32) + rescale * copy_minus_unperturbed).astype(
        jnp.bfloat16
    )
    return bred[None]


def solution(mesh):
    in_specs = (P("member", "band", None, None), P(), P(), P(), P(), P("member"), P(), P("member"))
    out_specs = P("member", "band", None, None)
    return jax.shard_map(shards, mesh=mesh, in_specs=in_specs, out_specs=out_specs, check_vma=False)
```

profile of v0, /device:TPU:1, one launch (start us, length us, event | category | flops | bytes accessed | tf_op | source)
XLA Modules:
  0.0 595.9 jit_solution(17415995898707282329)
XLA Ops:
  6.6 3.8 convert_reduce_fusion
  10.4 0.3 copy-done.2
  10.7 2.7 fusion.4
  13.5 5.5 fusion.17
  19.0 9.4 %copy.21 = bf16[240,15,2,384]{3,2,1,0:T(2,128)(2,1)} copy(bf16[240,15,2,384]{3,0,2,1:T(8,128)(2,1)S(1)} %fusion.17) | data formatting | bytes 11059200 | tf_op jit(solution)/shard_map/convert_element_type | solution.py:137
  28.4 7.7 %all-to-all-start = ((bf16[240,15,2,384]{3,2,1,0:T(2,128)(2,1)}), bf16[240,15,2,384]{3,2,1,0:T(2,128)(2,1)}, u32[]{:S(2)}, u32[]{:S(2)}) async-start(bf16[240,15,2,384]{3,2,1,0:T(2,128)(2,1)} %copy.21), calls=%async_computation | async-start | bytes 11059200 | tf_op jit(solution)/shard_map/all_to_all | solution.py:138
  37.0 72.8 %all-to-all-done = bf16[240,15,2,384]{3,2,1,0:T(2,128)(2,1)} async-done(((bf16[240,15,2,384]{3,2,1,0:T(2,128)(2,1)}), bf16[240,15,2,384]{3,2,1,0:T(2,128)(2,1)}, u32[]{:S(2)}, u32[]{:S(2)}) %all-to-all-start) | async-done | bytes 5529632 | tf_op jit(solution)/shard_map/all_to_all | solution.py:138
  109.8 6.1 %copy.22 = bf16[15,16,15,2,384]{4,3,2,1,0:T(2,128)(2,1)} copy(bf16[15,16,15,2,384]{4,3,2,0,1:T(2,128)(2,1)} %bitcast.7) | data formatting | bytes 11059200 | tf_op jit(solution)/shard_map/all_to_all | solution.py:138
  115.9 13.0 %reshape.48 = bf16[15,240,768]{2,1,0:T(8,128)(2,1)} reshape(bf16[15,16,15,2,384]{4,3,2,1,0:T(2,128)(2,1)} %copy.22) | data formatting | bytes 11059200 | tf_op jit(solution)/shard_map/reshape | solution.py:139
  128.9 13.3 %fusion.26 = f32[15,240,768]{2,1,0:T(8,128)} fusion(bf16[15,240,768]{2,1,0:T(8,128)(2,1)} %reshape.48, bf16[16,15,240,240]{3,2,1,0:T(8,128)(2,1)} %constant.56, s32[]{:T(128)S(6)} %select_n.17, bf16[384,384]{1,0:T(8,128)(2,1)S(1)} %copy-done.4, bf16[384,384]{1,0:T(8,128)(2,1)S(1)} %neg.3, bf16[384,384]{1,0:T(8,128)(2,1)S(1)} %copy-done.3), kind=kOutput, calls=%fused_computation.33 | convolution fusion | flops 5581320192 | bytes 19316740 | tf_op jit(solution)/shard_map/dot_general | solution.py:89
  142.1 8.9 %fusion.33 = bf16[15,240,768]{2,1,0:T(8,128)(2,1)} fusion(f32[15,240,768]{2,1,0:T(8,128)} %fusion.26, f32[240]{0:T(256)S(1)} %bitcast.68, bf16[16,15,240,240]{3,2,1,0:T(8,128)(2,1)} %constant.56, s32[]{:T(128)S(6)} %select_n.17), kind=kOutput, calls=%fused_computation.40 | convolution fusion | flops 1335398400 | bytes 18432964 | tf_op jit(solution)/shard_map/mlj,mlc->mjc/dot_general | solution.py:97
  151.0 11.6 %reshape.49 = bf16[15,240,2,384]{3,2,1,0:T(2,128)(2,1)} reshape(bf16[15,240,768]{2,1,0:T(8,128)(2,1)} %fusion.33) | data formatting | bytes 11059200 | tf_op jit(solution)/shard_map/reshape | solution.py:149
  162.5 6.2 %copy.24 = bf16[15,240,2,384]{3,2,0,1:T(2,128)(2,1)} copy(bf16[15,240,2,384]{3,2,1,0:T(2,128)(2,1)} %reshape.49) | data formatting | bytes 11059200 | tf_op jit(solution)/shard_map/reshape | solution.py:149
  168.8 13.4 %all-to-all-start.1 = ((bf16[15,240,2,384]{3,2,0,1:T(2,128)(2,1)}), bf16[15,240,2,384]{3,2,0,1:T(2,128)(2,1)}, u32[]{:S(2)}, u32[]{:S(2)}) async-start(bf16[15,240,2,384]{3,2,0,1:T(2,128)(2,1)} %copy.24), calls=%async_computation.1 | async-start | bytes 11059200 | tf_op jit(solution)/shard_map/all_to_all | solution.py:153
  182.2 0.3 all-reduce.2.cloned.1.call-start
  182.5 75.9 %all-to-all-done.1 = bf16[15,240,2,384]{3,2,0,1:T(2,128)(2,1)} async-done(((bf16[15,240,2,384]{3,2,0,1:T(2,128)(2,1)}), bf16[15,240,2,384]{3,2,0,1:T(2,128)(2,1)}, u32[]{:S(2)}, u32[]{:S(2)}) %all-to-all-start.1) | async-done | bytes 5529632 | tf_op jit(solution)/shard_map/all_to_all | solution.py:153
  258.3 5.2 copy.26
  263.5 11.2 %broadcast_select_fusion = (bf16[15,384,480]{1,2,0:T(8,128)(2,1)}, bf16[15,384,480]{1,2,0:T(8,128)(2,1)}) fusion(pred[]{:T(512)S(6)} %eq.15, bf16[2,240,480,1]{1,2,0,3:T(8,128)(2,1)S(1)} %copy-done.7, bf16[240,15,2,384]{3,2,1,0:T(2,128)(2,1)S(1)} %bitcast.67, bf16[1,15,384,480]{2,3,1,0:T(8,128)(2,1)} %param.11), kind=kOutput, calls=%fused_computation.38 | convolution fusion | flops 2687385600 | bytes 22579200 | tf_op jit(solution)/shard_map/mjre,rmw->jew/dot_general | solution.py:151
  275.4 0.7 multiply_reduce_fusion
  276.1 0.6 fusion.53
  276.7 265.6 %all-reduce.2.cloned.1.call-done = bf16[15,384,480]{1,2,0:T(8,128)(2,1)} async-done(((bf16[15,384,480]{1,2,0:T(8,128)(2,1)}), bf16[15,384,480]{1,2,0:T(8,128)(2,1)}) %all-reduce.2.cloned.1.call-update) | async-done | bytes 5529616 | tf_op jit(solution)/shard_map/psum | solution.py:17
  542.3 7.7 %fusion.16 = f32[]{:T(128)} fusion(bf16[15,384,480]{1,2,0:T(8,128)(2,1)} %all-reduce.2.cloned.1.call-done, bf16[15,384,480]{1,2,0:T(8,128)(2,1)} %get-tuple-element.6, f32[15]{0:T(128)S(1)} %sine_multiply_fusion), kind=kLoop, calls=%fused_computation.22 | loop fusion | flops 16588799 | bytes 11059264 | tf_op jit(solution)/shard_map/reduce_sum | solution.py:163
  550.6 28.4 %psum.15 = f32[]{:T(128)} all-reduce(f32[]{:T(128)} %fusion.16), channel_id=1, replica_groups=mesh['member'=16,'band'=16] {'band'}, use_global_device_ids=true, to_apply=%region_5.6 | all-reduce | flops 1 | bytes 8 | tf_op jit(solution)/shard_map/psum | solution.py:164
  580.4 8.7 %fusion.19 = bf16[1,15,384,480]{2,3,1,0:T(8,128)(2,1)} fusion(bf16[15,384,480]{1,2,0:T(8,128)(2,1)} %get-tuple-element.6, bf16[15,384,480]{1,2,0:T(8,128)(2,1)} %all-reduce.2.cloned.1.call-done, f32[]{:T(128)S(6)} %div.15), kind=kLoop, calls=%fused_computation.27 | loop fusion | flops 16588800 | bytes 16588804 | tf_op jit(solution)/shard_map/broadcast_in_dim | solution.py:176
  (23 shorter events, 0.3 us)
Async XLA Ops:
  6.5 30.3 %copy-start = (f32[32,240]{1,0:T(8,128)S(1)}, f32[32,240]{1,0:T(8,128)}, u32[]{:S(2)}) copy-start(f32[32,240]{1,0:T(8,128)} %param.15) | copy-start | bytes 92164
  6.5 4.2 copy-start.2
  6.6 6.9 %copy-start.5 = (f32[384]{0:T(512)S(1)}, f32[384]{0:T(512)}, u32[]{:S(2)}) copy-start(f32[384]{0:T(512)} %param.12) | copy-start | bytes 4612
  6.6 6.9 %copy-start.8 = (bf16[480,2,240,1]{0,2,1,3:T(8,128)(2,1)S(1)}, bf16[480,2,240,1]{0,2,1,3:T(8,128)(2,1)}, u32[]{:S(2)}) copy-start(bf16[480,2,240,1]{0,2,1,3:T(8,128)(2,1)} %constant.59) | copy-start | bytes 1382404
  28.4 7.7 %copy-start.3 = (bf16[384,384]{1,0:T(8,128)(2,1)S(1)}, bf16[384,384]{1,0:T(8,128)(2,1)}, u32[]{:S(2)}) copy-start(bf16[384,384]{1,0:T(8,128)(2,1)} %param.14) | copy-start | bytes 884740
  28.4 81.3 %all-to-all-start = ((bf16[240,15,2,384]{3,2,1,0:T(2,128)(2,1)}), bf16[240,15,2,384]{3,2,1,0:T(2,128)(2,1)}, u32[]{:S(2)}, u32[]{:S(2)}) async-start(bf16[240,15,2,384]{3,2,1,0:T(2,128)(2,1)} %copy.21), calls=%async_computation | async-start | bytes 11059200 | tf_op jit(solution)/shard_map/all_to_all | solution.py:138
  115.9 13.0 %copy-start.4 = (bf16[384,384]{1,0:T(8,128)(2,1)S(1)}, bf16[384,384]{1,0:T(8,128)(2,1)}, u32[]{:S(2)}) copy-start(bf16[384,384]{1,0:T(8,128)(2,1)} %param.13) | copy-start | bytes 884740
  168.8 89.5 %all-to-all-start.1 = ((bf16[15,240,2,384]{3,2,0,1:T(2,128)(2,1)}), bf16[15,240,2,384]{3,2,0,1:T(2,128)(2,1)}, u32[]{:S(2)}, u32[]{:S(2)}) async-start(bf16[15,240,2,384]{3,2,0,1:T(2,128)(2,1)} %copy.24), calls=%async_computation.1 | async-start | bytes 11059200 | tf_op jit(solution)/shard_map/all_to_all | solution.py:153
  182.2 360.1 %all-reduce.2.cloned.1.call-start = ((), (), s32[]{:S(2)}) async-start(), calls=%async_computation.2 | async-start | bytes 11059200 | tf_op jit(solution)/shard_map/psum | solution.py:17
  258.3 5.2 copy-start.7
  274.8 1.3 copy-start.6
  579.7 9.3 %copy-start.1 = (f32[32,240]{1,0:T(8,128)S(1)}, f32[32,240]{1,0:T(8,128)}, u32[]{:S(2)}) copy-start(f32[32,240]{1,0:T(8,128)} %param.15) | copy-start | bytes 92164
Sparse Core Ops, SparseCore 0:
  274.9 267.3 all-reduce.1
where the time goes:
time: 598 us; the launch traced here: 596 us
  waiting for transfers between devices  414 us (69%)
  local copies, waits for them, and re-layouts  51.8 us (9%)
  matrix products  39 us (7%)
  blocking collectives  28.4 us (5%)
  other arithmetic  24.3 us (4%)
  starting transfers between devices  21.4 us (4%)
  between operations  16.7 us (3%)
    psum x1, waiting for transfers between devices, broadcast(): return lax.psum(kept, axis)  266 us
    all_to_all x1, waiting for transfers between devices, shards(): lax.all_to_all(returned, 'band', split_axis=1, concat_axis=0, tiled=True)  75.9 us
    all_to_all x1, waiting for transfers between devices, shards(): lax.all_to_all(fourier, 'band', split_axis=0, concat_axis=1, tiled=True)  72.8 us
    psum x1, blocking collectives, shards(): spread_sum = lax.psum(partial_sum, 'band')  28.4 us
    reshape x2, local copies, waits for them, and re-layouts, shards(): returned = returned.reshape(mode_rows, H, 2, channels)  17.8 us
    all_to_all x1, starting transfers between devices, shards(): lax.all_to_all(returned, 'band', split_axis=1, concat_axis=0, tiled=True)  13.4 us
    dot_general x1, matrix products, spectral_pass(): jnp.dot(coeffs.reshape(mode_count * degree_count, channel_count), mixing_...  13.3 us
    reshape x1, local copies, waits for them, and re-layouts, shards(): moved = moved.reshape(mode_rows, H, 2 * channels)  13 us
  transfers between devices with their start and end apart: 3, of which 3 were waited for; matrix products, arithmetic and copies ran while one was open for 0% of the time, Pallas kernels for 0%

commit v1 on v0

v1 whole, which is shorter than its diff:
```python
import functools
import math

import jax
import jax.numpy as jnp
import numpy as np
from jax import lax
from jax.experimental import pallas as pl
from jax.experimental.pallas import tpu as pltpu
from jax.sharding import PartitionSpec as P

H = 240
W = 480
M = 240
L = 240
E = 384
BANDS = 16
ROWS = H // BANDS
OWN = M // BANDS
SLOTS = 32
DEPTH = 8
VMEM_LIMIT = 58 * 1024 * 1024


def legendre_table(degree_count, order_count, lat_count):
    colatitude = (np.arange(lat_count) + 0.5) * np.pi / lat_count
    cosines = np.cos(colatitude)
    sines = np.sin(colatitude)
    orders = np.arange(order_count)[:, None] * 1.0
    steps_up = np.arange(1, order_count) * 1.0
    log_factor = np.concatenate(
        [[0.0], np.cumsum(np.log((2.0 * steps_up - 1.0) / (2.0 * steps_up)))]
    )
    diagonal_start = np.exp(
        0.5 * np.log((2.0 * orders + 1.0) / 2.0)
        + 0.5 * log_factor[:, None]
        + orders * np.log(sines)[None, :]
    )
    result = np.zeros((order_count, degree_count, lat_count))
    previous = np.zeros(diagonal_start.shape)
    before_previous = np.zeros(diagonal_start.shape)
    for degree in range(degree_count):
        lower = degree - 1.0
        rising = np.sqrt(
            np.maximum(4.0 * degree * degree - 1.0, 1.0)
            / np.maximum(degree * degree - orders * orders, 1.0)
        )
        falling = np.sqrt(
            np.maximum(lower * lower - orders * orders, 0.0) / max(4.0 * lower * lower - 1.0, 1.0)
        )
        current = np.where(
            orders == degree,
            diagonal_start,
            np.where(
                degree > orders,
                rising * (cosines[None, :] * previous - falling * before_previous),
                0.0,
            ),
        )
        result[:, degree] = current
        before_previous = previous
        previous = current
    return result


def fourier_tables(lon_count, mode_order):
    longitude = 2.0 * np.pi * np.arange(lon_count)[:, None] / lon_count
    angles = longitude * (mode_order[None, :] * 1.0)
    forward_factor = math.sqrt(2.0 * math.pi) / lon_count
    forward_table = np.stack(
        [forward_factor * np.cos(angles), -forward_factor * np.sin(angles)], axis=1
    )
    inverse_factor = np.where(mode_order == 0, 1.0, 2.0) / math.sqrt(2.0 * math.pi)
    inverse_table = np.stack(
        [
            (inverse_factor[None, :] * np.cos(angles)).T,
            (-inverse_factor[None, :] * np.sin(angles)).T,
        ],
        axis=0,
    )
    return (forward_table, inverse_table)


def latitude_weights(lat_count):
    colatitude = (jnp.arange(lat_count, dtype=jnp.float32) + 0.5) * (math.pi / lat_count)
    return jnp.sin(colatitude) * (math.pi / lat_count)


def slot_tables():
    forward, inverse = fourier_tables(W, np.arange(M))
    ahead = np.zeros((BANDS, 2, 16, W))
    back = np.zeros((BANDS, 2, 16, W))
    ahead[:, :, :OWN] = forward.reshape(W, 2, OWN, BANDS).transpose(3, 1, 2, 0)
    back[:, :, :OWN] = inverse.reshape(2, OWN, BANDS, W).transpose(2, 0, 1, 3)
    return ahead.reshape(BANDS * SLOTS, W), back.reshape(BANDS * SLOTS, W).T


def rounded(table):
    return jnp.asarray(table, jnp.float32).astype(jnp.bfloat16)


def exchange_matrix():
    matrix = np.zeros((256, 256))
    for a in range(16):
        for b in range(16):
            matrix[b * 16 + a, a * 16 + b] = 1.0
    return matrix


def forward_kernel(weights_ref, x_ref, gain_ref, table_ref, out_ref):
    x = x_ref[0].astype(jnp.float32)
    centred = x - jnp.mean(x, axis=1, keepdims=True)
    variance = jnp.mean(jnp.square(centred), axis=1, keepdims=True)
    normed = (centred * lax.rsqrt(variance + 1e-05) * gain_ref[...]).astype(jnp.bfloat16)
    sums = jnp.dot(table_ref[...], normed, preferred_element_type=jnp.float32)
    sums = (sums * weights_ref[pl.program_id(0)]).astype(jnp.bfloat16)
    out_ref[...] = sums.reshape(BANDS, 1, SLOTS, E)


def forward_transform(x, gain, weights, table):
    return pl.pallas_call(
        forward_kernel,
        grid=(ROWS,),
        in_specs=[
            pl.BlockSpec(memory_space=pltpu.SMEM),
            pl.BlockSpec((1, W, E), lambda j: (j, 0, 0)),
            pl.BlockSpec((1, E), lambda j: (0, 0)),
            pl.BlockSpec((BANDS * SLOTS, W), lambda j: (0, 0)),
        ],
        out_specs=pl.BlockSpec((BANDS, 1, SLOTS, E), lambda j: (0, j, 0, 0)),
        out_shape=jax.ShapeDtypeStruct((BANDS, ROWS, SLOTS, E), jnp.bfloat16),
        compiler_params=pltpu.CompilerParams(vmem_limit_bytes=VMEM_LIMIT),
        cost_estimate=pl.CostEstimate(
            flops=2 * ROWS * BANDS * SLOTS * W * E, bytes_accessed=12 << 20, transcendentals=0
        ),
        name="forward_transform",
    )(weights, x, gain, table)


def spectral_kernel(
    band_ref, moved_ref, legendre_ref, gain_ref, real_ref, imag_ref, swap_ref, out_ref, by_mode, mixed
):
    swap = swap_ref[...]

    def to_modes(step, carry):
        rows = pl.ds(pl.multiple_of(step * 16, 16), 16)
        for part in range(2):
            block = moved_ref[rows, part * 16 : part * 16 + 16, :].reshape(256, E)
            turned = jnp.dot(swap, block, preferred_element_type=jnp.float32)
            by_mode[part, :, rows, :] = turned.astype(jnp.bfloat16).reshape(16, 16, E)
        return carry

    lax.fori_loop(0, H // 16, to_modes, 0)
    mix_real = real_ref[...]
    mix_imag = imag_ref[...]
    for i in range(OWN):
        low = 16 * i
        table = legendre_ref[0, i]
        ahead = table[low:]
        re = jnp.dot(ahead, by_mode[0, i], preferred_element_type=jnp.float32).astype(jnp.bfloat16)
        im = jnp.dot(ahead, by_mode[1, i], preferred_element_type=jnp.float32).astype(jnp.bfloat16)
        gain = gain_ref[low:]
        new_re = jnp.dot(re, mix_real, preferred_element_type=jnp.float32) - jnp.dot(
            im, mix_imag, preferred_element_type=jnp.float32
        )
        new_im = jnp.dot(re, mix_imag, preferred_element_type=jnp.float32) + jnp.dot(
            im, mix_real, preferred_element_type=jnp.float32
        )
        mixed[0, low:, :] = (new_re * gain).astype(jnp.bfloat16)
        mixed[1, low:, :] = (new_im * gain).astype(jnp.bfloat16)
        for part in range(2):
            spatial = lax.dot_general(
                table, mixed[part], (((0,), (0,)), ((), ())), preferred_element_type=jnp.float32
            )
            by_mode[part, i] = spatial.astype(jnp.bfloat16)

    def to_rows(step, carry):
        rows = pl.ds(pl.multiple_of(step * 16, 16), 16)
        for part in range(2):
            block = by_mode[part, :, rows, :].reshape(256, E)
            turned = jnp.dot(swap, block, preferred_element_type=jnp.float32)
            out_ref[rows, part * 16 : part * 16 + 16, :] = turned.astype(jnp.bfloat16).reshape(16, 16, E)
        return carry

    lax.fori_loop(0, H // 16, to_rows, 0)


def spectral_pass(band, moved, legendre, gain, mix_real, mix_imag, swap):
    whole = lambda *shape: pl.BlockSpec(shape, lambda step, band: (0,) * len(shape))
    return pl.pallas_call(
        spectral_kernel,
        grid_spec=pltpu.PrefetchScalarGridSpec(
            num_scalar_prefetch=1,
            grid=(1,),
            in_specs=[
                whole(H, SLOTS, E),
                pl.BlockSpec((1, OWN, L, H), lambda step, band: (band[0], 0, 0, 0)),
                whole(L, 1),
                whole(E, E),
                whole(E, E),
                whole(256, 256),
            ],
            out_specs=whole(H, SLOTS, E),
            scratch_shapes=[
                pltpu.VMEM((2, 16, H, E), jnp.bfloat16),
                pltpu.VMEM((2, L, E), jnp.bfloat16),
            ],
        ),
        out_shape=jax.ShapeDtypeStruct((H, SLOTS, E), jnp.bfloat16),
        compiler_params=pltpu.CompilerParams(vmem_limit_bytes=VMEM_LIMIT),
        cost_estimate=pl.CostEstimate(flops=8 << 30, bytes_accessed=14 << 20, transcendentals=0),
        name="spectral_pass",
    )(band, moved, legendre, gain, mix_real, mix_imag, swap)


def inverse_kernel(spatial_ref, x_ref, table_ref, out_ref):
    sums = jnp.dot(
        table_ref[...], spatial_ref[...].reshape(BANDS * SLOTS, E), preferred_element_type=jnp.float32
    )
    out_ref[0] = (x_ref[0].astype(jnp.float32) + jax.nn.gelu(sums)).astype(jnp.bfloat16)


def inverse_transform(spatial, x, table):
    return pl.pallas_call(
        inverse_kernel,
        grid=(ROWS,),
        in_specs=[
            pl.BlockSpec((BANDS, 1, SLOTS, E), lambda j: (0, j, 0, 0)),
            pl.BlockSpec((1, W, E), lambda j: (j, 0, 0)),
            pl.BlockSpec((W, BANDS * SLOTS), lambda j: (0, 0)),
        ],
        out_specs=pl.BlockSpec((1, W, E), lambda j: (j, 0, 0)),
        out_shape=jax.ShapeDtypeStruct((16, W, E), jnp.bfloat16),
        compiler_params=pltpu.CompilerParams(vmem_limit_bytes=VMEM_LIMIT),
        cost_estimate=pl.CostEstimate(
            flops=2 * ROWS * BANDS * SLOTS * W * E, bytes_accessed=18 << 20, transcendentals=ROWS * W * E
        ),
        name="inverse_transform",
    )(spatial, x, table)


def spread_kernel(weights_ref, own_ref, control_ref, out_ref):
    step = pl.program_id(0)
    difference = own_ref[0].astype(jnp.float32) - control_ref[0].astype(jnp.float32)
    partial = jnp.sum((difference * difference).reshape(W // 8, 8, E), axis=0) * weights_ref[step]

    @pl.when(step == 0)
    def _():
        out_ref[...] = partial

    @pl.when(step > 0)
    def _():
        out_ref[...] += partial


def spread_sums(weights, own, control):
    row = pl.BlockSpec((1, W, E), lambda j: (j, 0, 0))
    return pl.pallas_call(
        spread_kernel,
        grid=(ROWS,),
        in_specs=[pl.BlockSpec(memory_space=pltpu.SMEM), row, row],
        out_specs=pl.BlockSpec((8, E), lambda j: (0, 0)),
        out_shape=jax.ShapeDtypeStruct((8, E), jnp.float32),
        compiler_params=pltpu.CompilerParams(vmem_limit_bytes=VMEM_LIMIT),
        cost_estimate=pl.CostEstimate(flops=9 << 20, bytes_accessed=11 << 20, transcendentals=0),
        name="spread_sums",
    )(weights, own, control)


def rescale_kernel(scale_ref, own_ref, control_ref, out_ref):
    control = control_ref[...].astype(jnp.float32)
    difference = own_ref[...].astype(jnp.float32) - control
    out_ref[...] = (control + scale_ref[0] * difference).astype(jnp.bfloat16)


def rescaled(scale, own, control):
    row = pl.BlockSpec((1, W, E), lambda j: (j, 0, 0))
    return pl.pallas_call(
        rescale_kernel,
        grid=(ROWS,),
        in_specs=[pl.BlockSpec(memory_space=pltpu.SMEM), row, row],
        out_specs=row,
        out_shape=jax.ShapeDtypeStruct((ROWS, W, E), jnp.bfloat16),
        compiler_params=pltpu.CompilerParams(vmem_limit_bytes=VMEM_LIMIT),
        cost_estimate=pl.CostEstimate(flops=9 << 20, bytes_accessed=17 << 20, transcendentals=0),
        name="rescaled",
    )(scale, own, control)


def from_control(field):
    eighths = field.reshape(DEPTH, 2, W, E)
    piece = eighths[0]
    for z in range(1, DEPTH):
        arrived = lax.ppermute(eighths[z], "member", [(0, 2 * z)])
        piece = jnp.where(lax.axis_index("member") == 2 * z, arrived, piece)
    across = lax.ppermute(piece, "member", [(2 * z, 2 * z + 1) for z in range(DEPTH)])
    piece = jnp.where(lax.axis_index("member") % 2 == 1, across, piece)
    rings = [[2 * z + h for z in range(DEPTH)] for h in range(2)]
    return lax.all_gather(piece, "member", tiled=True, axis_index_groups=rings)


def summed_over_band(partial):
    copies = jnp.broadcast_to(partial[None], (BANDS,) + partial.shape)
    return jnp.sum(lax.all_to_all(copies, "band", split_axis=0, concat_axis=0, tiled=True))


def shards(
    copy_fields,
    norm_gain,
    mix_real,
    mix_imag,
    filter_bank,
    perturbation_draw_numbers,
    amplitudes,
    desired_magnitude_slot,
):
    band_index = lax.axis_index("band")
    ahead_np, back_np = slot_tables()
    legendre_np = legendre_table(L, M, H).reshape(OWN, BANDS, L, H).transpose(1, 0, 2, 3)
    x = jnp.transpose(copy_fields[0], (0, 2, 1))

    global_rows = band_index * ROWS + jnp.arange(ROWS, dtype=jnp.int32)
    weights = jnp.sin((global_rows.astype(jnp.float32) + 0.5) * (math.pi / H)) * (math.pi / H)
    total_weight = jnp.sum(latitude_weights(H)) * (E * W)
    bank_rows = filter_bank.shape[0]
    draw_onehot = (jnp.arange(bank_rows, dtype=jnp.int32) == perturbation_draw_numbers[0]).astype(
        jnp.float32
    )
    degree_gain = jnp.sum(draw_onehot[:, None] * filter_bank, axis=0)

    fourier = forward_transform(x, norm_gain[None, :], weights, rounded(ahead_np))
    moved = lax.all_to_all(fourier, "band", split_axis=0, concat_axis=0, tiled=True)
    returned = spectral_pass(
        band_index[None],
        moved.reshape(H, SLOTS, E),
        rounded(legendre_np),
        degree_gain[:, None],
        mix_real,
        mix_imag,
        rounded(exchange_matrix()),
    )
    spatial = lax.all_to_all(
        returned.reshape(BANDS, ROWS, SLOTS, E), "band", split_axis=0, concat_axis=0, tiled=True
    )
    forecast = inverse_transform(spatial, x, rounded(back_np))
    control = from_control(forecast)
    spread_sum = summed_over_band(spread_sums(weights, forecast, control))
    spread = spread_sum / total_weight
    target = jnp.sum(
        jnp.where(
            jnp.arange(amplitudes.shape[0], dtype=jnp.int32) == desired_magnitude_slot[0],
            amplitudes,
            0.0,
        )
    )
    scale = target / jnp.sqrt(spread + 1e-06)
    bred = rescaled(scale[None], forecast, control)
    return jnp.transpose(bred, (0, 2, 1))[None]


def solution(mesh):
    in_specs = (P("member", "band", None, None), P(), P(), P(), P(), P("member"), P(), P("member"))
    out_specs = P("member", "band", None, None)
    return jax.shard_map(shards, mesh=mesh, in_specs=in_specs, out_specs=out_specs, check_vma=False)
```

time: 598 us -> 444 us (0.74)
  waiting for transfers between devices: 414 us -> 219 us
  Pallas kernels: 0 us -> 78.7 us
  blocking collectives: 28.4 us -> 80.6 us
  local copies, waits for them, and re-layouts: 51.8 us -> 7.53 us
  matrix products: 39 us -> 0 us
  other arithmetic: 24.3 us -> 5.05 us
  starting transfers between devices: 21.4 us -> 34.2 us
    psum x1 -> x0, waiting for transfers between devices: 266 us -> none  [broadcast(): return lax.psum(kept, axis)]
    all_to_all x0 -> x1, blocking collectives: none -> 80.6 us  [shards(): lax.all_to_all(returned.reshape(BANDS, ROWS, SLOTS, E), 'band', split_axi...]
    pallas_call x0 -> x5, Pallas kernels: none -> 78.7 us  [the longest x1 24.4 us: spectral_pass(): pl.pallas_call(spectral_kernel, grid_spec=pltpu.PrefetchScalarGridSpec(nu...]
    all_gather x0 -> x1, waiting for transfers between devices: none -> 74.3 us  [from_control(): return lax.all_gather(piece, 'member', tiled=True, axis_index_groups=rings)]
    all_to_all x2, waiting for transfers between devices: 149 us -> 83.2 us  [the longest x1 79.2 us: shards(): lax.all_to_all(fourier, 'band', split_axis=0, concat_axis=0, tiled=True)]
    ppermute x0 -> x8, waiting for transfers between devices: none -> 61.4 us  [the longest x7 46.9 us: from_control(): arrived = lax.ppermute(eighths[z], 'member', [(0, 2 * z)])]
    dot_general x5 -> x0, matrix products: 39 us -> none  [the longest x1 13.3 us: spectral_pass(): jnp.dot(coeffs.reshape(mode_count * degree_count, channel_count), mixing_...]
    reshape x3 -> x0, local copies, waits for them, and re-layouts: 30.8 us -> none  [the longest x2 17.8 us: shards(): returned = returned.reshape(mode_rows, H, 2, channels)]
  transfers between devices with their start and end apart: 3 -> 11, of which waited for: 3 -> 8; matrix products, arithmetic and copies ran while one was open for 0% -> 1% of each run, Pallas kernels for 0% -> 0%
where the time goes in v1:
time: 444 us; the launch traced here: 442 us
  waiting for transfers between devices  219 us (49%)
  blocking collectives  80.6 us (18%)
  Pallas kernels  78.7 us (18%)
  starting transfers between devices  34.2 us (8%)
  between operations  16.7 us (4%)
  local copies, waits for them, and re-layouts  7.53 us (2%)
  other arithmetic  5.05 us (1%)
    all_to_all x1, blocking collectives, shards(): lax.all_to_all(returned.reshape(BANDS, ROWS, SLOTS, E), 'band', split_axi...  80.6 us
    all_to_all x1, waiting for transfers between devices, shards(): lax.all_to_all(fourier, 'band', split_axis=0, concat_axis=0, tiled=True)  79.2 us
    all_gather x1, waiting for transfers between devices, from_control(): return lax.all_gather(piece, 'member', tiled=True, axis_index_groups=rings)  74.3 us
    ppermute x7, waiting for transfers between devices, from_control(): arrived = lax.ppermute(eighths[z], 'member', [(0, 2 * z)])  46.9 us
    pallas_call x1, Pallas kernels, spectral_pass(): pl.pallas_call(spectral_kernel, grid_spec=pltpu.PrefetchScalarGridSpec(nu...  24.4 us
    ppermute x7, starting transfers between devices, from_control(): arrived = lax.ppermute(eighths[z], 'member', [(0, 2 * z)])  19.2 us
    pallas_call x1, Pallas kernels, inverse_transform(): pl.pallas_call(inverse_kernel, grid=(ROWS,), in_specs=[pl.BlockSpec((BAND...  15.7 us
    pallas_call x1, Pallas kernels, forward_transform(): pl.pallas_call(forward_kernel, grid=(ROWS,), in_specs=[pl.BlockSpec(memor...  15.4 us
  transfers between devices with their start and end apart: 11, of which 8 were waited for; matrix products, arithmetic and copies ran while one was open for 1% of the time, Pallas kernels for 0%

profile of v1, /device:TPU:1, one launch (start us, length us, event | category | flops | bytes accessed | tf_op | source)
XLA Modules:
  0.0 441.7 jit_solution(4860997065508284584)
XLA Ops:
  8.3 15.4 %forward_transform.1 = bf16[16,15,32,384]{3,2,1,0:T(8,128)(2,1)} custom-call(f32[15]{0:T(128)} %sine_multiply_fusion.weights_ref, bf16[15,480,384]{2,1,0:T(8,128)(2,1)} %bitcast.16, f32[1,384]{1,0:T(1,128)} %broadcast_in_dim.28.gain_ref, bf16[512,480]{1,0:T(8,128)(2,1)} %constant.62.table_ref), custom_call_target="tpu_custom_call" | custom-call | flops 2831155200 | bytes 12582912 | tf_op jit(solution)/shard_map/forward_transform/pallas_call | solution.py:121
  23.7 7.7 %all-to-all-start = ((bf16[16,15,32,384]{3,2,1,0:T(8,128)(2,1)}), bf16[16,15,32,384]{3,2,1,0:T(8,128)(2,1)}, u32[]{:S(2)}, u32[]{:S(2)}) async-start(bf16[16,15,32,384]{3,2,1,0:T(8,128)(2,1)} %forward_transform.1), calls=%async_computation | async-start | bytes 11796480 | tf_op jit(solution)/shard_map/all_to_all | solution.py:332
  33.0 79.2 %all-to-all-done = bf16[16,15,32,384]{3,2,1,0:T(8,128)(2,1)} async-done(((bf16[16,15,32,384]{3,2,1,0:T(8,128)(2,1)}), bf16[16,15,32,384]{3,2,1,0:T(8,128)(2,1)}, u32[]{:S(2)}, u32[]{:S(2)}) %all-to-all-start) | async-done | bytes 5898272 | tf_op jit(solution)/shard_map/all_to_all | solution.py:332
  112.2 24.4 %spectral_pass.1 = bf16[240,32,384]{2,1,0:T(8,128)(2,1)} custom-call(s32[1]{0:T(128)} %bitcast.1.band_ref, bf16[240,32,384]{2,1,0:T(8,128)(2,1)} %bitcast.4.moved_ref, bf16[16,15,240,240]{3,2,1,0:T(8,128)(2,1)} %constant.63.legendre_ref, f32[240,1]{1,0:T(8,128)} %copy.15.gain_ref, bf16[384,384]{1,0:T(8,128)(2,1)} %real_ref.1, bf16[384,384]{1,0:T(8,128)(2,1)} %imag_ref.1, ...), custom_call_target="tpu_custom_call" | custom-call | flops 8589934592 | bytes 14680064 | tf_op jit(solution)/shard_map/spectral_pass/pallas_call | solution.py:190
  136.6 80.6 %all_to_all.15.spatial_ref = bf16[16,15,32,384]{3,2,1,0:T(8,128)(2,1)} all-to-all(bf16[16,15,32,384]{3,2,1,0:T(8,128)(2,1)} %bitcast.15), channel_id=1, replica_groups=mesh['member'=16,'band'=16] {'band'}, dimensions={0} | all-to-all | bytes 11796480 | tf_op jit(solution)/shard_map/all_to_all | solution.py:342
  217.2 15.7 %inverse_transform.1.own_ref = bf16[16,480,384]{2,1,0:T(8,128)(2,1)} custom-call(bf16[16,15,32,384]{3,2,1,0:T(8,128)(2,1)} %all_to_all.15.spatial_ref, bf16[15,480,384]{2,1,0:T(8,128)(2,1)} %bitcast.17, bf16[480,512]{1,0:T(8,128)(2,1)} %constant.65.table_ref), custom_call_target="tpu_custom_call" | custom-call | flops 2831155200 | bytes 18874368 | tf_op jit(solution)/shard_map/inverse_transform/pallas_call | solution.py:224
  232.9 4.1 fusion.7
  237.0 3.5 collective-permute-start.6
  240.6 2.0 collective-permute-start.5
  242.6 2.9 collective-permute-start.4
  245.5 4.1 collective-permute-start.3
  249.6 2.2 collective-permute-start.2
  251.8 3.8 collective-permute-done.6
  255.7 2.2 collective-permute-start.1
  257.9 13.6 %collective-permute-done.5 = bf16[2,480,384]{2,1,0:T(8,128)(2,1)S(1)} collective-permute-done((bf16[2,480,384]{2,1,0:T(8,128)(2,1)S(1)}, bf16[2,480,384]{2,1,0:T(8,128)(2,1)S(1)}, u32[]{:S(2)}, u32[]{:S(2)}) %collective-permute-start.5) | collective-permute-done | bytes 737312 | tf_op jit(solution)/shard_map/ppermute | solution.py:294
  271.5 2.2 collective-permute-start
  273.6 13.7 %collective-permute-done.4 = bf16[2,480,384]{2,1,0:T(8,128)(2,1)} collective-permute-done((bf16[2,480,384]{2,1,0:T(8,128)(2,1)}, bf16[2,480,384]{2,1,0:T(8,128)(2,1)}, u32[]{:S(2)}, u32[]{:S(2)}) %collective-permute-start.4) | collective-permute-done | bytes 737312 | tf_op jit(solution)/shard_map/ppermute | solution.py:294
  287.4 15.8 %collective-permute-done.3 = bf16[2,480,384]{2,1,0:T(8,128)(2,1)} collective-permute-done((bf16[2,480,384]{2,1,0:T(8,128)(2,1)}, bf16[2,480,384]{2,1,0:T(8,128)(2,1)}, u32[]{:S(2)}, u32[]{:S(2)}) %collective-permute-start.3) | collective-permute-done | bytes 737312 | tf_op jit(solution)/shard_map/ppermute | solution.py:294
  306.0 14.4 %collective-permute-done.7 = bf16[2,480,384]{2,1,0:T(8,128)(2,1)S(1)} collective-permute-done((bf16[2,480,384]{2,1,0:T(8,128)(2,1)S(1)}, bf16[2,480,384]{2,1,0:T(8,128)(2,1)S(1)}, u32[]{:S(2)}, u32[]{:S(2)}) %collective-permute-start.7) | collective-permute-done | bytes 737312 | tf_op jit(solution)/shard_map/ppermute | solution.py:296
  321.4 74.3 %all-gather.2.cloned.1.call-done.control_ref = bf16[16,480,384]{2,1,0:T(8,128)(2,1)} async-done(((bf16[2,480,384]{2,1,0:T(8,128)(2,1)}), bf16[16,480,384]{2,1,0:T(8,128)(2,1)}) %all-gather.2.cloned.1.call-update) | async-done | bytes 5898256 | tf_op jit(solution)/shard_map/all_gather | solution.py:299
  395.7 11.1 %spread_sums.1 = f32[8,384]{1,0:T(8,128)} custom-call(f32[15]{0:T(128)} %sine_multiply_fusion.weights_ref, bf16[16,480,384]{2,1,0:T(8,128)(2,1)} %inverse_transform.1.own_ref, bf16[16,480,384]{2,1,0:T(8,128)(2,1)} %all-gather.2.cloned.1.call-done.control_ref), custom_call_target="tpu_custom_call" | custom-call | flops 9437184 | bytes 11534336 | tf_op jit(solution)/shard_map/spread_sums/pallas_call | solution.py:258
  408.2 5.9 %all-to-all-start.2 = ((f32[16,8,384]{2,1,0:T(8,128)}), f32[16,8,384]{2,1,0:T(8,128)S(1)}, u32[]{:S(2)}, u32[]{:S(2)}) async-start(f32[16,8,384]{2,1,0:T(8,128)} %broadcast_in_dim.30), calls=%async_computation.2 | async-start | bytes 393216 | tf_op jit(solution)/shard_map/all_to_all | solution.py:304
  416.8 4.0 all-to-all-done.2
  422.8 12.1 %rescaled.1 = bf16[15,480,384]{2,1,0:T(8,128)(2,1)} custom-call(f32[1]{0:T(128)} %bitcast.8.scale_ref, bf16[16,480,384]{2,1,0:T(8,128)(2,1)} %inverse_transform.1.own_ref, bf16[16,480,384]{2,1,0:T(8,128)(2,1)} %all-gather.2.cloned.1.call-done.control_ref), custom_call_target="tpu_custom_call" | custom-call | flops 9437184 | bytes 17825792 | tf_op jit(solution)/shard_map/rescaled/pallas_call | solution.py:278
  (21 shorter events, 9.9 us)
Async XLA Ops:
  23.7 8.4 %copy-start = (f32[32,240]{1,0:T(8,128)S(1)}, f32[32,240]{1,0:T(8,128)}, u32[]{:S(2)}) copy-start(f32[32,240]{1,0:T(8,128)} %param.16) | copy-start | bytes 92164
  23.7 88.5 %all-to-all-start = ((bf16[16,15,32,384]{3,2,1,0:T(8,128)(2,1)}), bf16[16,15,32,384]{3,2,1,0:T(8,128)(2,1)}, u32[]{:S(2)}, u32[]{:S(2)}) async-start(bf16[16,15,32,384]{3,2,1,0:T(8,128)(2,1)} %forward_transform.1), calls=%async_computation | async-start | bytes 11796480 | tf_op jit(solution)/shard_map/all_to_all | solution.py:332
  31.4 364.3 %all-gather.2.cloned.1.call-start = ((), (), s32[]{:S(2)}) async-start(), calls=%async_computation.3 | async-start | bytes 6635520 | tf_op jit(solution)/shard_map/all_gather | solution.py:299
  237.0 18.7 %collective-permute-start.6 = (bf16[2,480,384]{2,1,0:T(8,128)(2,1)S(1)}, bf16[2,480,384]{2,1,0:T(8,128)(2,1)S(1)}, u32[]{:S(2)}, u32[]{:S(2)}) collective-permute-start(bf16[2,480,384]{2,1,0:T(8,128)(2,1)S(1)} %get-tuple-element.5), channel_id=1, source_target_pairs={{0,32},{1,33},{2,34},{3,35},{4,36},{5,37},{6,38},{7,39},{8,40},{9,... | collective-permute-start | bytes 2211848 | tf_op jit(solution)/shard_map/ppermute | solution.py:294
  240.6 30.9 %collective-permute-start.5 = (bf16[2,480,384]{2,1,0:T(8,128)(2,1)S(1)}, bf16[2,480,384]{2,1,0:T(8,128)(2,1)S(1)}, u32[]{:S(2)}, u32[]{:S(2)}) collective-permute-start(bf16[2,480,384]{2,1,0:T(8,128)(2,1)S(1)} %get-tuple-element.6), channel_id=1, source_target_pairs={{0,64},{1,65},{2,66},{3,67},{4,68},{5,69},{6,70},{7,71},{8,72},{9,... | collective-permute-start | bytes 2211848 | tf_op jit(solution)/shard_map/ppermute | solution.py:294
  242.6 44.7 %collective-permute-start.4 = (bf16[2,480,384]{2,1,0:T(8,128)(2,1)}, bf16[2,480,384]{2,1,0:T(8,128)(2,1)}, u32[]{:S(2)}, u32[]{:S(2)}) collective-permute-start(bf16[2,480,384]{2,1,0:T(8,128)(2,1)} %get-tuple-element.7), channel_id=1, source_target_pairs={{0,96},{1,97},{2,98},{3,99},{4,100},{5,101},{6,102},{7,103},{8,104... | collective-permute-start | bytes 2211848 | tf_op jit(solution)/shard_map/ppermute | solution.py:294
  245.5 57.6 %collective-permute-start.3 = (bf16[2,480,384]{2,1,0:T(8,128)(2,1)}, bf16[2,480,384]{2,1,0:T(8,128)(2,1)}, u32[]{:S(2)}, u32[]{:S(2)}) collective-permute-start(bf16[2,480,384]{2,1,0:T(8,128)(2,1)} %get-tuple-element.8), channel_id=1, source_target_pairs={{0,128},{1,129},{2,130},{3,131},{4,132},{5,133},{6,134},{7,135},{8... | collective-permute-start | bytes 2211848 | tf_op jit(solution)/shard_map/ppermute | solution.py:294
  249.6 53.5 %collective-permute-start.2 = (bf16[2,480,384]{2,1,0:T(8,128)(2,1)}, bf16[2,480,384]{2,1,0:T(8,128)(2,1)}, u32[]{:S(2)}, u32[]{:S(2)}) collective-permute-start(bf16[2,480,384]{2,1,0:T(8,128)(2,1)} %get-tuple-element.9), channel_id=1, source_target_pairs={{0,160},{1,161},{2,162},{3,163},{4,164},{5,165},{6,166},{7,167},{8... | collective-permute-start | bytes 2211848 | tf_op jit(solution)/shard_map/ppermute | solution.py:294
  255.7 47.5 %collective-permute-start.1 = (bf16[2,480,384]{2,1,0:T(8,128)(2,1)S(1)}, bf16[2,480,384]{2,1,0:T(8,128)(2,1)}, u32[]{:S(2)}, u32[]{:S(2)}) collective-permute-start(bf16[2,480,384]{2,1,0:T(8,128)(2,1)S(1)} %get-tuple-element.10), channel_id=1, source_target_pairs={{0,192},{1,193},{2,194},{3,195},{4,196},{5,197},{6,198},{7,199},{8... | collective-permute-start | bytes 2211848 | tf_op jit(solution)/shard_map/ppermute | solution.py:294
  271.5 31.7 %collective-permute-start = (bf16[2,480,384]{2,1,0:T(8,128)(2,1)S(1)}, bf16[2,480,384]{2,1,0:T(8,128)(2,1)}, u32[]{:S(2)}, u32[]{:S(2)}) collective-permute-start(bf16[2,480,384]{2,1,0:T(8,128)(2,1)S(1)} %get-tuple-element.11), channel_id=1, source_target_pairs={{0,224},{1,225},{2,226},{3,227},{4,228},{5,229},{6,230},{7,231},{8... | collective-permute-start | bytes 2211848 | tf_op jit(solution)/shard_map/ppermute | solution.py:294
  304.6 15.8 %collective-permute-start.7 = (bf16[2,480,384]{2,1,0:T(8,128)(2,1)S(1)}, bf16[2,480,384]{2,1,0:T(8,128)(2,1)S(1)}, u32[]{:S(2)}, u32[]{:S(2)}) collective-permute-start(bf16[2,480,384]{2,1,0:T(8,128)(2,1)S(1)} %fusion.5), channel_id=1, source_target_pairs={{0,16},{32,48},{64,80},{96,112},{128,144},{160,176},{192,208},{224... | collective-permute-start | bytes 2211848 | tf_op jit(solution)/shard_map/ppermute | solution.py:296
  321.4 94.7 %copy-start.1 = (f32[8]{0:T(128)S(1)}, f32[8]{0:T(128)}, u32[]{:S(2)}) copy-start(f32[8]{0:T(128)} %param.18) | copy-start | bytes 100
  408.2 12.6 %all-to-all-start.2 = ((f32[16,8,384]{2,1,0:T(8,128)}), f32[16,8,384]{2,1,0:T(8,128)S(1)}, u32[]{:S(2)}, u32[]{:S(2)}) async-start(f32[16,8,384]{2,1,0:T(8,128)} %broadcast_in_dim.30), calls=%async_computation.2 | async-start | bytes 393216 | tf_op jit(solution)/shard_map/all_to_all | solution.py:304
Sparse Core Ops, SparseCore 0:
  321.5 74.1 all-gather.1

commit v2 on v1

v2 whole, which is shorter than its diff:
```python
import functools
import math

import jax
import jax.numpy as jnp
import numpy as np
from jax import lax
from jax.experimental import pallas as pl
from jax.experimental.pallas import tpu as pltpu
from jax.sharding import PartitionSpec as P

H = 240
W = 480
M = 240
L = 240
E = 384
BANDS = 16
ROWS = H // BANDS
OWN = M // BANDS
SLOTS = 32
DEPTH = 8
RINGS = [[2 * z + h for z in range(DEPTH)] for h in range(2)]
STEP = 3
VMEM_LIMIT = 58 * 1024 * 1024


def legendre_table(degree_count, order_count, lat_count):
    colatitude = (np.arange(lat_count) + 0.5) * np.pi / lat_count
    cosines = np.cos(colatitude)
    sines = np.sin(colatitude)
    orders = np.arange(order_count)[:, None] * 1.0
    steps_up = np.arange(1, order_count) * 1.0
    log_factor = np.concatenate(
        [[0.0], np.cumsum(np.log((2.0 * steps_up - 1.0) / (2.0 * steps_up)))]
    )
    diagonal_start = np.exp(
        0.5 * np.log((2.0 * orders + 1.0) / 2.0)
        + 0.5 * log_factor[:, None]
        + orders * np.log(sines)[None, :]
    )
    result = np.zeros((order_count, degree_count, lat_count))
    previous = np.zeros(diagonal_start.shape)
    before_previous = np.zeros(diagonal_start.shape)
    for degree in range(degree_count):
        lower = degree - 1.0
        rising = np.sqrt(
            np.maximum(4.0 * degree * degree - 1.0, 1.0)
            / np.maximum(degree * degree - orders * orders, 1.0)
        )
        falling = np.sqrt(
            np.maximum(lower * lower - orders * orders, 0.0) / max(4.0 * lower * lower - 1.0, 1.0)
        )
        current = np.where(
            orders == degree,
            diagonal_start,
            np.where(
                degree > orders,
                rising * (cosines[None, :] * previous - falling * before_previous),
                0.0,
            ),
        )
        result[:, degree] = current
        before_previous = previous
        previous = current
    return result


def fourier_tables(lon_count, mode_order):
    longitude = 2.0 * np.pi * np.arange(lon_count)[:, None] / lon_count
    angles = longitude * (mode_order[None, :] * 1.0)
    forward_factor = math.sqrt(2.0 * math.pi) / lon_count
    forward_table = np.stack(
        [forward_factor * np.cos(angles), -forward_factor * np.sin(angles)], axis=1
    )
    inverse_factor = np.where(mode_order == 0, 1.0, 2.0) / math.sqrt(2.0 * math.pi)
    inverse_table = np.stack(
        [
            (inverse_factor[None, :] * np.cos(angles)).T,
            (-inverse_factor[None, :] * np.sin(angles)).T,
        ],
        axis=0,
    )
    return (forward_table, inverse_table)


def latitude_weights(lat_count):
    colatitude = (jnp.arange(lat_count, dtype=jnp.float32) + 0.5) * (math.pi / lat_count)
    return jnp.sin(colatitude) * (math.pi / lat_count)


def slot_tables():
    forward, inverse = fourier_tables(W, np.arange(M))
    ahead = np.zeros((W, 2, 16, BANDS))
    back = np.zeros((2, 16, BANDS, W))
    ahead[:, :, :OWN] = forward.reshape(W, 2, OWN, BANDS)
    back[:, :OWN] = inverse.reshape(2, OWN, BANDS, W)
    ahead = ahead.reshape(W, 2, DEPTH, 2, BANDS)
    back = back.reshape(2, DEPTH, 2, BANDS, W)
    rows = BANDS * SLOTS
    return (
        ahead.transpose(4, 2, 1, 3, 0).reshape(rows, W),
        back.transpose(3, 1, 0, 2, 4).reshape(rows, W).T,
        ahead.transpose(2, 4, 1, 3, 0).reshape(rows, W),
        back.transpose(1, 3, 0, 2, 4).reshape(rows, W).T,
    )


def rounded(table):
    return jnp.asarray(table, jnp.float32).astype(jnp.bfloat16)


def exchange_matrix():
    matrix = np.zeros((256, 256))
    for a in range(16):
        for b in range(16):
            matrix[b * 16 + a, a * 16 + b] = 1.0
    return matrix


def forward_kernel(weights_ref, x_ref, gain_ref, table_ref, out_ref):
    rows = x_ref.shape[0]
    for j in range(rows):
        x = x_ref[j].astype(jnp.float32)
        centred = x - jnp.mean(x, axis=1, keepdims=True)
        variance = jnp.mean(jnp.square(centred), axis=1, keepdims=True)
        normed = (centred * lax.rsqrt(variance + 1e-05) * gain_ref[...]).astype(jnp.bfloat16)
        sums = jnp.dot(table_ref[...], normed, preferred_element_type=jnp.float32)
        sums = (sums * weights_ref[pl.program_id(0) * rows + j]).astype(jnp.bfloat16)
        out_ref[:, j] = sums.reshape(out_ref.shape[0], out_ref.shape[2], E)


def forward_transform(x, gain, weights, table, groups, step):
    rows = x.shape[0]
    size = BANDS * SLOTS // groups
    return pl.pallas_call(
        forward_kernel,
        grid=(rows // step,),
        in_specs=[
            pl.BlockSpec(memory_space=pltpu.SMEM),
            pl.BlockSpec((step, W, E), lambda j: (j, 0, 0)),
            pl.BlockSpec((1, E), lambda j: (0, 0)),
            pl.BlockSpec((BANDS * SLOTS, W), lambda j: (0, 0)),
        ],
        out_specs=pl.BlockSpec((groups, step, size, E), lambda j: (0, j, 0, 0)),
        out_shape=jax.ShapeDtypeStruct((groups, rows, size, E), jnp.bfloat16),
        compiler_params=pltpu.CompilerParams(vmem_limit_bytes=VMEM_LIMIT),
        cost_estimate=pl.CostEstimate(
            flops=2 * rows * BANDS * SLOTS * W * E, bytes_accessed=rows << 20, transcendentals=0
        ),
        name="forward_transform",
    )(weights, x, gain, table)


def mix_degrees(table, values, gain, mixing):
    coeffs = jnp.dot(table, values, preferred_element_type=jnp.float32).astype(jnp.bfloat16)
    return (jnp.dot(coeffs, mixing, preferred_element_type=jnp.float32) * gain).astype(jnp.bfloat16)


def to_latitudes(table, mixed):
    return lax.dot_general(
        table, mixed, (((0,), (0,)), ((), ())), preferred_element_type=jnp.float32
    ).astype(jnp.bfloat16)


def shared_spectral_kernel(
    place_ref, re_ref, im_ref, legendre_ref, gain_ref, mixing_ref, out_re_ref, out_im_ref
):
    table = legendre_ref[0, 0]
    values = jnp.concatenate([re_ref[0], im_ref[0]], axis=1)
    spatial = to_latitudes(table, mix_degrees(table, values, gain_ref[...], mixing_ref[...]))
    out_re_ref[0] = spatial[:, :E]
    out_im_ref[0] = spatial[:, E:]


def shared_spectral_pass(place, moved, legendre, gain, mixing):
    row = lambda first: pl.BlockSpec((1, H, E), lambda o, place: (first + o, 0, 0))
    whole = lambda *shape: pl.BlockSpec(shape, lambda o, place: (0,) * len(shape))
    pair = jax.ShapeDtypeStruct((2, H, E), jnp.bfloat16)
    out_re, out_im = pl.pallas_call(
        shared_spectral_kernel,
        grid_spec=pltpu.PrefetchScalarGridSpec(
            num_scalar_prefetch=1,
            grid=(2,),
            in_specs=[
                row(0),
                row(2),
                pl.BlockSpec(
                    (1, 1, L, H),
                    lambda o, place: (place[0], jnp.minimum(2 * place[1] + o, OWN - 1), 0, 0),
                ),
                whole(L, 1),
                whole(2 * E, 2 * E),
            ],
            out_specs=[row(0), row(0)],
        ),
        out_shape=[pair, pair],
        compiler_params=pltpu.CompilerParams(vmem_limit_bytes=VMEM_LIMIT),
        cost_estimate=pl.CostEstimate(flops=1 << 30, bytes_accessed=4 << 20, transcendentals=0),
        name="shared_spectral_pass",
    )(place, moved, moved, legendre, gain, mixing)
    return jnp.concatenate([out_re, out_im], axis=0)


def spectral_kernel(
    band_ref, moved_ref, legendre_ref, gain_ref, mixing_ref, swap_ref, out_ref, by_mode, mixed
):
    swap = swap_ref[...]
    halves = [(half, lanes) for half, lanes in ((0, slice(0, E)), (16, slice(E, 2 * E)))]
    unroll = 3

    def place_of(slot):
        z, part, o = slot // 4, (slot // 2) % 2, slot % 2
        return 2 * z + o, slice(part * E, part * E + E)

    def to_modes(step, carry):
        for piece in range(unroll):
            rows = pl.ds(pl.multiple_of((step * unroll + piece) * 16, 16), 16)
            block = jnp.concatenate(
                [moved_ref[rows, half : half + 16, :].reshape(256, E) for half, _ in halves], axis=1
            )
            turned = jnp.dot(swap, block, preferred_element_type=jnp.float32).astype(jnp.bfloat16)
            turned = turned.reshape(16, 16, 2 * E)
            for half, lanes in halves:
                for k in range(16):
                    i, part = place_of(half + k)
                    by_mode[i, rows, part] = turned[k, :, lanes]
        return carry

    lax.fori_loop(0, H // 16 // unroll, to_modes, 0)
    mixing = mixing_ref[...]
    for i in range(OWN):
        low = 16 * i
        table = legendre_ref[0, i]
        mixed[low:, :] = mix_degrees(table[low:], by_mode[i], gain_ref[low:], mixing)
        by_mode[i] = to_latitudes(table, mixed[...])

    def to_rows(step, carry):
        for piece in range(unroll):
            rows = pl.ds(pl.multiple_of((step * unroll + piece) * 16, 16), 16)
            blocks = []
            for half, _ in halves:
                slots = []
                for k in range(16):
                    i, part = place_of(half + k)
                    slots.append(by_mode[i, rows, part])
                blocks.append(jnp.concatenate(slots, axis=0))
            block = jnp.concatenate(blocks, axis=1)
            turned = jnp.dot(swap, block, preferred_element_type=jnp.float32).astype(jnp.bfloat16)
            turned = turned.reshape(16, 16, 2 * E)
            for half, lanes in halves:
                out_ref[rows, half : half + 16, :] = turned[:, :, lanes]
        return carry

    lax.fori_loop(0, H // 16 // unroll, to_rows, 0)


def spectral_pass(band, moved, legendre, gain, mixing, swap):
    whole = lambda *shape: pl.BlockSpec(shape, lambda step, band: (0,) * len(shape))
    return pl.pallas_call(
        spectral_kernel,
        grid_spec=pltpu.PrefetchScalarGridSpec(
            num_scalar_prefetch=1,
            grid=(1,),
            in_specs=[
                whole(H, SLOTS, E),
                pl.BlockSpec((1, OWN, L, H), lambda step, band: (band[0], 0, 0, 0)),
                whole(L, 1),
                whole(2 * E, 2 * E),
                whole(256, 256),
            ],
            out_specs=whole(H, SLOTS, E),
            scratch_shapes=[
                pltpu.VMEM((16, H, 2 * E), jnp.bfloat16),
                pltpu.VMEM((L, 2 * E), jnp.bfloat16),
            ],
        ),
        out_shape=jax.ShapeDtypeStruct((H, SLOTS, E), jnp.bfloat16),
        compiler_params=pltpu.CompilerParams(vmem_limit_bytes=VMEM_LIMIT),
        cost_estimate=pl.CostEstimate(flops=8 << 30, bytes_accessed=14 << 20, transcendentals=0),
        name="spectral_pass",
    )(band, moved, legendre, gain, mixing, swap)


def inverse_kernel(spatial_ref, x_ref, table_ref, out_ref):
    for j in range(x_ref.shape[0]):
        spatial = spatial_ref[:, j].reshape(BANDS * SLOTS, E)
        sums = jnp.dot(table_ref[...], spatial, preferred_element_type=jnp.float32)
        out_ref[j] = (x_ref[j].astype(jnp.float32) + jax.nn.gelu(sums)).astype(jnp.bfloat16)


def inverse_transform(spatial, x, table, step, flops):
    rows = x.shape[0]
    groups, _, size, _ = spatial.shape
    return pl.pallas_call(
        inverse_kernel,
        grid=(rows // step,),
        in_specs=[
            pl.BlockSpec((groups, step, size, E), lambda j: (0, j, 0, 0)),
            pl.BlockSpec((step, W, E), lambda j: (j, 0, 0)),
            pl.BlockSpec((W, BANDS * SLOTS), lambda j: (0, 0)),
        ],
        out_specs=pl.BlockSpec((step, W, E), lambda j: (j, 0, 0)),
        out_shape=jax.ShapeDtypeStruct((rows, W, E), jnp.bfloat16),
        compiler_params=pltpu.CompilerParams(vmem_limit_bytes=VMEM_LIMIT),
        cost_estimate=pl.CostEstimate(
            flops=flops, bytes_accessed=rows << 20, transcendentals=rows * W * E
        ),
        name="inverse_transform",
    )(spatial, x, table)


def difference_of(share, own, control):
    return jnp.where(share > 0.0, own.astype(jnp.float32) - control, 0.0)


def spread_kernel(weights_ref, share_ref, own_ref, control_ref, out_ref):
    step = pl.program_id(0)
    partial = 0.0
    for j in range(STEP):
        difference = difference_of(share_ref[0], own_ref[j], control_ref[j].astype(jnp.float32))
        squares = jnp.sum((difference * difference).reshape(W // 8, 8, E), axis=0)
        partial = partial + squares * weights_ref[step * STEP + j]

    @pl.when(step == 0)
    def _():
        out_ref[...] = partial

    @pl.when(step > 0)
    def _():
        out_ref[...] += partial


def spread_sums(weights, share, own, control):
    row = pl.BlockSpec((STEP, W, E), lambda j: (j, 0, 0))
    return pl.pallas_call(
        spread_kernel,
        grid=(ROWS // STEP,),
        in_specs=[pl.BlockSpec(memory_space=pltpu.SMEM), pl.BlockSpec(memory_space=pltpu.SMEM), row, row],
        out_specs=pl.BlockSpec((8, E), lambda j: (0, 0)),
        out_shape=jax.ShapeDtypeStruct((8, E), jnp.float32),
        compiler_params=pltpu.CompilerParams(vmem_limit_bytes=VMEM_LIMIT),
        cost_estimate=pl.CostEstimate(flops=9 << 20, bytes_accessed=11 << 20, transcendentals=0),
        name="spread_sums",
    )(weights, share, own, control)


def rescale_kernel(scale_ref, share_ref, own_ref, control_ref, out_ref):
    control = control_ref[...].astype(jnp.float32)
    difference = difference_of(share_ref[0], own_ref[...], control)
    out_ref[...] = (control + scale_ref[0] * difference).astype(jnp.bfloat16)


def rescaled(scale, share, own, control):
    row = pl.BlockSpec((STEP, W, E), lambda j: (j, 0, 0))
    return pl.pallas_call(
        rescale_kernel,
        grid=(ROWS // STEP,),
        in_specs=[pl.BlockSpec(memory_space=pltpu.SMEM), pl.BlockSpec(memory_space=pltpu.SMEM), row, row],
        out_specs=row,
        out_shape=jax.ShapeDtypeStruct((ROWS, W, E), jnp.bfloat16),
        compiler_params=pltpu.CompilerParams(vmem_limit_bytes=VMEM_LIMIT),
        cost_estimate=pl.CostEstimate(flops=9 << 20, bytes_accessed=17 << 20, transcendentals=0),
        name="rescaled",
    )(scale, share, own, control)


def scattered(pieces):
    member = lax.axis_index("member")
    kept = pieces[0]
    for z in range(1, DEPTH):
        arrived = lax.ppermute(pieces[z], "member", [(0, 2 * z)])
        kept = jnp.where(member == 2 * z, arrived, kept)
    return kept


def exchanged_along_z(pieces, z):
    result = pieces
    for shift in range(1, DEPTH):
        block = lax.dynamic_index_in_dim(pieces, (z + shift) % DEPTH, 0, keepdims=False)
        pairs = [(ring[a], ring[(a + shift) % DEPTH]) for ring in RINGS for a in range(DEPTH)]
        arrived = lax.ppermute(block, "member", pairs)
        result = lax.dynamic_update_index_in_dim(result, arrived, (z - shift) % DEPTH, 0)
    return result


def to_everyone(piece):
    across = lax.ppermute(piece, "member", [(2 * z, 2 * z + 1) for z in range(DEPTH)])
    piece = jnp.where(lax.axis_index("member") % 2 == 1, across, piece)
    return lax.all_gather(piece, "member", tiled=True, axis_index_groups=RINGS)


def doubled_along_z(value):
    z = lax.axis_index("member") // 2
    for stride in (4, 2, 1):
        pairs = [(2 * a, 2 * (a + stride)) for a in range(0, DEPTH, 2 * stride)]
        arrived = lax.ppermute(value, "member", pairs)
        value = jnp.where(z % (2 * stride) == stride, arrived, value)
    return value


def summed_over_band(partial):
    copies = jnp.broadcast_to(partial[None], (BANDS,) + partial.shape)
    return jnp.sum(lax.all_to_all(copies, "band", split_axis=0, concat_axis=0, tiled=True))


def shards(
    copy_fields,
    norm_gain,
    mix_real,
    mix_imag,
    filter_bank,
    perturbation_draw_numbers,
    amplitudes,
    desired_magnitude_slot,
):
    band_index = lax.axis_index("band")
    ahead_np, back_np, shared_ahead_np, shared_back_np = slot_tables()
    legendre_np = legendre_table(L, M, H).reshape(OWN, BANDS, L, H).transpose(1, 0, 2, 3)
    x = jnp.transpose(copy_fields[0], (0, 2, 1))

    global_rows = band_index * ROWS + jnp.arange(ROWS, dtype=jnp.int32)
    weights = jnp.sin((global_rows.astype(jnp.float32) + 0.5) * (math.pi / H)) * (math.pi / H)
    total_weight = jnp.sum(latitude_weights(H)) * (E * W)
    bank_rows = filter_bank.shape[0]
    draw_onehot = (jnp.arange(bank_rows, dtype=jnp.int32) == perturbation_draw_numbers[0]).astype(
        jnp.float32
    )
    degree_gain = jnp.sum(draw_onehot[:, None] * filter_bank, axis=0)

    legendre = rounded(legendre_np)
    gain = degree_gain[:, None]
    member = lax.axis_index("member")
    place = jnp.stack([band_index, member // 2])
    share = jnp.where(member > 0, 1.0, 0.0)[None]

    mixing = jnp.concatenate(
        [jnp.concatenate([mix_real, mix_imag], 1), jnp.concatenate([-mix_imag, mix_real], 1)], 0
    )
    z = member // 2

    fourier = forward_transform(x, norm_gain[None, :], weights, rounded(ahead_np), BANDS, STEP)
    moved = lax.all_to_all(fourier, "band", split_axis=0, concat_axis=0, tiled=True)

    control_x = scattered(
        [x[2 * a : 2 * a + 2] for a in range(DEPTH - 1)] + [jnp.concatenate([x[ROWS - 1 :]] * 2)]
    )
    control_gain = doubled_along_z(degree_gain[None, :])
    control_weights = lax.dynamic_slice(jnp.pad(weights, (0, 1)), (2 * z,), (2,))
    control_fourier = forward_transform(
        control_x, norm_gain[None, :], control_weights, rounded(shared_ahead_np), DEPTH, 2
    )
    control_fourier = exchanged_along_z(control_fourier, z).reshape(DEPTH, 2, BANDS, 4, E)
    control_fourier = control_fourier.transpose(2, 0, 1, 3, 4).reshape(BANDS, 16, 4, E)[:, :ROWS]
    moved, control_fourier = lax.optimization_barrier((moved, control_fourier))
    control_moved = lax.all_to_all(control_fourier, "band", split_axis=0, concat_axis=0, tiled=True)
    returned = spectral_pass(
        band_index[None],
        moved.reshape(H, SLOTS, E),
        legendre,
        gain,
        mixing,
        rounded(exchange_matrix()),
    )
    control_spatial = shared_spectral_pass(
        place,
        control_moved.reshape(H, 4, E).transpose(1, 0, 2),
        legendre,
        control_gain.reshape(L, 1),
        mixing,
    )
    control_spatial = lax.all_to_all(
        control_spatial.transpose(1, 0, 2).reshape(BANDS, ROWS, 4, E),
        "band",
        split_axis=0,
        concat_axis=0,
        tiled=True,
    )
    control_spatial, returned = lax.optimization_barrier((control_spatial, returned))
    spatial = lax.all_to_all(
        returned.reshape(BANDS, ROWS, SLOTS, E), "band", split_axis=0, concat_axis=0, tiled=True
    )
    control_spatial = jnp.pad(control_spatial, ((0, 0), (0, 1), (0, 0), (0, 0)))
    control_spatial = control_spatial.reshape(BANDS, DEPTH, 2, 4, E).transpose(1, 2, 0, 3, 4)
    control_spatial = exchanged_along_z(control_spatial.reshape(DEPTH, 2, BANDS * 4, E), z)
    control = to_everyone(
        inverse_transform(control_spatial, control_x, rounded(shared_back_np), 2, 1 << 29)
    )

    forecast = inverse_transform(spatial, x, rounded(back_np), STEP, 1 << 38)
    spread_sum = summed_over_band(spread_sums(weights, share, forecast, control))
    spread = spread_sum / total_weight
    target = jnp.sum(
        jnp.where(
            jnp.arange(amplitudes.shape[0], dtype=jnp.int32) == desired_magnitude_slot[0],
            amplitudes,
            0.0,
        )
    )
    scale = target / jnp.sqrt(spread + 1e-06)
    bred = rescaled(scale[None], share, forecast, control)
    return jnp.transpose(bred, (0, 2, 1))[None]


def solution(mesh):
    in_specs = (P("member", "band", None, None), P(), P(), P(), P(), P("member"), P(), P("member"))
    out_specs = P("member", "band", None, None)
    return jax.shard_map(shards, mesh=mesh, in_specs=in_specs, out_specs=out_specs, check_vma=False)
```

time: 444 us -> 423 us (0.953)
  blocking collectives: 80.6 us -> 0 us
  starting transfers between devices: 34.2 us -> 87.8 us
  local copies, waits for them, and re-layouts: 7.53 us -> 24 us
  Pallas kernels: 78.7 us -> 66.5 us
  other arithmetic: 5.05 us -> 10.2 us
    ppermute x8 -> x25, waiting for transfers between devices: 61.4 us -> 143 us  [the longest x1 62.2 us: to_everyone(): lax.ppermute(piece, 'member', [(2 * z, 2 * z + 1) for z in range(DEPTH)])]
    all_to_all x1 -> x0, blocking collectives: 80.6 us -> none  [shards(): lax.all_to_all(returned.reshape(BANDS, ROWS, SLOTS, E), 'band', split_axi...]
    all_to_all x1, waiting for transfers between devices: 79.2 us -> 0.01 us  [shards(): lax.all_to_all(fourier, 'band', split_axis=0, concat_axis=0, tiled=True)]
    ppermute x8 -> x25, starting transfers between devices: 20.5 us -> 54.1 us  [the longest x7 18.3 us: scattered(): arrived = lax.ppermute(pieces[z], 'member', [(0, 2 * z)])]
    all_to_all x0 -> x3, starting transfers between devices: none -> 20.2 us  [the longest x1 10.2 us: shards(): lax.all_to_all(control_fourier, 'band', split_axis=0, concat_axis=0, tile...]
    all_gather x1, waiting for transfers between devices: 74.3 us -> 63.1 us  [to_everyone(): return lax.all_gather(piece, 'member', tiled=True, axis_index_groups=RINGS)]
    pallas_call x4 -> x7, Pallas kernels: 54.3 us -> 47.7 us  [the longest x2 14 us: inverse_transform(): pl.pallas_call(inverse_kernel, grid=(rows // step,), in_specs=[pl.BlockSp...]
    pallas_call x1, Pallas kernels: 24.4 us -> 18.8 us  [spectral_pass(): pl.pallas_call(spectral_kernel, grid_spec=pltpu.PrefetchScalarGridSpec(nu...]
  transfers between devices with their start and end apart: 11 -> 31, of which waited for: 8 -> 13; matrix products, arithmetic and copies ran while one was open for 1% -> 6% of each run, Pallas kernels for 0% -> 9%
where the time goes in v2:
time: 423 us; the launch traced here: 421 us
  waiting for transfers between devices  215 us (51%)
  starting transfers between devices  87.8 us (21%)
  Pallas kernels  66.5 us (16%)
  local copies, waits for them, and re-layouts  24 us (6%)
  between operations  17.5 us (4%)
  other arithmetic  10.2 us (2%)
    all_gather x1, waiting for transfers between devices, to_everyone(): return lax.all_gather(piece, 'member', tiled=True, axis_index_groups=RINGS)  63.1 us
    ppermute x1, waiting for transfers between devices, to_everyone(): lax.ppermute(piece, 'member', [(2 * z, 2 * z + 1) for z in range(DEPTH)])  62.2 us
    ppermute x7, waiting for transfers between devices, scattered(): arrived = lax.ppermute(pieces[z], 'member', [(0, 2 * z)])  51.9 us
    ppermute x14, waiting for transfers between devices, exchanged_along_z(): arrived = lax.ppermute(block, 'member', pairs)  28.5 us
    pallas_call x1, Pallas kernels, spectral_pass(): pl.pallas_call(spectral_kernel, grid_spec=pltpu.PrefetchScalarGridSpec(nu...  18.8 us
    ppermute x7, starting transfers between devices, scattered(): arrived = lax.ppermute(pieces[z], 'member', [(0, 2 * z)])  18.3 us
    ppermute x14, starting transfers between devices, exchanged_along_z(): arrived = lax.ppermute(block, 'member', pairs)  18.2 us
    ppermute x3, starting transfers between devices, doubled_along_z(): arrived = lax.ppermute(value, 'member', pairs)  16.3 us
  transfers between devices with their start and end apart: 31, of which 13 were waited for; matrix products, arithmetic and copies ran while one was open for 6% of the time, Pallas kernels for 9%

profile of v2, /device:TPU:1, one launch (start us, length us, event | category | flops | bytes accessed | tf_op | source)
XLA Modules:
  0.0 421.1 jit_solution(5926378927133384614)
XLA Ops:
  8.4 9.7 %forward_transform.2 = bf16[16,15,32,384]{3,2,1,0:T(8,128)(2,1)} custom-call(f32[15]{0:T(128)} %sine_multiply_fusion.weights_ref, bf16[15,480,384]{2,1,0:T(8,128)(2,1)} %bitcast.92, f32[1,384]{1,0:T(1,128)} %broadcast_in_dim.76.gain_ref, bf16[512,480]{1,0:T(8,128)(2,1)} %constant.276.table_ref), custom_call_target="tpu_custom_call" | custom-call | flops 2831155200 | bytes 15728640 | tf_op jit(solution)/shard_map/forward_transform/pallas_call | solution.py:135
  18.2 7.6 %all-to-all-start = ((bf16[16,15,32,384]{3,2,1,0:T(8,128)(2,1)}), bf16[16,15,32,384]{3,2,1,0:T(8,128)(2,1)}, u32[]{:S(2)}, u32[]{:S(2)}) async-start(bf16[16,15,32,384]{3,2,1,0:T(8,128)(2,1)} %forward_transform.2), calls=%async_computation | async-start | bytes 11796480 | tf_op jit(solution)/shard_map/all_to_all | solution.py:442
  26.9 6.9 %collective-permute-start = (bf16[2,480,384]{2,1,0:T(8,128)(2,1)S(1)}, bf16[2,480,384]{2,1,0:T(8,128)(2,1)S(1)}, u32[]{:S(2)}, u32[]{:S(2)}) collective-permute-start(bf16[2,480,384]{2,1,0:T(8,128)(2,1)S(1)} %pad_maximum_fusion), channel_id=1, source_target_pairs={{0,224},{1,225},{2,226},{3,227},{4,228},{5,229},{6,230},{7,231},{8... | collective-permute-start | bytes 2211848 | tf_op jit(solution)/shard_map/ppermute | solution.py:371
  44.8 4.6 %collective-permute-done = bf16[2,480,384]{2,1,0:T(8,128)(2,1)S(1)} collective-permute-done((bf16[2,480,384]{2,1,0:T(8,128)(2,1)S(1)}, bf16[2,480,384]{2,1,0:T(8,128)(2,1)S(1)}, u32[]{:S(2)}, u32[]{:S(2)}) %collective-permute-start) | collective-permute-done | bytes 737312 | tf_op jit(solution)/shard_map/ppermute | solution.py:371
  58.2 12.4 %collective-permute-done.5 = bf16[2,480,384]{2,1,0:T(8,128)(2,1)S(1)} collective-permute-done((bf16[2,480,384]{2,1,0:T(8,128)(2,1)}, bf16[2,480,384]{2,1,0:T(8,128)(2,1)S(1)}, u32[]{:S(2)}, u32[]{:S(2)}) %collective-permute-start.5) | collective-permute-done | bytes 737312 | tf_op jit(solution)/shard_map/ppermute | solution.py:371
  70.7 15.8 %collective-permute-done.4 = bf16[2,480,384]{2,1,0:T(8,128)(2,1)} collective-permute-done((bf16[2,480,384]{2,1,0:T(8,128)(2,1)}, bf16[2,480,384]{2,1,0:T(8,128)(2,1)}, u32[]{:S(2)}, u32[]{:S(2)}) %collective-permute-start.4) | collective-permute-done | bytes 737312 | tf_op jit(solution)/shard_map/ppermute | solution.py:371
  86.5 15.8 %collective-permute-done.3 = bf16[2,480,384]{2,1,0:T(8,128)(2,1)} collective-permute-done((bf16[2,480,384]{2,1,0:T(8,128)(2,1)}, bf16[2,480,384]{2,1,0:T(8,128)(2,1)}, u32[]{:S(2)}, u32[]{:S(2)}) %collective-permute-start.3) | collective-permute-done | bytes 737312 | tf_op jit(solution)/shard_map/ppermute | solution.py:371
  108.9 8.2 %collective-permute-start.14 = (f32[1,240]{1,0:T(1,128)S(1)}, f32[1,240]{1,0:T(1,128)S(1)}, u32[]{:S(2)}, u32[]{:S(2)}) collective-permute-start(f32[1,240]{1,0:T(1,128)S(1)} %bitcast.104), channel_id=1, source_target_pairs={{0,128},{1,129},{2,130},{3,131},{4,132},{5,133},{6,134},{7,135},{8... | collective-permute-start | bytes 2888 | tf_op jit(solution)/shard_map/ppermute | solution.py:396
  119.5 4.4 %collective-permute-start.15 = (f32[1,240]{1,0:T(1,128)S(1)}, f32[1,240]{1,0:T(1,128)S(1)}, u32[]{:S(2)}, u32[]{:S(2)}) collective-permute-start(f32[1,240]{1,0:T(1,128)S(1)} %broadcast_select_fusion.1), channel_id=1, source_target_pairs={{0,64},{128,192},{1,65},{129,193},{2,66},{130,194},{3,67},{131,195... | collective-permute-start | bytes 2888 | tf_op jit(solution)/shard_map/ppermute | solution.py:396
  128.4 5.6 %collective-permute-done.9 = bf16[2,64,384]{2,1,0:T(8,128)(2,1)S(1)} collective-permute-done((bf16[2,64,384]{2,1,0:T(8,128)(2,1)S(1)}, bf16[2,64,384]{2,1,0:T(8,128)(2,1)S(1)}, u32[]{:S(2)}, u32[]{:S(2)}) %collective-permute-start.9) | collective-permute-done | bytes 98336 | tf_op jit(solution)/shard_map/ppermute | solution.py:381
  137.3 5.5 %collective-permute-done.10 = bf16[2,64,384]{2,1,0:T(8,128)(2,1)S(1)} collective-permute-done((bf16[2,64,384]{2,1,0:T(8,128)(2,1)S(1)}, bf16[2,64,384]{2,1,0:T(8,128)(2,1)S(1)}, u32[]{:S(2)}, u32[]{:S(2)}) %collective-permute-start.10) | collective-permute-done | bytes 98336 | tf_op jit(solution)/shard_map/ppermute | solution.py:381
  148.7 10.2 %all-to-all-start.1 = ((bf16[16,15,4,384]{3,2,1,0:T(4,128)(2,1)}), bf16[16,15,4,384]{3,2,1,0:T(4,128)(2,1)S(1)}, u32[]{:S(2)}, u32[]{:S(2)}) async-start(bf16[16,15,4,384]{3,2,1,0:T(4,128)(2,1)} %slice.44), calls=%async_computation.1 | async-start | bytes 1474560 | tf_op jit(solution)/shard_map/all_to_all | solution.py:455
  165.9 5.4 %all-to-all-done.1 = bf16[16,15,4,384]{3,2,1,0:T(4,128)(2,1)S(1)} async-done(((bf16[16,15,4,384]{3,2,1,0:T(4,128)(2,1)}), bf16[16,15,4,384]{3,2,1,0:T(4,128)(2,1)S(1)}, u32[]{:S(2)}, u32[]{:S(2)}) %all-to-all-start.1) | async-done | bytes 737312 | tf_op jit(solution)/shard_map/all_to_all | solution.py:455
  172.3 4.8 %shared_spectral_pass.1 = (bf16[2,240,384]{2,1,0:T(8,128)(2,1)}, bf16[2,240,384]{2,1,0:T(8,128)(2,1)}) custom-call(s32[2]{0:T(128)} %pad_add_fusion.place_ref, bf16[4,240,384]{2,1,0:T(8,128)(2,1)} %bitcast.97, bf16[4,240,384]{2,1,0:T(8,128)(2,1)} %bitcast.98, bf16[16,15,240,240]{3,2,1,0:T(8,128)(2,1)} %constant.278.legendre_ref, f32[240,1]{1,0:T(8,128)} %copy.31.gain_ref, ...), custom_call_target="tpu_custom_call" | custom-call | flops 1073741824 | bytes 4194304 | tf_op jit(solution)/shard_map/shared_spectral_pass/pallas_call | solution.py:179
  179.4 4.3 %all-to-all-start.2 = ((bf16[16,15,4,384]{3,2,1,0:T(4,128)(2,1)}), bf16[16,15,4,384]{3,2,1,0:T(4,128)(2,1)S(1)}, u32[]{:S(2)}, u32[]{:S(2)}) async-start(bf16[16,15,4,384]{3,2,1,0:T(4,128)(2,1)} %bitcast.29), calls=%async_computation.2 | async-start | bytes 1474560 | tf_op jit(solution)/shard_map/all_to_all | solution.py:471
  183.7 18.8 %spectral_pass.1 = bf16[240,32,384]{2,1,0:T(8,128)(2,1)} custom-call(s32[1]{0:T(128)} %bitcast.2.band_ref, bf16[240,32,384]{2,1,0:T(8,128)(2,1)} %bitcast.30.moved_ref, bf16[16,15,240,240]{3,2,1,0:T(8,128)(2,1)} %constant.278.legendre_ref, f32[240,1]{1,0:T(8,128)} %copy.33.gain_ref, bf16[768,768]{1,0:T(8,128)(2,1)} %maximum_maximum_fusion.mixing_ref, ...), custom_call_target="tpu_custom_call" | custom-call | flops 8589934592 | bytes 14680064 | tf_op jit(solution)/shard_map/spectral_pass/pallas_call | solution.py:259
  202.5 5.8 %all-to-all-start.3 = ((bf16[16,15,32,384]{3,2,1,0:T(8,128)(2,1)}), bf16[16,15,32,384]{3,2,1,0:T(8,128)(2,1)}, u32[]{:S(2)}, u32[]{:S(2)}) async-start(bf16[16,15,32,384]{3,2,1,0:T(8,128)(2,1)} %bitcast.91), calls=%async_computation.3 | async-start | bytes 11796480 | tf_op jit(solution)/shard_map/all_to_all | solution.py:479
  225.1 13.4 %collective-permute-done.19 = bf16[2,64,384]{2,1,0:T(8,128)(2,1)S(1)} collective-permute-done((bf16[2,64,384]{2,1,0:T(8,128)(2,1)S(1)}, bf16[2,64,384]{2,1,0:T(8,128)(2,1)S(1)}, u32[]{:S(2)}, u32[]{:S(2)}) %collective-permute-start.19) | collective-permute-done | bytes 98336 | tf_op jit(solution)/shard_map/ppermute | solution.py:381
  244.2 62.2 %collective-permute-done.24 = bf16[2,480,384]{2,1,0:T(8,128)(2,1)S(1)} collective-permute-done((bf16[2,480,384]{2,1,0:T(8,128)(2,1)}, bf16[2,480,384]{2,1,0:T(8,128)(2,1)S(1)}, u32[]{:S(2)}, u32[]{:S(2)}) %collective-permute-start.24) | collective-permute-done | bytes 737312 | tf_op jit(solution)/shard_map/ppermute | solution.py:387
  308.5 10.6 %inverse_transform.2.own_ref = bf16[15,480,384]{2,1,0:T(8,128)(2,1)} custom-call(bf16[16,15,32,384]{3,2,1,0:T(8,128)(2,1)} %all-to-all-done.3.spatial_ref, bf16[15,480,384]{2,1,0:T(8,128)(2,1)} %bitcast.96, bf16[480,512]{1,0:T(8,128)(2,1)} %constant.280.table_ref), custom_call_target="tpu_custom_call" | custom-call | flops 274877906944 | bytes 15728640 | tf_op jit(solution)/shard_map/inverse_transform/pallas_call | solution.py:294
  319.1 63.1 %all-gather.2.cloned.1.call-done.control_ref = bf16[16,480,384]{2,1,0:T(8,128)(2,1)} async-done(((bf16[2,480,384]{2,1,0:T(8,128)(2,1)}), bf16[16,480,384]{2,1,0:T(8,128)(2,1)}) %all-gather.2.cloned.1.call-update) | async-done | bytes 5898256 | tf_op jit(solution)/shard_map/all_gather | solution.py:389
  382.2 7.2 %spread_sums.1 = f32[8,384]{1,0:T(8,128)} custom-call(f32[15]{0:T(128)} %sine_multiply_fusion.weights_ref, f32[1]{0:T(128)} %bitcast.1.share_ref, bf16[15,480,384]{2,1,0:T(8,128)(2,1)} %inverse_transform.2.own_ref, bf16[16,480,384]{2,1,0:T(8,128)(2,1)} %all-gather.2.cloned.1.call-done.control_ref), custom_call_target="tpu_custom_call" | custom-call | flops 9437184 | bytes 11534336 | tf_op jit(solution)/shard_map/spread_sums/pallas_call | solution.py:335
  390.8 5.9 %all-to-all-start.4 = ((f32[16,8,384]{2,1,0:T(8,128)}), f32[16,8,384]{2,1,0:T(8,128)S(1)}, u32[]{:S(2)}, u32[]{:S(2)}) async-start(f32[16,8,384]{2,1,0:T(8,128)} %broadcast_in_dim.93), calls=%async_computation.4 | async-start | bytes 393216 | tf_op jit(solution)/shard_map/all_to_all | solution.py:403
  405.4 8.9 %rescaled.1 = bf16[15,480,384]{2,1,0:T(8,128)(2,1)} custom-call(f32[1]{0:T(128)} %bitcast.49.scale_ref, f32[1]{0:T(128)} %bitcast.1.share_ref, bf16[15,480,384]{2,1,0:T(8,128)(2,1)} %inverse_transform.2.own_ref, bf16[16,480,384]{2,1,0:T(8,128)(2,1)} %all-gather.2.cloned.1.call-done.control_ref), custom_call_target="tpu_custom_call" | custom-call | flops 9437184 | bytes 17825792 | tf_op jit(solution)/shard_map/rescaled/pallas_call | solution.py:355
  (106 shorter events, 86.5 us)
Async XLA Ops:
  18.2 130.5 %all-to-all-start = ((bf16[16,15,32,384]{3,2,1,0:T(8,128)(2,1)}), bf16[16,15,32,384]{3,2,1,0:T(8,128)(2,1)}, u32[]{:S(2)}, u32[]{:S(2)}) async-start(bf16[16,15,32,384]{3,2,1,0:T(8,128)(2,1)} %forward_transform.2), calls=%async_computation | async-start | bytes 11796480 | tf_op jit(solution)/shard_map/all_to_all | solution.py:442
  26.9 22.5 %collective-permute-start = (bf16[2,480,384]{2,1,0:T(8,128)(2,1)S(1)}, bf16[2,480,384]{2,1,0:T(8,128)(2,1)S(1)}, u32[]{:S(2)}, u32[]{:S(2)}) collective-permute-start(bf16[2,480,384]{2,1,0:T(8,128)(2,1)S(1)} %pad_maximum_fusion), channel_id=1, source_target_pairs={{0,224},{1,225},{2,226},{3,227},{4,228},{5,229},{6,230},{7,231},{8... | collective-permute-start | bytes 2211848 | tf_op jit(solution)/shard_map/ppermute | solution.py:371
  37.8 17.0 %collective-permute-start.6 = (bf16[2,480,384]{2,1,0:T(8,128)(2,1)S(1)}, bf16[2,480,384]{2,1,0:T(8,128)(2,1)S(1)}, u32[]{:S(2)}, u32[]{:S(2)}) collective-permute-start(bf16[2,480,384]{2,1,0:T(8,128)(2,1)S(1)} %get-tuple-element.17), channel_id=1, source_target_pairs={{0,32},{1,33},{2,34},{3,35},{4,36},{5,37},{6,38},{7,39},{8,40},{9,... | collective-permute-start | bytes 2211848 | tf_op jit(solution)/shard_map/ppermute | solution.py:371
  39.1 31.6 %collective-permute-start.5 = (bf16[2,480,384]{2,1,0:T(8,128)(2,1)}, bf16[2,480,384]{2,1,0:T(8,128)(2,1)S(1)}, u32[]{:S(2)}, u32[]{:S(2)}) collective-permute-start(bf16[2,480,384]{2,1,0:T(8,128)(2,1)} %get-tuple-element.18), channel_id=1, source_target_pairs={{0,64},{1,65},{2,66},{3,67},{4,68},{5,69},{6,70},{7,71},{8,72},{9,... | collective-permute-start | bytes 2211848 | tf_op jit(solution)/shard_map/ppermute | solution.py:371
  40.4 46.1 %collective-permute-start.4 = (bf16[2,480,384]{2,1,0:T(8,128)(2,1)}, bf16[2,480,384]{2,1,0:T(8,128)(2,1)}, u32[]{:S(2)}, u32[]{:S(2)}) collective-permute-start(bf16[2,480,384]{2,1,0:T(8,128)(2,1)} %get-tuple-element.19), channel_id=1, source_target_pairs={{0,96},{1,97},{2,98},{3,99},{4,100},{5,101},{6,102},{7,103},{8,104... | collective-permute-start | bytes 2211848 | tf_op jit(solution)/shard_map/ppermute | solution.py:371
  42.6 59.7 %collective-permute-start.3 = (bf16[2,480,384]{2,1,0:T(8,128)(2,1)}, bf16[2,480,384]{2,1,0:T(8,128)(2,1)}, u32[]{:S(2)}, u32[]{:S(2)}) collective-permute-start(bf16[2,480,384]{2,1,0:T(8,128)(2,1)} %get-tuple-element.20), channel_id=1, source_target_pairs={{0,128},{1,129},{2,130},{3,131},{4,132},{5,133},{6,134},{7,135},{8... | collective-permute-start | bytes 2211848 | tf_op jit(solution)/shard_map/ppermute | solution.py:371
  49.4 53.0 %collective-permute-start.2 = (bf16[2,480,384]{2,1,0:T(8,128)(2,1)}, bf16[2,480,384]{2,1,0:T(8,128)(2,1)}, u32[]{:S(2)}, u32[]{:S(2)}) collective-permute-start(bf16[2,480,384]{2,1,0:T(8,128)(2,1)} %get-tuple-element.21), channel_id=1, source_target_pairs={{0,160},{1,161},{2,162},{3,163},{4,164},{5,165},{6,166},{7,167},{8... | collective-permute-start | bytes 2211848 | tf_op jit(solution)/shard_map/ppermute | solution.py:371
  54.8 47.6 %collective-permute-start.1 = (bf16[2,480,384]{2,1,0:T(8,128)(2,1)S(1)}, bf16[2,480,384]{2,1,0:T(8,128)(2,1)}, u32[]{:S(2)}, u32[]{:S(2)}) collective-permute-start(bf16[2,480,384]{2,1,0:T(8,128)(2,1)S(1)} %get-tuple-element.22), channel_id=1, source_target_pairs={{0,192},{1,193},{2,194},{3,195},{4,196},{5,197},{6,198},{7,199},{8... | collective-permute-start | bytes 2211848 | tf_op jit(solution)/shard_map/ppermute | solution.py:371
  108.9 10.5 %collective-permute-start.14 = (f32[1,240]{1,0:T(1,128)S(1)}, f32[1,240]{1,0:T(1,128)S(1)}, u32[]{:S(2)}, u32[]{:S(2)}) collective-permute-start(f32[1,240]{1,0:T(1,128)S(1)} %bitcast.104), channel_id=1, source_target_pairs={{0,128},{1,129},{2,130},{3,131},{4,132},{5,133},{6,134},{7,135},{8... | collective-permute-start | bytes 2888 | tf_op jit(solution)/shard_map/ppermute | solution.py:396
  119.5 40.5 %collective-permute-start.15 = (f32[1,240]{1,0:T(1,128)S(1)}, f32[1,240]{1,0:T(1,128)S(1)}, u32[]{:S(2)}, u32[]{:S(2)}) collective-permute-start(f32[1,240]{1,0:T(1,128)S(1)} %broadcast_select_fusion.1), channel_id=1, source_target_pairs={{0,64},{128,192},{1,65},{129,193},{2,66},{130,194},{3,67},{131,195... | collective-permute-start | bytes 2888 | tf_op jit(solution)/shard_map/ppermute | solution.py:396
  123.9 20.9 %collective-permute-start.13 = (bf16[2,64,384]{2,1,0:T(8,128)(2,1)S(1)}, bf16[2,64,384]{2,1,0:T(8,128)(2,1)S(1)}, u32[]{:S(2)}, u32[]{:S(2)}) collective-permute-start(bf16[2,64,384]{2,1,0:T(8,128)(2,1)S(1)} %get-tuple-element.30), channel_id=1, source_target_pairs={{0,224},{32,0},{64,32},{96,64},{128,96},{160,128},{192,160},{224,1... | collective-permute-start | bytes 294920 | tf_op jit(solution)/shard_map/ppermute | solution.py:381
  124.0 20.2 %collective-permute-start.12 = (bf16[2,64,384]{2,1,0:T(8,128)(2,1)S(1)}, bf16[2,64,384]{2,1,0:T(8,128)(2,1)S(1)}, u32[]{:S(2)}, u32[]{:S(2)}) collective-permute-start(bf16[2,64,384]{2,1,0:T(8,128)(2,1)S(1)} %get-tuple-element.31), channel_id=1, source_target_pairs={{0,192},{32,224},{64,0},{96,32},{128,64},{160,96},{192,128},{224,1... | collective-permute-start | bytes 294920 | tf_op jit(solution)/shard_map/ppermute | solution.py:381
  124.5 19.0 %collective-permute-start.11 = (bf16[2,64,384]{2,1,0:T(8,128)(2,1)S(1)}, bf16[2,64,384]{2,1,0:T(8,128)(2,1)S(1)}, u32[]{:S(2)}, u32[]{:S(2)}) collective-permute-start(bf16[2,64,384]{2,1,0:T(8,128)(2,1)S(1)} %get-tuple-element.32), channel_id=1, source_target_pairs={{0,160},{32,192},{64,224},{96,0},{128,32},{160,64},{192,96},{224,1... | collective-permute-start | bytes 294920 | tf_op jit(solution)/shard_map/ppermute | solution.py:381
  148.7 22.6 %all-to-all-start.1 = ((bf16[16,15,4,384]{3,2,1,0:T(4,128)(2,1)}), bf16[16,15,4,384]{3,2,1,0:T(4,128)(2,1)S(1)}, u32[]{:S(2)}, u32[]{:S(2)}) async-start(bf16[16,15,4,384]{3,2,1,0:T(4,128)(2,1)} %slice.44), calls=%async_computation.1 | async-start | bytes 1474560 | tf_op jit(solution)/shard_map/all_to_all | solution.py:455
  179.4 23.1 %all-to-all-start.2 = ((bf16[16,15,4,384]{3,2,1,0:T(4,128)(2,1)}), bf16[16,15,4,384]{3,2,1,0:T(4,128)(2,1)S(1)}, u32[]{:S(2)}, u32[]{:S(2)}) async-start(bf16[16,15,4,384]{3,2,1,0:T(4,128)(2,1)} %bitcast.29), calls=%async_computation.2 | async-start | bytes 1474560 | tf_op jit(solution)/shard_map/all_to_all | solution.py:471
  202.5 105.9 %all-to-all-start.3 = ((bf16[16,15,32,384]{3,2,1,0:T(8,128)(2,1)}), bf16[16,15,32,384]{3,2,1,0:T(8,128)(2,1)}, u32[]{:S(2)}, u32[]{:S(2)}) async-start(bf16[16,15,32,384]{3,2,1,0:T(8,128)(2,1)} %bitcast.91), calls=%async_computation.3 | async-start | bytes 11796480 | tf_op jit(solution)/shard_map/all_to_all | solution.py:479
  208.3 173.9 %all-gather.2.cloned.1.call-start = ((), (), s32[]{:S(2)}) async-start(), calls=%async_computation.5 | async-start | bytes 6635520 | tf_op jit(solution)/shard_map/all_gather | solution.py:389
  217.0 21.6 %collective-permute-start.23 = (bf16[2,64,384]{2,1,0:T(8,128)(2,1)S(1)}, bf16[2,64,384]{2,1,0:T(8,128)(2,1)S(1)}, u32[]{:S(2)}, u32[]{:S(2)}) collective-permute-start(bf16[2,64,384]{2,1,0:T(8,128)(2,1)S(1)} %get-tuple-element.23), channel_id=1, source_target_pairs={{0,224},{32,0},{64,32},{96,64},{128,96},{160,128},{192,160},{224,1... | collective-permute-start | bytes 294920 | tf_op jit(solution)/shard_map/ppermute | solution.py:381
  217.9 20.6 %collective-permute-start.22 = (bf16[2,64,384]{2,1,0:T(8,128)(2,1)S(1)}, bf16[2,64,384]{2,1,0:T(8,128)(2,1)S(1)}, u32[]{:S(2)}, u32[]{:S(2)}) collective-permute-start(bf16[2,64,384]{2,1,0:T(8,128)(2,1)S(1)} %get-tuple-element.24), channel_id=1, source_target_pairs={{0,192},{32,224},{64,0},{96,32},{128,64},{160,96},{192,128},{224,1... | collective-permute-start | bytes 294920 | tf_op jit(solution)/shard_map/ppermute | solution.py:381
  219.4 19.1 %collective-permute-start.21 = (bf16[2,64,384]{2,1,0:T(8,128)(2,1)S(1)}, bf16[2,64,384]{2,1,0:T(8,128)(2,1)S(1)}, u32[]{:S(2)}, u32[]{:S(2)}) collective-permute-start(bf16[2,64,384]{2,1,0:T(8,128)(2,1)S(1)} %get-tuple-element.25), channel_id=1, source_target_pairs={{0,160},{32,192},{64,224},{96,0},{128,32},{160,64},{192,96},{224,1... | collective-permute-start | bytes 294920 | tf_op jit(solution)/shard_map/ppermute | solution.py:381
  222.1 16.4 %collective-permute-start.20 = (bf16[2,64,384]{2,1,0:T(8,128)(2,1)S(1)}, bf16[2,64,384]{2,1,0:T(8,128)(2,1)S(1)}, u32[]{:S(2)}, u32[]{:S(2)}) collective-permute-start(bf16[2,64,384]{2,1,0:T(8,128)(2,1)S(1)} %get-tuple-element.26), channel_id=1, source_target_pairs={{0,128},{32,160},{64,192},{96,224},{128,0},{160,32},{192,64},{224,... | collective-permute-start | bytes 294920 | tf_op jit(solution)/shard_map/ppermute | solution.py:381
  224.4 14.1 %collective-permute-start.19 = (bf16[2,64,384]{2,1,0:T(8,128)(2,1)S(1)}, bf16[2,64,384]{2,1,0:T(8,128)(2,1)S(1)}, u32[]{:S(2)}, u32[]{:S(2)}) collective-permute-start(bf16[2,64,384]{2,1,0:T(8,128)(2,1)S(1)} %get-tuple-element.27), channel_id=1, source_target_pairs={{0,96},{32,128},{64,160},{96,192},{128,224},{160,0},{192,32},{224,... | collective-permute-start | bytes 294920 | tf_op jit(solution)/shard_map/ppermute | solution.py:381
  242.8 63.6 %collective-permute-start.24 = (bf16[2,480,384]{2,1,0:T(8,128)(2,1)}, bf16[2,480,384]{2,1,0:T(8,128)(2,1)S(1)}, u32[]{:S(2)}, u32[]{:S(2)}) collective-permute-start(bf16[2,480,384]{2,1,0:T(8,128)(2,1)} %inverse_transform.3), channel_id=1, source_target_pairs={{0,16},{32,48},{64,80},{96,112},{128,144},{160,176},{192,208},{224... | collective-permute-start | bytes 2211848 | tf_op jit(solution)/shard_map/ppermute | solution.py:387
  390.8 12.6 %all-to-all-start.4 = ((f32[16,8,384]{2,1,0:T(8,128)}), f32[16,8,384]{2,1,0:T(8,128)S(1)}, u32[]{:S(2)}, u32[]{:S(2)}) async-start(f32[16,8,384]{2,1,0:T(8,128)} %broadcast_in_dim.93), calls=%async_computation.4 | async-start | bytes 393216 | tf_op jit(solution)/shard_map/all_to_all | solution.py:403
  (13 other events, 175.5 us)
Sparse Core Ops, SparseCore 0:
  308.6 73.5 all-gather.1

commit v3 on v2

--- a/solution.py
+++ b/solution.py
@@ -21,6 +21,7 @@
 DEPTH = 8
 RINGS = [[2 * z + h for z in range(DEPTH)] for h in range(2)]
 STEP = 3
+TOTAL_WEIGHT = float(np.sum(np.sin((np.arange(H) + 0.5) * np.pi / H)) * np.pi / H * E * W)
 VMEM_LIMIT = 58 * 1024 * 1024
 
 
@@ -83,11 +84,6 @@
     return (forward_table, inverse_table)
 
 
-def latitude_weights(lat_count):
-    colatitude = (jnp.arange(lat_count, dtype=jnp.float32) + 0.5) * (math.pi / lat_count)
-    return jnp.sin(colatitude) * (math.pi / lat_count)
-
-
 def slot_tables():
     forward, inverse = fourier_tables(W, np.arange(M))
     ahead = np.zeros((W, 2, 16, BANDS))
@@ -129,7 +125,7 @@
         out_ref[:, j] = sums.reshape(out_ref.shape[0], out_ref.shape[2], E)
 
 
-def forward_transform(x, gain, weights, table, groups, step):
+def forward_transform(x, gain, weights, table, groups, step, flops):
     rows = x.shape[0]
     size = BANDS * SLOTS // groups
     return pl.pallas_call(
@@ -144,9 +140,7 @@
         out_specs=pl.BlockSpec((groups, step, size, E), lambda j: (0, j, 0, 0)),
         out_shape=jax.ShapeDtypeStruct((groups, rows, size, E), jnp.bfloat16),
         compiler_params=pltpu.CompilerParams(vmem_limit_bytes=VMEM_LIMIT),
-        cost_estimate=pl.CostEstimate(
-            flops=2 * rows * BANDS * SLOTS * W * E, bytes_accessed=rows << 20, transcendentals=0
-        ),
+        cost_estimate=pl.CostEstimate(flops=flops, bytes_accessed=rows << 20, transcendentals=0),
         name="forward_transform",
     )(weights, x, gain, table)
 
@@ -313,7 +307,7 @@
     return jnp.where(share > 0.0, own.astype(jnp.float32) - control, 0.0)
 
 
-def spread_kernel(weights_ref, share_ref, own_ref, control_ref, out_ref):
+def spread_kernel(weights_ref, share_ref, own_ref, control_ref, out_ref, total):
     step = pl.program_id(0)
     partial = 0.0
     for j in range(STEP):
@@ -323,45 +317,62 @@
 
     @pl.when(step == 0)
     def _():
-        out_ref[...] = partial
+        total[...] = partial
 
     @pl.when(step > 0)
     def _():
-        out_ref[...] += partial
+        total[...] += partial
+
+    @pl.when(step == ROWS // STEP - 1)
+    def _():
+        lanes = total[:, :128] + total[:, 128:256] + total[:, 256:]
+        out_ref[...] = jnp.broadcast_to(lanes[None], out_ref.shape)
 
 
 def spread_sums(weights, share, own, control):
     row = pl.BlockSpec((STEP, W, E), lambda j: (j, 0, 0))
+    scalars = pl.BlockSpec(memory_space=pltpu.SMEM)
     return pl.pallas_call(
         spread_kernel,
         grid=(ROWS // STEP,),
-        in_specs=[pl.BlockSpec(memory_space=pltpu.SMEM), pl.BlockSpec(memory_space=pltpu.SMEM), row, row],
-        out_specs=pl.BlockSpec((8, E), lambda j: (0, 0)),
-        out_shape=jax.ShapeDtypeStruct((8, E), jnp.float32),
+        in_specs=[scalars, scalars, row, row],
+        out_specs=pl.BlockSpec((BANDS, 8, 128), lambda j: (0, 0, 0)),
+        out_shape=jax.ShapeDtypeStruct((BANDS, 8, 128), jnp.float32),
+        scratch_shapes=[pltpu.VMEM((8, E), jnp.float32)],
         compiler_params=pltpu.CompilerParams(vmem_limit_bytes=VMEM_LIMIT),
         cost_estimate=pl.CostEstimate(flops=9 << 20, bytes_accessed=11 << 20, transcendentals=0),
         name="spread_sums",
     )(weights, share, own, control)
 
 
-def rescale_kernel(scale_ref, share_ref, own_ref, control_ref, out_ref):
-    control = control_ref[...].astype(jnp.float32)
-    difference = difference_of(share_ref[0], own_ref[...], control)
-    out_ref[...] = (control + scale_ref[0] * difference).astype(jnp.bfloat16)
-
-
-def rescaled(scale, share, own, control):
+def rescale_kernel(share_ref, target_ref, sums_ref, own_ref, control_ref, out_ref):
+    total = jnp.sum(jnp.sum(sums_ref[...], axis=0), axis=(0, 1), keepdims=True)
+    scale = target_ref[0] / jnp.sqrt(total * (1.0 / TOTAL_WEIGHT) + 1e-06)
+    for j in range(STEP):
+        control = control_ref[j].astype(jnp.float32)
+        difference = difference_of(share_ref[0], own_ref[j], control)
+        out_ref[j] = (control + scale * difference).astype(jnp.bfloat16)
+
+
+def rescaled(share, target, sums, own, control):
     row = pl.BlockSpec((STEP, W, E), lambda j: (j, 0, 0))
+    scalars = pl.BlockSpec(memory_space=pltpu.SMEM)
     return pl.pallas_call(
         rescale_kernel,
         grid=(ROWS // STEP,),
-        in_specs=[pl.BlockSpec(memory_space=pltpu.SMEM), pl.BlockSpec(memory_space=pltpu.SMEM), row, row],
+        in_specs=[
+            scalars,
+            scalars,
+            pl.BlockSpec((BANDS, 8, 128), lambda j: (0, 0, 0)),
+            row,
+            row,
+        ],
         out_specs=row,
         out_shape=jax.ShapeDtypeStruct((ROWS, W, E), jnp.bfloat16),
         compiler_params=pltpu.CompilerParams(vmem_limit_bytes=VMEM_LIMIT),
         cost_estimate=pl.CostEstimate(flops=9 << 20, bytes_accessed=17 << 20, transcendentals=0),
         name="rescaled",
-    )(scale, share, own, control)
+    )(share, target, sums, own, control)
 
 
 def scattered(pieces):
@@ -373,22 +384,6 @@
     return kept
 
 
-def exchanged_along_z(pieces, z):
-    result = pieces
-    for shift in range(1, DEPTH):
-        block = lax.dynamic_index_in_dim(pieces, (z + shift) % DEPTH, 0, keepdims=False)
-        pairs = [(ring[a], ring[(a + shift) % DEPTH]) for ring in RINGS for a in range(DEPTH)]
-        arrived = lax.ppermute(block, "member", pairs)
-        result = lax.dynamic_update_index_in_dim(result, arrived, (z - shift) % DEPTH, 0)
-    return result
-
-
-def to_everyone(piece):
-    across = lax.ppermute(piece, "member", [(2 * z, 2 * z + 1) for z in range(DEPTH)])
-    piece = jnp.where(lax.axis_index("member") % 2 == 1, across, piece)
-    return lax.all_gather(piece, "member", tiled=True, axis_index_groups=RINGS)
-
-
 def doubled_along_z(value):
     z = lax.axis_index("member") // 2
     for stride in (4, 2, 1):
@@ -398,9 +393,15 @@
     return value
 
 
-def summed_over_band(partial):
-    copies = jnp.broadcast_to(partial[None], (BANDS,) + partial.shape)
-    return jnp.sum(lax.all_to_all(copies, "band", split_axis=0, concat_axis=0, tiled=True))
+def exchanged_along_z(pieces):
+    return lax.all_to_all(
+        pieces, "member", split_axis=0, concat_axis=0, axis_index_groups=RINGS, tiled=True
+    )
+
+
+def across(value):
+    arrived = lax.ppermute(value, "member", [(2 * z, 2 * z + 1) for z in range(DEPTH)])
+    return jnp.where(lax.axis_index("member") % 2 == 1, arrived, value)
 
 
 def shards(
@@ -420,7 +421,6 @@
 
     global_rows = band_index * ROWS + jnp.arange(ROWS, dtype=jnp.int32)
     weights = jnp.sin((global_rows.astype(jnp.float32) + 0.5) * (math.pi / H)) * (math.pi / H)
-    total_weight = jnp.sum(latitude_weights(H)) * (E * W)
     bank_rows = filter_bank.shape[0]
     draw_onehot = (jnp.arange(bank_rows, dtype=jnp.int32) == perturbation_draw_numbers[0]).astype(
         jnp.float32
@@ -438,20 +438,23 @@
     )
     z = member // 2
 
-    fourier = forward_transform(x, norm_gain[None, :], weights, rounded(ahead_np), BANDS, STEP)
+    fourier = forward_transform(x, norm_gain[None, :], weights, rounded(ahead_np), BANDS, STEP, 1 << 37)
     moved = lax.all_to_all(fourier, "band", split_axis=0, concat_axis=0, tiled=True)
 
-    control_x = scattered(
-        [x[2 * a : 2 * a + 2] for a in range(DEPTH - 1)] + [jnp.concatenate([x[ROWS - 1 :]] * 2)]
-    )
-    control_gain = doubled_along_z(degree_gain[None, :])
+    control_x = across(
+        scattered(
+            [x[2 * a : 2 * a + 2] for a in range(DEPTH - 1)]
+            + [jnp.concatenate([x[ROWS - 1 :]] * 2)]
+        )
+    )
+    control_gain = across(doubled_along_z(degree_gain[None, :]))
     control_weights = lax.dynamic_slice(jnp.pad(weights, (0, 1)), (2 * z,), (2,))
     control_fourier = forward_transform(
-        control_x, norm_gain[None, :], control_weights, rounded(shared_ahead_np), DEPTH, 2
-    )
-    control_fourier = exchanged_along_z(control_fourier, z).reshape(DEPTH, 2, BANDS, 4, E)
+        control_x, norm_gain[None, :], control_weights, rounded(shared_ahead_np), DEPTH, 2, 1 << 29
+    )
+    moved, control_fourier = lax.optimization_barrier((moved, control_fourier))
+    control_fourier = exchanged_along_z(control_fourier).reshape(DEPTH, 2, BANDS, 4, E)
     control_fourier = control_fourier.transpose(2, 0, 1, 3, 4).reshape(BANDS, 16, 4, E)[:, :ROWS]
-    moved, control_fourier = lax.optimization_barrier((moved, control_fourier))
     control_moved = lax.all_to_all(control_fourier, "band", split_axis=0, concat_axis=0, tiled=True)
     returned = spectral_pass(
         band_index[None],
@@ -475,20 +478,24 @@
         concat_axis=0,
         tiled=True,
     )
+    control_spatial = jnp.pad(control_spatial, ((0, 0), (0, 1), (0, 0), (0, 0)))
+    control_spatial = control_spatial.reshape(BANDS, DEPTH, 2, 4, E).transpose(1, 2, 0, 3, 4)
+    control_spatial = exchanged_along_z(control_spatial.reshape(DEPTH, 2, BANDS * 4, E))
     control_spatial, returned = lax.optimization_barrier((control_spatial, returned))
     spatial = lax.all_to_all(
         returned.reshape(BANDS, ROWS, SLOTS, E), "band", split_axis=0, concat_axis=0, tiled=True
     )
-    control_spatial = jnp.pad(control_spatial, ((0, 0), (0, 1), (0, 0), (0, 0)))
-    control_spatial = control_spatial.reshape(BANDS, DEPTH, 2, 4, E).transpose(1, 2, 0, 3, 4)
-    control_spatial = exchanged_along_z(control_spatial.reshape(DEPTH, 2, BANDS * 4, E), z)
-    control = to_everyone(
-        inverse_transform(control_spatial, control_x, rounded(shared_back_np), 2, 1 << 29)
-    )
+    control = inverse_transform(control_spatial, control_x, rounded(shared_back_np), 2, 1 << 29)
+    control = lax.all_gather(control, "member", tiled=True, axis_index_groups=RINGS)
 
     forecast = inverse_transform(spatial, x, rounded(back_np), STEP, 1 << 38)
-    spread_sum = summed_over_band(spread_sums(weights, share, forecast, control))
-    spread = spread_sum / total_weight
+    sums = lax.all_to_all(
+        spread_sums(weights, share, forecast, control),
+        "band",
+        split_axis=0,
+        concat_axis=0,
+        tiled=True,
+    )
     target = jnp.sum(
         jnp.where(
             jnp.arange(amplitudes.shape[0], dtype=jnp.int32) == desired_magnitude_slot[0],
@@ -496,8 +503,7 @@
             0.0,
         )
     )
-    scale = target / jnp.sqrt(spread + 1e-06)
-    bred = rescaled(scale[None], share, forecast, control)
+    bred = rescaled(share, target[None], sums, forecast, control)
     return jnp.transpose(bred, (0, 2, 1))[None]
 
 

time: 423 us -> 375 us (0.89)
  waiting for transfers between devices: 215 us -> 173 us
  blocking collectives: 0 us -> 15.8 us
  local copies, waits for them, and re-layouts: 24 us -> 14.8 us
  starting transfers between devices: 87.8 us -> 80.7 us
    all_to_all x1, waiting for transfers between devices: 0.01 us -> 76.7 us  [shards(): lax.all_to_all(returned.reshape(BANDS, ROWS, SLOTS, E), 'band', split_axi...]
    ppermute x15 -> x2, waiting for transfers between devices: 90.8 us -> 15.2 us  [across(): lax.ppermute(value, 'member', [(2 * z, 2 * z + 1) for z in range(DEPTH)])]
    all_gather x1, waiting for transfers between devices: 63.1 us -> 0.01 us  [shards(): lax.all_gather(control, 'member', tiled=True, axis_index_groups=RINGS)]
    all_to_all x0 -> x1, blocking collectives: none -> 15.8 us  [shards(): lax.all_to_all(control_spatial.transpose(1, 0, 2).reshape(BANDS, ROWS, 4,...]
    all_to_all x2 -> x3, starting transfers between devices: 10.1 us -> 25.1 us  [the longest x1 12.5 us: shards(): lax.all_to_all(spread_sums(weights, share, forecast, control), 'band', sp...]
    ppermute x15 -> x2, starting transfers between devices: 19.5 us -> 7.39 us  [across(): lax.ppermute(value, 'member', [(2 * z, 2 * z + 1) for z in range(DEPTH)])]
    all_to_all x2 -> x3, waiting for transfers between devices: 3.95 us -> 15.1 us  [the longest x2 9.87 us: exchanged_along_z(): lax.all_to_all(pieces, 'member', split_axis=0, concat_axis=0, axis_index_...]
    ppermute x3, waiting for transfers between devices: 0.01 us -> 7 us  [doubled_along_z(): arrived = lax.ppermute(value, 'member', pairs)]
  transfers between devices with their start and end apart: 31 -> 19, of which waited for: 13 -> 14; matrix products, arithmetic and copies ran while one was open for 6% -> 4% of each run, Pallas kernels for 9% -> 10%
where the time goes in v3:
time: 375 us; the launch traced here: 374 us
  waiting for transfers between devices  173 us (46%)
  starting transfers between devices  80.7 us (22%)
  Pallas kernels  67.8 us (18%)
  blocking collectives  15.8 us (4%)
  between operations  15 us (4%)
  local copies, waits for them, and re-layouts  14.8 us (4%)
  other arithmetic  6.73 us (2%)
    all_to_all x1, waiting for transfers between devices, shards(): lax.all_to_all(returned.reshape(BANDS, ROWS, SLOTS, E), 'band', split_axi...  76.7 us
    ppermute x7, waiting for transfers between devices, scattered(): arrived = lax.ppermute(pieces[z], 'member', [(0, 2 * z)])  55.9 us
    pallas_call x1, Pallas kernels, spectral_pass(): pl.pallas_call(spectral_kernel, grid_spec=pltpu.PrefetchScalarGridSpec(nu...  18.8 us
    ppermute x7, starting transfers between devices, scattered(): arrived = lax.ppermute(pieces[z], 'member', [(0, 2 * z)])  18.2 us
    all_to_all x1, blocking collectives, shards(): lax.all_to_all(control_spatial.transpose(1, 0, 2).reshape(BANDS, ROWS, 4,...  15.8 us
    ppermute x2, waiting for transfers between devices, across(): lax.ppermute(value, 'member', [(2 * z, 2 * z + 1) for z in range(DEPTH)])  15.2 us
    pallas_call x2, Pallas kernels, inverse_transform(): pl.pallas_call(inverse_kernel, grid=(rows // step,), in_specs=[pl.BlockSp...  13.9 us
    pallas_call x2, Pallas kernels, forward_transform(): pl.pallas_call(forward_kernel, grid=(rows // step,), in_specs=[pl.BlockSp...  12.9 us
  transfers between devices with their start and end apart: 19, of which 14 were waited for; matrix products, arithmetic and copies ran while one was open for 4% of the time, Pallas kernels for 10%

profile of v3, /device:TPU:1, one launch (start us, length us, event | category | flops | bytes accessed | tf_op | source)
XLA Modules:
  0.0 373.8 jit_solution(1243509372967705615)
XLA Ops:
  8.4 9.7 %forward_transform.2 = bf16[16,15,32,384]{3,2,1,0:T(8,128)(2,1)} custom-call(f32[15]{0:T(128)} %sine_multiply_fusion.weights_ref, bf16[15,480,384]{2,1,0:T(8,128)(2,1)} %bitcast.38, f32[1,384]{1,0:T(1,128)} %broadcast_in_dim.28.gain_ref, bf16[512,480]{1,0:T(8,128)(2,1)} %constant.111.table_ref), custom_call_target="tpu_custom_call" | custom-call | flops 137438953472 | bytes 15728640 | tf_op jit(solution)/shard_map/forward_transform/pallas_call | solution.py:131
  18.0 7.6 %all-to-all-start = ((bf16[16,15,32,384]{3,2,1,0:T(8,128)(2,1)}), bf16[16,15,32,384]{3,2,1,0:T(8,128)(2,1)}, u32[]{:S(2)}, u32[]{:S(2)}) async-start(bf16[16,15,32,384]{3,2,1,0:T(8,128)(2,1)} %forward_transform.2), calls=%async_computation | async-start | bytes 11796480 | tf_op jit(solution)/shard_map/all_to_all | solution.py:442
  26.8 6.8 %collective-permute-start = (bf16[2,480,384]{2,1,0:T(8,128)(2,1)S(1)}, bf16[2,480,384]{2,1,0:T(8,128)(2,1)S(1)}, u32[]{:S(2)}, u32[]{:S(2)}) collective-permute-start(bf16[2,480,384]{2,1,0:T(8,128)(2,1)S(1)} %pad_maximum_fusion), channel_id=1, source_target_pairs={{0,224},{1,225},{2,226},{3,227},{4,228},{5,229},{6,230},{7,231},{8... | collective-permute-start | bytes 2211848 | tf_op jit(solution)/shard_map/ppermute | solution.py:382
  51.5 13.6 %collective-permute-done.1 = bf16[2,480,384]{2,1,0:T(8,128)(2,1)S(1)} collective-permute-done((bf16[2,480,384]{2,1,0:T(8,128)(2,1)S(1)}, bf16[2,480,384]{2,1,0:T(8,128)(2,1)S(1)}, u32[]{:S(2)}, u32[]{:S(2)}) %collective-permute-start.1) | collective-permute-done | bytes 737312 | tf_op jit(solution)/shard_map/ppermute | solution.py:382
  67.3 13.7 %collective-permute-done.2 = bf16[2,480,384]{2,1,0:T(8,128)(2,1)S(1)} collective-permute-done((bf16[2,480,384]{2,1,0:T(8,128)(2,1)}, bf16[2,480,384]{2,1,0:T(8,128)(2,1)S(1)}, u32[]{:S(2)}, u32[]{:S(2)}) %collective-permute-start.2) | collective-permute-done | bytes 737312 | tf_op jit(solution)/shard_map/ppermute | solution.py:382
  81.0 8.3 %collective-permute-done.5 = bf16[2,480,384]{2,1,0:T(8,128)(2,1)} collective-permute-done((bf16[2,480,384]{2,1,0:T(8,128)(2,1)}, bf16[2,480,384]{2,1,0:T(8,128)(2,1)}, u32[]{:S(2)}, u32[]{:S(2)}) %collective-permute-start.5) | collective-permute-done | bytes 737312 | tf_op jit(solution)/shard_map/ppermute | solution.py:382
  89.3 15.7 %collective-permute-done.6 = bf16[2,480,384]{2,1,0:T(8,128)(2,1)} collective-permute-done((bf16[2,480,384]{2,1,0:T(8,128)(2,1)S(1)}, bf16[2,480,384]{2,1,0:T(8,128)(2,1)}, u32[]{:S(2)}, u32[]{:S(2)}) %collective-permute-start.6) | collective-permute-done | bytes 737312 | tf_op jit(solution)/shard_map/ppermute | solution.py:382
  108.4 14.4 %collective-permute-done.7 = bf16[2,480,384]{2,1,0:T(8,128)(2,1)S(1)} collective-permute-done((bf16[2,480,384]{2,1,0:T(8,128)(2,1)S(1)}, bf16[2,480,384]{2,1,0:T(8,128)(2,1)S(1)}, u32[]{:S(2)}, u32[]{:S(2)}) %collective-permute-start.7) | collective-permute-done | bytes 737312 | tf_op jit(solution)/shard_map/ppermute | solution.py:403
  126.9 8.3 %all-to-all-start.1 = ((bf16[8,2,64,384]{3,2,1,0:T(8,128)(2,1)}), bf16[8,2,64,384]{3,2,1,0:T(8,128)(2,1)S(1)}, u32[]{:S(2)}, u32[]{:S(2)}) async-start(bf16[8,2,64,384]{3,2,1,0:T(8,128)(2,1)} %forward_transform.3), calls=%async_computation.1 | async-start | bytes 1572864 | tf_op jit(solution)/shard_map/all_to_all | solution.py:397
  136.0 7.3 %collective-permute-start.8 = (f32[1,240]{1,0:T(1,128)S(1)}, f32[1,240]{1,0:T(1,128)S(1)}, u32[]{:S(2)}, u32[]{:S(2)}) collective-permute-start(f32[1,240]{1,0:T(1,128)S(1)} %bitcast.49), channel_id=1, source_target_pairs={{0,128},{1,129},{2,130},{3,131},{4,132},{5,133},{6,134},{7,135},{8... | collective-permute-start | bytes 2888 | tf_op jit(solution)/shard_map/ppermute | solution.py:391
  143.3 6.4 %collective-permute-done.8 = f32[1,240]{1,0:T(1,128)S(1)} collective-permute-done((f32[1,240]{1,0:T(1,128)S(1)}, f32[1,240]{1,0:T(1,128)S(1)}, u32[]{:S(2)}, u32[]{:S(2)}) %collective-permute-start.8) | collective-permute-done | bytes 992 | tf_op jit(solution)/shard_map/ppermute | solution.py:391
  153.0 5.8 %all-to-all-done.1 = bf16[8,2,64,384]{3,2,1,0:T(8,128)(2,1)S(1)} async-done(((bf16[8,2,64,384]{3,2,1,0:T(8,128)(2,1)}), bf16[8,2,64,384]{3,2,1,0:T(8,128)(2,1)S(1)}, u32[]{:S(2)}, u32[]{:S(2)}) %all-to-all-start.1) | async-done | bytes 786464 | tf_op jit(solution)/shard_map/all_to_all | solution.py:397
  160.5 7.7 %all-to-all-start.2 = ((bf16[16,15,4,384]{3,2,1,0:T(4,128)(2,1)}), bf16[16,15,4,384]{3,2,1,0:T(4,128)(2,1)S(1)}, u32[]{:S(2)}, u32[]{:S(2)}) async-start(bf16[16,15,4,384]{3,2,1,0:T(4,128)(2,1)} %slice.44), calls=%async_computation.2 | async-start | bytes 1474560 | tf_op jit(solution)/shard_map/all_to_all | solution.py:458
  169.3 6.1 %collective-permute-start.11 = (f32[1,240]{1,0:T(1,128)S(1)}, f32[1,240]{1,0:T(1,128)S(1)}, u32[]{:S(2)}, u32[]{:S(2)}) collective-permute-start(f32[1,240]{1,0:T(1,128)S(1)} %broadcast_select_fusion.3), channel_id=1, source_target_pairs={{0,16},{32,48},{64,80},{96,112},{128,144},{160,176},{192,208},{224... | collective-permute-start | bytes 2888 | tf_op jit(solution)/shard_map/ppermute | solution.py:403
  181.6 4.8 %shared_spectral_pass.1 = (bf16[2,240,384]{2,1,0:T(8,128)(2,1)}, bf16[2,240,384]{2,1,0:T(8,128)(2,1)}) custom-call(s32[2]{0:T(128)} %pad_add_fusion.place_ref, bf16[4,240,384]{2,1,0:T(8,128)(2,1)} %bitcast.36, bf16[4,240,384]{2,1,0:T(8,128)(2,1)} %bitcast.37, bf16[16,15,240,240]{3,2,1,0:T(8,128)(2,1)} %constant.113.legendre_ref, f32[240,1]{1,0:T(8,128)} %copy.25.gain_ref, ...), custom_call_target="tpu_custom_call" | custom-call | flops 1073741824 | bytes 4194304 | tf_op jit(solution)/shard_map/shared_spectral_pass/pallas_call | solution.py:173
  187.9 15.8 %all_to_all.35 = bf16[16,15,4,384]{3,2,1,0:T(4,128)(2,1)S(1)} all-to-all(bf16[16,15,4,384]{3,2,1,0:T(4,128)(2,1)S(1)} %bitcast.48), channel_id=1, replica_groups=mesh['member'=16,'band'=16] {'band'}, dimensions={0} | all-to-all | bytes 1474560 | tf_op jit(solution)/shard_map/all_to_all | solution.py:474
  210.5 18.8 %spectral_pass.1 = bf16[240,32,384]{2,1,0:T(8,128)(2,1)} custom-call(s32[1]{0:T(128)} %bitcast.3.band_ref, bf16[240,32,384]{2,1,0:T(8,128)(2,1)} %bitcast.19.moved_ref, bf16[16,15,240,240]{3,2,1,0:T(8,128)(2,1)} %constant.113.legendre_ref, f32[240,1]{1,0:T(8,128)} %copy.28.gain_ref, bf16[768,768]{1,0:T(8,128)(2,1)} %maximum_maximum_fusion.mixing_ref, ...), custom_call_target="tpu_custom_call" | custom-call | flops 8589934592 | bytes 14680064 | tf_op jit(solution)/shard_map/spectral_pass/pallas_call | solution.py:253
  234.2 4.9 %all-to-all-start.5 = ((bf16[16,15,32,384]{3,2,1,0:T(8,128)(2,1)}), bf16[16,15,32,384]{3,2,1,0:T(8,128)(2,1)}, u32[]{:S(2)}, u32[]{:S(2)}) async-start(bf16[16,15,32,384]{3,2,1,0:T(8,128)(2,1)} %bitcast.35), calls=%async_computation.5 | async-start | bytes 11796480 | tf_op jit(solution)/shard_map/all_to_all | solution.py:485
  243.2 76.7 %all-to-all-done.5.spatial_ref = bf16[16,15,32,384]{3,2,1,0:T(8,128)(2,1)} async-done(((bf16[16,15,32,384]{3,2,1,0:T(8,128)(2,1)}), bf16[16,15,32,384]{3,2,1,0:T(8,128)(2,1)}, u32[]{:S(2)}, u32[]{:S(2)}) %all-to-all-start.5) | async-done | bytes 5898272 | tf_op jit(solution)/shard_map/all_to_all | solution.py:485
  319.9 10.6 %inverse_transform.2.own_ref = bf16[15,480,384]{2,1,0:T(8,128)(2,1)} custom-call(bf16[16,15,32,384]{3,2,1,0:T(8,128)(2,1)} %all-to-all-done.5.spatial_ref, bf16[15,480,384]{2,1,0:T(8,128)(2,1)} %bitcast.42, bf16[480,512]{1,0:T(8,128)(2,1)} %constant.115.table_ref), custom_call_target="tpu_custom_call" | custom-call | flops 274877906944 | bytes 15728640 | tf_op jit(solution)/shard_map/inverse_transform/pallas_call | solution.py:288
  330.5 7.2 %spread_sums.1 = f32[16,8,128]{2,1,0:T(8,128)} custom-call(f32[15]{0:T(128)} %sine_multiply_fusion.weights_ref, f32[1]{0:T(128)} %bitcast.share_ref, bf16[15,480,384]{2,1,0:T(8,128)(2,1)} %inverse_transform.2.own_ref, bf16[16,480,384]{2,1,0:T(8,128)(2,1)} %all-gather.2.cloned.1.call-done.control_ref), custom_call_target="tpu_custom_call" | custom-call | flops 9437184 | bytes 11534336 | tf_op jit(solution)/shard_map/spread_sums/pallas_call | solution.py:335
  337.7 12.5 %all-to-all-start.6 = ((f32[16,8,128]{2,1,0:T(8,128)}), f32[16,8,128]{2,1,0:T(8,128)S(1)}, u32[]{:S(2)}, u32[]{:S(2)}) async-start(f32[16,8,128]{2,1,0:T(8,128)} %spread_sums.1), calls=%async_computation.6 | async-start | bytes 131072 | tf_op jit(solution)/shard_map/all_to_all | solution.py:492
  350.9 5.2 %all-to-all-done.6.sums_ref = f32[16,8,128]{2,1,0:T(8,128)S(1)} async-done(((f32[16,8,128]{2,1,0:T(8,128)}), f32[16,8,128]{2,1,0:T(8,128)S(1)}, u32[]{:S(2)}, u32[]{:S(2)}) %all-to-all-start.6) | async-done | bytes 65568 | tf_op jit(solution)/shard_map/all_to_all | solution.py:492
  356.7 10.3 %rescaled.1 = bf16[15,480,384]{2,1,0:T(8,128)(2,1)} custom-call(f32[1]{0:T(128)} %bitcast.share_ref, f32[1]{0:T(128)} %bitcast.2.target_ref, f32[16,8,128]{2,1,0:T(8,128)} %copy-done.3, bf16[15,480,384]{2,1,0:T(8,128)(2,1)} %inverse_transform.2.own_ref, bf16[16,480,384]{2,1,0:T(8,128)(2,1)} %all-gather.2.cloned.1.call-done.control_ref), custom_call_target="tpu_custom_call" | custom-call | flops 9437184 | bytes 17825792 | tf_op jit(solution)/shard_map/rescaled/pallas_call | solution.py:360
  (67 shorter events, 60.7 us)
Async XLA Ops:
  18.0 108.9 %all-to-all-start = ((bf16[16,15,32,384]{3,2,1,0:T(8,128)(2,1)}), bf16[16,15,32,384]{3,2,1,0:T(8,128)(2,1)}, u32[]{:S(2)}, u32[]{:S(2)}) async-start(bf16[16,15,32,384]{3,2,1,0:T(8,128)(2,1)} %forward_transform.2), calls=%async_computation | async-start | bytes 11796480 | tf_op jit(solution)/shard_map/all_to_all | solution.py:442
  26.8 22.5 %collective-permute-start = (bf16[2,480,384]{2,1,0:T(8,128)(2,1)S(1)}, bf16[2,480,384]{2,1,0:T(8,128)(2,1)S(1)}, u32[]{:S(2)}, u32[]{:S(2)}) collective-permute-start(bf16[2,480,384]{2,1,0:T(8,128)(2,1)S(1)} %pad_maximum_fusion), channel_id=1, source_target_pairs={{0,224},{1,225},{2,226},{3,227},{4,228},{5,229},{6,230},{7,231},{8... | collective-permute-start | bytes 2211848 | tf_op jit(solution)/shard_map/ppermute | solution.py:382
  37.6 27.4 %collective-permute-start.1 = (bf16[2,480,384]{2,1,0:T(8,128)(2,1)S(1)}, bf16[2,480,384]{2,1,0:T(8,128)(2,1)S(1)}, u32[]{:S(2)}, u32[]{:S(2)}) collective-permute-start(bf16[2,480,384]{2,1,0:T(8,128)(2,1)S(1)} %get-tuple-element.22), channel_id=1, source_target_pairs={{0,192},{1,193},{2,194},{3,195},{4,196},{5,197},{6,198},{7,199},{8... | collective-permute-start | bytes 2211848 | tf_op jit(solution)/shard_map/ppermute | solution.py:382
  39.0 42.0 %collective-permute-start.2 = (bf16[2,480,384]{2,1,0:T(8,128)(2,1)}, bf16[2,480,384]{2,1,0:T(8,128)(2,1)S(1)}, u32[]{:S(2)}, u32[]{:S(2)}) collective-permute-start(bf16[2,480,384]{2,1,0:T(8,128)(2,1)} %get-tuple-element.21), channel_id=1, source_target_pairs={{0,160},{1,161},{2,162},{3,163},{4,164},{5,165},{6,166},{7,167},{8... | collective-permute-start | bytes 2211848 | tf_op jit(solution)/shard_map/ppermute | solution.py:382
  40.3 40.7 %collective-permute-start.3 = (bf16[2,480,384]{2,1,0:T(8,128)(2,1)}, bf16[2,480,384]{2,1,0:T(8,128)(2,1)}, u32[]{:S(2)}, u32[]{:S(2)}) collective-permute-start(bf16[2,480,384]{2,1,0:T(8,128)(2,1)} %get-tuple-element.20), channel_id=1, source_target_pairs={{0,128},{1,129},{2,130},{3,131},{4,132},{5,133},{6,134},{7,135},{8... | collective-permute-start | bytes 2211848 | tf_op jit(solution)/shard_map/ppermute | solution.py:382
  42.5 38.5 %collective-permute-start.4 = (bf16[2,480,384]{2,1,0:T(8,128)(2,1)}, bf16[2,480,384]{2,1,0:T(8,128)(2,1)}, u32[]{:S(2)}, u32[]{:S(2)}) collective-permute-start(bf16[2,480,384]{2,1,0:T(8,128)(2,1)} %get-tuple-element.19), channel_id=1, source_target_pairs={{0,96},{1,97},{2,98},{3,99},{4,100},{5,101},{6,102},{7,103},{8,104... | collective-permute-start | bytes 2211848 | tf_op jit(solution)/shard_map/ppermute | solution.py:382
  49.3 40.0 %collective-permute-start.5 = (bf16[2,480,384]{2,1,0:T(8,128)(2,1)}, bf16[2,480,384]{2,1,0:T(8,128)(2,1)}, u32[]{:S(2)}, u32[]{:S(2)}) collective-permute-start(bf16[2,480,384]{2,1,0:T(8,128)(2,1)} %get-tuple-element.18), channel_id=1, source_target_pairs={{0,64},{1,65},{2,66},{3,67},{4,68},{5,69},{6,70},{7,71},{8,72},{9,... | collective-permute-start | bytes 2211848 | tf_op jit(solution)/shard_map/ppermute | solution.py:382
  65.1 39.9 %collective-permute-start.6 = (bf16[2,480,384]{2,1,0:T(8,128)(2,1)S(1)}, bf16[2,480,384]{2,1,0:T(8,128)(2,1)}, u32[]{:S(2)}, u32[]{:S(2)}) collective-permute-start(bf16[2,480,384]{2,1,0:T(8,128)(2,1)S(1)} %get-tuple-element.17), channel_id=1, source_target_pairs={{0,32},{1,33},{2,34},{3,35},{4,36},{5,37},{6,38},{7,39},{8,40},{9,... | collective-permute-start | bytes 2211848 | tf_op jit(solution)/shard_map/ppermute | solution.py:382
  67.2 40.5 %copy-start.5 = (f32[15]{0:T(128)S(1)}, f32[15]{0:T(128)}, u32[]{:S(2)}) copy-start(f32[15]{0:T(128)} %sine_multiply_fusion.weights_ref) | copy-start | bytes 184
  106.3 16.4 %collective-permute-start.7 = (bf16[2,480,384]{2,1,0:T(8,128)(2,1)S(1)}, bf16[2,480,384]{2,1,0:T(8,128)(2,1)S(1)}, u32[]{:S(2)}, u32[]{:S(2)}) collective-permute-start(bf16[2,480,384]{2,1,0:T(8,128)(2,1)S(1)} %fusion.5), channel_id=1, source_target_pairs={{0,16},{32,48},{64,80},{96,112},{128,144},{160,176},{192,208},{224... | collective-permute-start | bytes 2211848 | tf_op jit(solution)/shard_map/ppermute | solution.py:403
  123.7 12.2 %copy-start.4 = (f32[32,240]{1,0:T(8,128)S(1)}, f32[32,240]{1,0:T(8,128)}, u32[]{:S(2)}) copy-start(f32[32,240]{1,0:T(8,128)} %param.18) | copy-start | bytes 92164
  123.7 27.3 %copy-start.1 = (bf16[384,384]{1,0:T(8,128)(2,1)S(1)}, bf16[384,384]{1,0:T(8,128)(2,1)}, u32[]{:S(2)}) copy-start(bf16[384,384]{1,0:T(8,128)(2,1)} %param.17) | copy-start | bytes 884740
  126.9 31.9 %all-to-all-start.1 = ((bf16[8,2,64,384]{3,2,1,0:T(8,128)(2,1)}), bf16[8,2,64,384]{3,2,1,0:T(8,128)(2,1)S(1)}, u32[]{:S(2)}, u32[]{:S(2)}) async-start(bf16[8,2,64,384]{3,2,1,0:T(8,128)(2,1)} %forward_transform.3), calls=%async_computation.1 | async-start | bytes 1572864 | tf_op jit(solution)/shard_map/all_to_all | solution.py:397
  136.0 13.7 %collective-permute-start.8 = (f32[1,240]{1,0:T(1,128)S(1)}, f32[1,240]{1,0:T(1,128)S(1)}, u32[]{:S(2)}, u32[]{:S(2)}) collective-permute-start(f32[1,240]{1,0:T(1,128)S(1)} %bitcast.49), channel_id=1, source_target_pairs={{0,128},{1,129},{2,130},{3,131},{4,132},{5,133},{6,134},{7,135},{8... | collective-permute-start | bytes 2888 | tf_op jit(solution)/shard_map/ppermute | solution.py:391
  149.7 2.0 collective-permute-start.9
  151.7 17.6 %collective-permute-start.10 = (f32[1,240]{1,0:T(1,128)S(1)}, f32[1,240]{1,0:T(1,128)S(1)}, u32[]{:S(2)}, u32[]{:S(2)}) collective-permute-start(f32[1,240]{1,0:T(1,128)S(1)} %broadcast_select_fusion.2), channel_id=1, source_target_pairs={{0,32},{64,96},{128,160},{192,224},{1,33},{65,97},{129,161},{193,2... | collective-permute-start | bytes 2888 | tf_op jit(solution)/shard_map/ppermute | solution.py:391
  159.0 9.2 %copy-start.2 = (bf16[384,384]{1,0:T(8,128)(2,1)S(1)}, bf16[384,384]{1,0:T(8,128)(2,1)}, u32[]{:S(2)}) copy-start(bf16[384,384]{1,0:T(8,128)(2,1)} %param.16) | copy-start | bytes 884740
  160.5 20.1 %all-to-all-start.2 = ((bf16[16,15,4,384]{3,2,1,0:T(4,128)(2,1)}), bf16[16,15,4,384]{3,2,1,0:T(4,128)(2,1)S(1)}, u32[]{:S(2)}, u32[]{:S(2)}) async-start(bf16[16,15,4,384]{3,2,1,0:T(4,128)(2,1)} %slice.44), calls=%async_computation.2 | async-start | bytes 1474560 | tf_op jit(solution)/shard_map/all_to_all | solution.py:458
  169.3 7.5 %collective-permute-start.11 = (f32[1,240]{1,0:T(1,128)S(1)}, f32[1,240]{1,0:T(1,128)S(1)}, u32[]{:S(2)}, u32[]{:S(2)}) collective-permute-start(f32[1,240]{1,0:T(1,128)S(1)} %broadcast_select_fusion.3), channel_id=1, source_target_pairs={{0,16},{32,48},{64,80},{96,112},{128,144},{160,176},{192,208},{224... | collective-permute-start | bytes 2888 | tf_op jit(solution)/shard_map/ppermute | solution.py:403
  205.5 27.8 %all-to-all-start.4 = ((bf16[8,2,64,384]{3,2,1,0:T(8,128)(2,1)}), bf16[8,2,64,384]{3,2,1,0:T(8,128)(2,1)S(1)}, u32[]{:S(2)}, u32[]{:S(2)}) async-start(bf16[8,2,64,384]{3,2,1,0:T(8,128)(2,1)} %reshape.38), calls=%async_computation.4 | async-start | bytes 1572864 | tf_op jit(solution)/shard_map/all_to_all | solution.py:397
  234.2 85.7 %all-to-all-start.5 = ((bf16[16,15,32,384]{3,2,1,0:T(8,128)(2,1)}), bf16[16,15,32,384]{3,2,1,0:T(8,128)(2,1)}, u32[]{:S(2)}, u32[]{:S(2)}) async-start(bf16[16,15,32,384]{3,2,1,0:T(8,128)(2,1)} %bitcast.35), calls=%async_computation.5 | async-start | bytes 11796480 | tf_op jit(solution)/shard_map/all_to_all | solution.py:485
  239.1 91.4 %all-gather.2.cloned.1.call-start = ((), (), s32[]{:S(2)}) async-start(), calls=%async_computation.7 | async-start | bytes 6635520 | tf_op jit(solution)/shard_map/all_gather | solution.py:489
  330.5 19.8 %copy-start.6 = (f32[8]{0:T(128)S(1)}, f32[8]{0:T(128)}, u32[]{:S(2)}) copy-start(f32[8]{0:T(128)} %param.20) | copy-start | bytes 100
  337.7 18.4 %all-to-all-start.6 = ((f32[16,8,128]{2,1,0:T(8,128)}), f32[16,8,128]{2,1,0:T(8,128)S(1)}, u32[]{:S(2)}, u32[]{:S(2)}) async-start(f32[16,8,128]{2,1,0:T(8,128)} %spread_sums.1), calls=%async_computation.6 | async-start | bytes 131072 | tf_op jit(solution)/shard_map/all_to_all | solution.py:492
  (2 other events, 1.5 us)
Sparse Core Ops, SparseCore 0:
  243.3 69.6 all-gather.1

commit v4 on v3

--- a/solution.py
+++ b/solution.py
@@ -303,15 +303,11 @@
     )(spatial, x, table)
 
 
-def difference_of(share, own, control):
-    return jnp.where(share > 0.0, own.astype(jnp.float32) - control, 0.0)
-
-
-def spread_kernel(weights_ref, share_ref, own_ref, control_ref, out_ref, total):
+def spread_kernel(weights_ref, own_ref, control_ref, out_ref, total):
     step = pl.program_id(0)
     partial = 0.0
     for j in range(STEP):
-        difference = difference_of(share_ref[0], own_ref[j], control_ref[j].astype(jnp.float32))
+        difference = own_ref[j].astype(jnp.float32) - control_ref[j].astype(jnp.float32)
         squares = jnp.sum((difference * difference).reshape(W // 8, 8, E), axis=0)
         partial = partial + squares * weights_ref[step * STEP + j]
 
@@ -329,39 +325,38 @@
         out_ref[...] = jnp.broadcast_to(lanes[None], out_ref.shape)
 
 
-def spread_sums(weights, share, own, control):
+def spread_sums(weights, own, control):
     row = pl.BlockSpec((STEP, W, E), lambda j: (j, 0, 0))
     scalars = pl.BlockSpec(memory_space=pltpu.SMEM)
     return pl.pallas_call(
         spread_kernel,
         grid=(ROWS // STEP,),
-        in_specs=[scalars, scalars, row, row],
+        in_specs=[scalars, row, row],
         out_specs=pl.BlockSpec((BANDS, 8, 128), lambda j: (0, 0, 0)),
         out_shape=jax.ShapeDtypeStruct((BANDS, 8, 128), jnp.float32),
         scratch_shapes=[pltpu.VMEM((8, E), jnp.float32)],
         compiler_params=pltpu.CompilerParams(vmem_limit_bytes=VMEM_LIMIT),
         cost_estimate=pl.CostEstimate(flops=9 << 20, bytes_accessed=11 << 20, transcendentals=0),
         name="spread_sums",
-    )(weights, share, own, control)
-
-
-def rescale_kernel(share_ref, target_ref, sums_ref, own_ref, control_ref, out_ref):
+    )(weights, own, control)
+
+
+def rescale_kernel(target_ref, sums_ref, own_ref, control_ref, out_ref):
     total = jnp.sum(jnp.sum(sums_ref[...], axis=0), axis=(0, 1), keepdims=True)
     scale = target_ref[0] / jnp.sqrt(total * (1.0 / TOTAL_WEIGHT) + 1e-06)
     for j in range(STEP):
         control = control_ref[j].astype(jnp.float32)
-        difference = difference_of(share_ref[0], own_ref[j], control)
+        difference = own_ref[j].astype(jnp.float32) - control
         out_ref[j] = (control + scale * difference).astype(jnp.bfloat16)
 
 
-def rescaled(share, target, sums, own, control):
+def rescaled(target, sums, own, control):
     row = pl.BlockSpec((STEP, W, E), lambda j: (j, 0, 0))
     scalars = pl.BlockSpec(memory_space=pltpu.SMEM)
     return pl.pallas_call(
         rescale_kernel,
         grid=(ROWS // STEP,),
         in_specs=[
-            scalars,
             scalars,
             pl.BlockSpec((BANDS, 8, 128), lambda j: (0, 0, 0)),
             row,
@@ -372,25 +367,27 @@
         compiler_params=pltpu.CompilerParams(vmem_limit_bytes=VMEM_LIMIT),
         cost_estimate=pl.CostEstimate(flops=9 << 20, bytes_accessed=17 << 20, transcendentals=0),
         name="rescaled",
-    )(share, target, sums, own, control)
-
-
-def scattered(pieces):
+    )(target, sums, own, control)
+
+
+def in_three(value):
+    parts = []
+    for _ in range(3):
+        parts.append(lax.reduce_precision(value, exponent_bits=8, mantissa_bits=7))
+        value = value - parts[-1]
+    return jnp.stack(parts).astype(jnp.bfloat16)
+
+
+def scattered(field, extra):
     member = lax.axis_index("member")
-    kept = pieces[0]
+    kept = jnp.concatenate([field[:2].reshape(2 * W, E), extra])
     for z in range(1, DEPTH):
-        arrived = lax.ppermute(pieces[z], "member", [(0, 2 * z)])
+        piece = field[2 * z : min(2 * z + 2, ROWS)].reshape(-1, E)
+        arrived = lax.ppermute(jnp.concatenate([piece, extra]), "member", [(0, 2 * z)])
+        if 2 * z + 1 == ROWS:
+            arrived = jnp.concatenate([arrived[:W], arrived])
         kept = jnp.where(member == 2 * z, arrived, kept)
     return kept
-
-
-def doubled_along_z(value):
-    z = lax.axis_index("member") // 2
-    for stride in (4, 2, 1):
-        pairs = [(2 * a, 2 * (a + stride)) for a in range(0, DEPTH, 2 * stride)]
-        arrived = lax.ppermute(value, "member", pairs)
-        value = jnp.where(z % (2 * stride) == stride, arrived, value)
-    return value
 
 
 def exchanged_along_z(pieces):
@@ -431,7 +428,6 @@
     gain = degree_gain[:, None]
     member = lax.axis_index("member")
     place = jnp.stack([band_index, member // 2])
-    share = jnp.where(member > 0, 1.0, 0.0)[None]
 
     mixing = jnp.concatenate(
         [jnp.concatenate([mix_real, mix_imag], 1), jnp.concatenate([-mix_imag, mix_real], 1)], 0
@@ -441,21 +437,18 @@
     fourier = forward_transform(x, norm_gain[None, :], weights, rounded(ahead_np), BANDS, STEP, 1 << 37)
     moved = lax.all_to_all(fourier, "band", split_axis=0, concat_axis=0, tiled=True)
 
-    control_x = across(
-        scattered(
-            [x[2 * a : 2 * a + 2] for a in range(DEPTH - 1)]
-            + [jnp.concatenate([x[ROWS - 1 :]] * 2)]
-        )
-    )
-    control_gain = across(doubled_along_z(degree_gain[None, :]))
+    control_parts = across(
+        scattered(x, jnp.pad(in_three(degree_gain), ((0, 16 - 3), (0, E - L))))
+    )
+    control_x = control_parts[: 2 * W].reshape(2, W, E)
+    control_gain = jnp.sum(control_parts[2 * W : 2 * W + 3, :L].astype(jnp.float32), axis=0)
     control_weights = lax.dynamic_slice(jnp.pad(weights, (0, 1)), (2 * z,), (2,))
     control_fourier = forward_transform(
-        control_x, norm_gain[None, :], control_weights, rounded(shared_ahead_np), DEPTH, 2, 1 << 29
+        control_x, norm_gain[None, :], control_weights, rounded(shared_ahead_np), DEPTH, 2, 32 << 30
     )
     moved, control_fourier = lax.optimization_barrier((moved, control_fourier))
     control_fourier = exchanged_along_z(control_fourier).reshape(DEPTH, 2, BANDS, 4, E)
     control_fourier = control_fourier.transpose(2, 0, 1, 3, 4).reshape(BANDS, 16, 4, E)[:, :ROWS]
-    control_moved = lax.all_to_all(control_fourier, "band", split_axis=0, concat_axis=0, tiled=True)
     returned = spectral_pass(
         band_index[None],
         moved.reshape(H, SLOTS, E),
@@ -464,6 +457,8 @@
         mixing,
         rounded(exchange_matrix()),
     )
+    returned, control_fourier = lax.optimization_barrier((returned, control_fourier))
+    control_moved = lax.all_to_all(control_fourier, "band", split_axis=0, concat_axis=0, tiled=True)
     control_spatial = shared_spectral_pass(
         place,
         control_moved.reshape(H, 4, E).transpose(1, 0, 2),
@@ -490,7 +485,7 @@
 
     forecast = inverse_transform(spatial, x, rounded(back_np), STEP, 1 << 38)
     sums = lax.all_to_all(
-        spread_sums(weights, share, forecast, control),
+        spread_sums(weights, forecast, control),
         "band",
         split_axis=0,
         concat_axis=0,
@@ -503,7 +498,7 @@
             0.0,
         )
     )
-    bred = rescaled(share, target[None], sums, forecast, control)
+    bred = rescaled(jnp.where(member > 0, target, 0.0)[None], sums, forecast, control)
     return jnp.transpose(bred, (0, 2, 1))[None]
 
 

time: 375 us -> 388 us (1.035)
  blocking collectives: 15.8 us -> 43.4 us
  starting transfers between devices: 80.7 us -> 58.6 us
  waiting for transfers between devices: 173 us -> 179 us
    all_to_all x0 -> x1, blocking collectives: none -> 27.6 us  [exchanged_along_z(): lax.all_to_all(pieces, 'member', split_axis=0, concat_axis=0, axis_index_...]
    ppermute x2 -> x1, waiting for transfers between devices: 15.2 us -> 28.1 us  [across(): lax.ppermute(value, 'member', [(2 * z, 2 * z + 1) for z in range(DEPTH)])]
    all_to_all x2 -> x1, waiting for transfers between devices: 9.87 us -> 0.59 us  [exchanged_along_z(): lax.all_to_all(pieces, 'member', split_axis=0, concat_axis=0, axis_index_...]
    all_to_all x2 -> x1, starting transfers between devices: 12.5 us -> 3.87 us  [exchanged_along_z(): lax.all_to_all(pieces, 'member', split_axis=0, concat_axis=0, axis_index_...]
    ppermute x10 -> x7, starting transfers between devices: 28.1 us -> 19.4 us  [scattered(): lax.ppermute(jnp.concatenate([piece, extra]), 'member', [(0, 2 * z)])]
    all_to_all x1, waiting for transfers between devices: 3.03 us -> 11.1 us  [shards(): lax.all_to_all(control_fourier, 'band', split_axis=0, concat_axis=0, tile...]
    ppermute x2 -> x1, starting transfers between devices: 7.39 us -> 1.34 us  [across(): lax.ppermute(value, 'member', [(2 * z, 2 * z + 1) for z in range(DEPTH)])]
    ppermute x10 -> x7, waiting for transfers between devices: 62.9 us -> 58.1 us  [scattered(): lax.ppermute(jnp.concatenate([piece, extra]), 'member', [(0, 2 * z)])]
  transfers between devices with their start and end apart: 19 -> 14, of which waited for: 14 -> 9; matrix products, arithmetic and copies ran while one was open for 4% -> 2% of each run, Pallas kernels for 10% -> 12%
where the time goes in v4:
time: 388 us; the launch traced here: 386 us
  waiting for transfers between devices  179 us (46%)
  Pallas kernels  67.3 us (17%)
  starting transfers between devices  58.6 us (15%)
  blocking collectives  43.4 us (11%)
  between operations  15.6 us (4%)
  local copies, waits for them, and re-layouts  12.8 us (3%)
  other arithmetic  8.92 us (2%)
    all_to_all x1, waiting for transfers between devices, shards(): lax.all_to_all(returned.reshape(BANDS, ROWS, SLOTS, E), 'band', split_axi...  76.6 us
    ppermute x7, waiting for transfers between devices, scattered(): lax.ppermute(jnp.concatenate([piece, extra]), 'member', [(0, 2 * z)])  58.1 us
    ppermute x1, waiting for transfers between devices, across(): lax.ppermute(value, 'member', [(2 * z, 2 * z + 1) for z in range(DEPTH)])  28.1 us
    all_to_all x1, blocking collectives, exchanged_along_z(): lax.all_to_all(pieces, 'member', split_axis=0, concat_axis=0, axis_index_...  27.6 us
    ppermute x7, starting transfers between devices, scattered(): lax.ppermute(jnp.concatenate([piece, extra]), 'member', [(0, 2 * z)])  19.4 us
    pallas_call x1, Pallas kernels, spectral_pass(): pl.pallas_call(spectral_kernel, grid_spec=pltpu.PrefetchScalarGridSpec(nu...  18.9 us
    all_to_all x1, blocking collectives, shards(): lax.all_to_all(control_spatial.transpose(1, 0, 2).reshape(BANDS, ROWS, 4,...  15.8 us
    pallas_call x2, Pallas kernels, inverse_transform(): pl.pallas_call(inverse_kernel, grid=(rows // step,), in_specs=[pl.BlockSp...  13.9 us
  transfers between devices with their start and end apart: 14, of which 9 were waited for; matrix products, arithmetic and copies ran while one was open for 2% of the time, Pallas kernels for 12%

profile of v4, /device:TPU:1, one launch (start us, length us, event | category | flops | bytes accessed | tf_op | source)
XLA Modules:
  0.0 385.6 jit_solution(95966314774826795)
XLA Ops:
  13.8 8.9 %collective-permute-start.1 = (bf16[976,384]{1,0:T(8,128)(2,1)}, bf16[976,384]{1,0:T(8,128)(2,1)S(1)}, u32[]{:S(2)}, u32[]{:S(2)}) collective-permute-start(bf16[976,384]{1,0:T(8,128)(2,1)} %get-tuple-element.33), channel_id=1, source_target_pairs={{0,192},{1,193},{2,194},{3,195},{4,196},{5,197},{6,198},{7,199},{8... | collective-permute-start | bytes 2248712 | tf_op jit(solution)/shard_map/ppermute | solution.py:386
  27.0 9.7 %forward_transform.2 = bf16[16,15,32,384]{3,2,1,0:T(8,128)(2,1)} custom-call(f32[15]{0:T(128)} %sine_multiply_fusion.weights_ref, bf16[15,480,384]{2,1,0:T(8,128)(2,1)} %bitcast.48, f32[1,384]{1,0:T(1,128)} %broadcast_in_dim.21.gain_ref, bf16[512,480]{1,0:T(8,128)(2,1)} %constant.87.table_ref), custom_call_target="tpu_custom_call" | custom-call | flops 137438953472 | bytes 15728640 | tf_op jit(solution)/shard_map/forward_transform/pallas_call | solution.py:131
  36.7 6.4 %all-to-all-start = ((bf16[16,15,32,384]{3,2,1,0:T(8,128)(2,1)}), bf16[16,15,32,384]{3,2,1,0:T(8,128)(2,1)}, u32[]{:S(2)}, u32[]{:S(2)}) async-start(bf16[16,15,32,384]{3,2,1,0:T(8,128)(2,1)} %forward_transform.2), calls=%async_computation | async-start | bytes 11796480 | tf_op jit(solution)/shard_map/all_to_all | solution.py:438
  52.4 10.2 %collective-permute-done.2 = bf16[976,384]{1,0:T(8,128)(2,1)S(1)} collective-permute-done((bf16[976,384]{1,0:T(8,128)(2,1)}, bf16[976,384]{1,0:T(8,128)(2,1)S(1)}, u32[]{:S(2)}, u32[]{:S(2)}) %collective-permute-start.2) | collective-permute-done | bytes 749600 | tf_op jit(solution)/shard_map/ppermute | solution.py:386
  62.6 15.7 %collective-permute-done.4 = bf16[976,384]{1,0:T(8,128)(2,1)} collective-permute-done((bf16[976,384]{1,0:T(8,128)(2,1)}, bf16[976,384]{1,0:T(8,128)(2,1)}, u32[]{:S(2)}, u32[]{:S(2)}) %collective-permute-start.4) | collective-permute-done | bytes 749600 | tf_op jit(solution)/shard_map/ppermute | solution.py:386
  78.3 16.1 %collective-permute-done.5 = bf16[976,384]{1,0:T(8,128)(2,1)} collective-permute-done((bf16[976,384]{1,0:T(8,128)(2,1)}, bf16[976,384]{1,0:T(8,128)(2,1)}, u32[]{:S(2)}, u32[]{:S(2)}) %collective-permute-start.5) | collective-permute-done | bytes 749600 | tf_op jit(solution)/shard_map/ppermute | solution.py:386
  94.4 16.1 %collective-permute-done.6 = bf16[976,384]{1,0:T(8,128)(2,1)} collective-permute-done((bf16[976,384]{1,0:T(8,128)(2,1)}, bf16[976,384]{1,0:T(8,128)(2,1)}, u32[]{:S(2)}, u32[]{:S(2)}) %collective-permute-start.6) | collective-permute-done | bytes 749600 | tf_op jit(solution)/shard_map/ppermute | solution.py:386
  113.2 28.1 %collective-permute-done.7 = bf16[976,384]{1,0:T(8,128)(2,1)S(1)} collective-permute-done((bf16[976,384]{1,0:T(8,128)(2,1)S(1)}, bf16[976,384]{1,0:T(8,128)(2,1)S(1)}, u32[]{:S(2)}, u32[]{:S(2)}) %collective-permute-start.7) | collective-permute-done | bytes 749600 | tf_op jit(solution)/shard_map/ppermute | solution.py:400
  142.4 3.1 forward_transform.3
  145.5 3.9 %all-to-all-start.1 = ((bf16[8,2,64,384]{3,2,1,0:T(8,128)(2,1)}), bf16[8,2,64,384]{3,2,1,0:T(8,128)(2,1)S(1)}, u32[]{:S(2)}, u32[]{:S(2)}) async-start(bf16[8,2,64,384]{3,2,1,0:T(8,128)(2,1)} %forward_transform.3), calls=%async_computation.1 | async-start | bytes 1572864 | tf_op jit(solution)/shard_map/all_to_all | solution.py:394
  151.4 18.9 %spectral_pass.1 = bf16[240,32,384]{2,1,0:T(8,128)(2,1)} custom-call(s32[1]{0:T(128)} %bitcast.2.band_ref, bf16[240,32,384]{2,1,0:T(8,128)(2,1)} %bitcast.18.moved_ref, bf16[16,15,240,240]{3,2,1,0:T(8,128)(2,1)} %constant.89.legendre_ref, f32[240,1]{1,0:T(8,128)} %copy.23.gain_ref, bf16[768,768]{1,0:T(8,128)(2,1)} %maximum_maximum_fusion.mixing_ref, ...), custom_call_target="tpu_custom_call" | custom-call | flops 8589934592 | bytes 14680064 | tf_op jit(solution)/shard_map/spectral_pass/pallas_call | solution.py:253
  172.5 7.8 %all-to-all-start.2 = ((bf16[16,15,4,384]{3,2,1,0:T(4,128)(2,1)}), bf16[16,15,4,384]{3,2,1,0:T(4,128)(2,1)S(1)}, u32[]{:S(2)}, u32[]{:S(2)}) async-start(bf16[16,15,4,384]{3,2,1,0:T(4,128)(2,1)} %slice.58), calls=%async_computation.2 | async-start | bytes 1474560 | tf_op jit(solution)/shard_map/all_to_all | solution.py:461
  181.7 11.1 %all-to-all-done.2 = bf16[16,15,4,384]{3,2,1,0:T(4,128)(2,1)S(1)} async-done(((bf16[16,15,4,384]{3,2,1,0:T(4,128)(2,1)}), bf16[16,15,4,384]{3,2,1,0:T(4,128)(2,1)S(1)}, u32[]{:S(2)}, u32[]{:S(2)}) %all-to-all-start.2) | async-done | bytes 737312 | tf_op jit(solution)/shard_map/all_to_all | solution.py:461
  193.7 4.8 %shared_spectral_pass.1 = (bf16[2,240,384]{2,1,0:T(8,128)(2,1)}, bf16[2,240,384]{2,1,0:T(8,128)(2,1)}) custom-call(s32[2]{0:T(128)} %pad_add_fusion.place_ref, bf16[4,240,384]{2,1,0:T(8,128)(2,1)} %bitcast.44, bf16[4,240,384]{2,1,0:T(8,128)(2,1)} %bitcast.45, bf16[16,15,240,240]{3,2,1,0:T(8,128)(2,1)} %constant.89.legendre_ref, f32[240,1]{1,0:T(8,128)} %copy.26.gain_ref, ...), custom_call_target="tpu_custom_call" | custom-call | flops 1073741824 | bytes 4194304 | tf_op jit(solution)/shard_map/shared_spectral_pass/pallas_call | solution.py:173
  200.0 15.8 %all_to_all.35 = bf16[16,15,4,384]{3,2,1,0:T(4,128)(2,1)S(1)} all-to-all(bf16[16,15,4,384]{3,2,1,0:T(4,128)(2,1)S(1)} %bitcast.58), channel_id=1, replica_groups=mesh['member'=16,'band'=16] {'band'}, dimensions={0} | all-to-all | bytes 1474560 | tf_op jit(solution)/shard_map/all_to_all | solution.py:469
  216.7 27.6 %all_to_all.36.spatial_ref = bf16[8,2,64,384]{3,2,1,0:T(8,128)(2,1)} all-to-all(bf16[8,2,64,384]{3,2,1,0:T(8,128)(2,1)S(1)} %reshape.102), channel_id=1, replica_groups={{0,32,64,96,128,160,192,224},{16,48,80,112,144,176,208,240},{1,33,65,97..., dimensions={0} | all-to-all | bytes 1572864 | tf_op jit(solution)/shard_map/all_to_all | solution.py:394
  244.3 7.1 %all-to-all-start.5 = ((bf16[16,15,32,384]{3,2,1,0:T(8,128)(2,1)}), bf16[16,15,32,384]{3,2,1,0:T(8,128)(2,1)}, u32[]{:S(2)}, u32[]{:S(2)}) async-start(bf16[16,15,32,384]{3,2,1,0:T(8,128)(2,1)} %bitcast.43), calls=%async_computation.5 | async-start | bytes 11796480 | tf_op jit(solution)/shard_map/all_to_all | solution.py:480
  252.3 3.3 inverse_transform.3
  255.6 76.6 %all-to-all-done.5.spatial_ref = bf16[16,15,32,384]{3,2,1,0:T(8,128)(2,1)} async-done(((bf16[16,15,32,384]{3,2,1,0:T(8,128)(2,1)}), bf16[16,15,32,384]{3,2,1,0:T(8,128)(2,1)}, u32[]{:S(2)}, u32[]{:S(2)}) %all-to-all-start.5) | async-done | bytes 5898272 | tf_op jit(solution)/shard_map/all_to_all | solution.py:480
  332.2 10.7 %inverse_transform.2.own_ref = bf16[15,480,384]{2,1,0:T(8,128)(2,1)} custom-call(bf16[16,15,32,384]{3,2,1,0:T(8,128)(2,1)} %all-to-all-done.5.spatial_ref, bf16[15,480,384]{2,1,0:T(8,128)(2,1)} %bitcast.49, bf16[480,512]{1,0:T(8,128)(2,1)} %constant.91.table_ref), custom_call_target="tpu_custom_call" | custom-call | flops 274877906944 | bytes 15728640 | tf_op jit(solution)/shard_map/inverse_transform/pallas_call | solution.py:288
  342.8 7.0 %spread_sums.1 = f32[16,8,128]{2,1,0:T(8,128)} custom-call(f32[15]{0:T(128)} %sine_multiply_fusion.weights_ref, bf16[15,480,384]{2,1,0:T(8,128)(2,1)} %inverse_transform.2.own_ref, bf16[16,480,384]{2,1,0:T(8,128)(2,1)} %all-gather.2.cloned.1.call-done.control_ref), custom_call_target="tpu_custom_call" | custom-call | flops 9437184 | bytes 11534336 | tf_op jit(solution)/shard_map/spread_sums/pallas_call | solution.py:331
  349.8 12.5 %all-to-all-start.6 = ((f32[16,8,128]{2,1,0:T(8,128)}), f32[16,8,128]{2,1,0:T(8,128)S(1)}, u32[]{:S(2)}, u32[]{:S(2)}) async-start(f32[16,8,128]{2,1,0:T(8,128)} %spread_sums.1), calls=%async_computation.6 | async-start | bytes 131072 | tf_op jit(solution)/shard_map/all_to_all | solution.py:487
  363.6 4.6 %all-to-all-done.6.sums_ref = f32[16,8,128]{2,1,0:T(8,128)S(1)} async-done(((f32[16,8,128]{2,1,0:T(8,128)}), f32[16,8,128]{2,1,0:T(8,128)S(1)}, u32[]{:S(2)}, u32[]{:S(2)}) %all-to-all-start.6) | async-done | bytes 65568 | tf_op jit(solution)/shard_map/all_to_all | solution.py:487
  368.8 9.9 %rescaled.1 = bf16[15,480,384]{2,1,0:T(8,128)(2,1)} custom-call(f32[1]{0:T(128)} %bitcast.1.target_ref, f32[16,8,128]{2,1,0:T(8,128)} %copy-done.3, bf16[15,480,384]{2,1,0:T(8,128)(2,1)} %inverse_transform.2.own_ref, bf16[16,480,384]{2,1,0:T(8,128)(2,1)} %all-gather.2.cloned.1.call-done.control_ref), custom_call_target="tpu_custom_call" | custom-call | flops 9437184 | bytes 17825792 | tf_op jit(solution)/shard_map/rescaled/pallas_call | solution.py:356
  (64 shorter events, 34.4 us)
Async XLA Ops:
  8.0 0.5 copy-start.4
  13.8 12.7 %copy-start.6 = (f32[384]{0:T(512)S(1)}, f32[384]{0:T(512)}, u32[]{:S(2)}) copy-start(f32[384]{0:T(512)} %param.15) | copy-start | bytes 4612
  13.8 36.4 %collective-permute-start.1 = (bf16[976,384]{1,0:T(8,128)(2,1)}, bf16[976,384]{1,0:T(8,128)(2,1)S(1)}, u32[]{:S(2)}, u32[]{:S(2)}) collective-permute-start(bf16[976,384]{1,0:T(8,128)(2,1)} %get-tuple-element.33), channel_id=1, source_target_pairs={{0,192},{1,193},{2,194},{3,195},{4,196},{5,197},{6,198},{7,199},{8... | collective-permute-start | bytes 2248712 | tf_op jit(solution)/shard_map/ppermute | solution.py:386
  24.5 23.5 %collective-permute-start = (bf16[496,384]{1,0:T(8,128)(2,1)}, bf16[496,384]{1,0:T(8,128)(2,1)S(1)}, u32[]{:S(2)}, u32[]{:S(2)}) collective-permute-start(bf16[496,384]{1,0:T(8,128)(2,1)} %pad_maximum_fusion.7), channel_id=1, source_target_pairs={{0,224},{1,225},{2,226},{3,227},{4,228},{5,229},{6,230},{7,231},{8... | collective-permute-start | bytes 1142792 | tf_op jit(solution)/shard_map/ppermute | solution.py:386
  36.7 108.8 %all-to-all-start = ((bf16[16,15,32,384]{3,2,1,0:T(8,128)(2,1)}), bf16[16,15,32,384]{3,2,1,0:T(8,128)(2,1)}, u32[]{:S(2)}, u32[]{:S(2)}) async-start(bf16[16,15,32,384]{3,2,1,0:T(8,128)(2,1)} %forward_transform.2), calls=%async_computation | async-start | bytes 11796480 | tf_op jit(solution)/shard_map/all_to_all | solution.py:438
  43.1 19.5 %collective-permute-start.2 = (bf16[976,384]{1,0:T(8,128)(2,1)}, bf16[976,384]{1,0:T(8,128)(2,1)S(1)}, u32[]{:S(2)}, u32[]{:S(2)}) collective-permute-start(bf16[976,384]{1,0:T(8,128)(2,1)} %get-tuple-element.29), channel_id=1, source_target_pairs={{0,160},{1,161},{2,162},{3,163},{4,164},{5,165},{6,166},{7,167},{8... | collective-permute-start | bytes 2248712 | tf_op jit(solution)/shard_map/ppermute | solution.py:386
  44.4 18.2 %collective-permute-start.3 = (bf16[976,384]{1,0:T(8,128)(2,1)}, bf16[976,384]{1,0:T(8,128)(2,1)S(1)}, u32[]{:S(2)}, u32[]{:S(2)}) collective-permute-start(bf16[976,384]{1,0:T(8,128)(2,1)} %get-tuple-element.30), channel_id=1, source_target_pairs={{0,128},{1,129},{2,130},{3,131},{4,132},{5,133},{6,134},{7,135},{8... | collective-permute-start | bytes 2248712 | tf_op jit(solution)/shard_map/ppermute | solution.py:386
  45.8 32.5 %collective-permute-start.4 = (bf16[976,384]{1,0:T(8,128)(2,1)}, bf16[976,384]{1,0:T(8,128)(2,1)}, u32[]{:S(2)}, u32[]{:S(2)}) collective-permute-start(bf16[976,384]{1,0:T(8,128)(2,1)} %get-tuple-element.31), channel_id=1, source_target_pairs={{0,96},{1,97},{2,98},{3,99},{4,100},{5,101},{6,102},{7,103},{8,104... | collective-permute-start | bytes 2248712 | tf_op jit(solution)/shard_map/ppermute | solution.py:386
  48.0 46.4 %collective-permute-start.5 = (bf16[976,384]{1,0:T(8,128)(2,1)}, bf16[976,384]{1,0:T(8,128)(2,1)}, u32[]{:S(2)}, u32[]{:S(2)}) collective-permute-start(bf16[976,384]{1,0:T(8,128)(2,1)} %get-tuple-element.32), channel_id=1, source_target_pairs={{0,64},{1,65},{2,66},{3,67},{4,68},{5,69},{6,70},{7,71},{8,72},{9,... | collective-permute-start | bytes 2248712 | tf_op jit(solution)/shard_map/ppermute | solution.py:386
  50.1 60.3 %collective-permute-start.6 = (bf16[976,384]{1,0:T(8,128)(2,1)}, bf16[976,384]{1,0:T(8,128)(2,1)}, u32[]{:S(2)}, u32[]{:S(2)}) collective-permute-start(bf16[976,384]{1,0:T(8,128)(2,1)} %get-tuple-element.28), channel_id=1, source_target_pairs={{0,32},{1,33},{2,34},{3,35},{4,36},{5,37},{6,38},{7,39},{8,40},{9,... | collective-permute-start | bytes 2248712 | tf_op jit(solution)/shard_map/ppermute | solution.py:386
  62.6 47.8 %copy-start.1 = (bf16[976,384]{1,0:T(8,128)(2,1)}, bf16[976,384]{1,0:T(8,128)(2,1)S(1)}, u32[]{:S(2)}) copy-start(bf16[976,384]{1,0:T(8,128)(2,1)S(1)} %collective-permute-done.3) | copy-start | bytes 2248708
  110.4 2.2 copy-start.7
  111.2 30.1 %collective-permute-start.7 = (bf16[976,384]{1,0:T(8,128)(2,1)S(1)}, bf16[976,384]{1,0:T(8,128)(2,1)S(1)}, u32[]{:S(2)}, u32[]{:S(2)}) collective-permute-start(bf16[976,384]{1,0:T(8,128)(2,1)S(1)} %fusion.6), channel_id=1, source_target_pairs={{0,16},{32,48},{64,80},{96,112},{128,144},{160,176},{192,208},{224... | collective-permute-start | bytes 2248712 | tf_op jit(solution)/shard_map/ppermute | solution.py:400
  145.5 3.9 %copy-start.5 = (f32[240]{0:T(256)S(1)}, f32[240]{0:T(256)}, u32[]{:S(2)}) copy-start(f32[240]{0:T(256)} %copy-done.4) | copy-start | bytes 2884
  145.5 4.7 %copy-start = (bf16[384,384]{1,0:T(8,128)(2,1)S(1)}, bf16[384,384]{1,0:T(8,128)(2,1)}, u32[]{:S(2)}) copy-start(bf16[384,384]{1,0:T(8,128)(2,1)} %param.17) | copy-start | bytes 884740
  145.5 4.8 %copy-start.2 = (bf16[384,384]{1,0:T(8,128)(2,1)S(1)}, bf16[384,384]{1,0:T(8,128)(2,1)}, u32[]{:S(2)}) copy-start(bf16[384,384]{1,0:T(8,128)(2,1)} %param.16) | copy-start | bytes 884740
  145.5 25.3 %all-to-all-start.1 = ((bf16[8,2,64,384]{3,2,1,0:T(8,128)(2,1)}), bf16[8,2,64,384]{3,2,1,0:T(8,128)(2,1)S(1)}, u32[]{:S(2)}, u32[]{:S(2)}) async-start(bf16[8,2,64,384]{3,2,1,0:T(8,128)(2,1)} %forward_transform.3), calls=%async_computation.1 | async-start | bytes 1572864 | tf_op jit(solution)/shard_map/all_to_all | solution.py:394
  172.5 20.2 %all-to-all-start.2 = ((bf16[16,15,4,384]{3,2,1,0:T(4,128)(2,1)}), bf16[16,15,4,384]{3,2,1,0:T(4,128)(2,1)S(1)}, u32[]{:S(2)}, u32[]{:S(2)}) async-start(bf16[16,15,4,384]{3,2,1,0:T(4,128)(2,1)} %slice.58), calls=%async_computation.2 | async-start | bytes 1474560 | tf_op jit(solution)/shard_map/all_to_all | solution.py:461
  244.3 87.9 %all-to-all-start.5 = ((bf16[16,15,32,384]{3,2,1,0:T(8,128)(2,1)}), bf16[16,15,32,384]{3,2,1,0:T(8,128)(2,1)}, u32[]{:S(2)}, u32[]{:S(2)}) async-start(bf16[16,15,32,384]{3,2,1,0:T(8,128)(2,1)} %bitcast.43), calls=%async_computation.5 | async-start | bytes 11796480 | tf_op jit(solution)/shard_map/all_to_all | solution.py:480
  251.4 91.5 %all-gather.2.cloned.1.call-start = ((), (), s32[]{:S(2)}) async-start(), calls=%async_computation.7 | async-start | bytes 6635520 | tf_op jit(solution)/shard_map/all_gather | solution.py:484
  342.8 19.6 %copy-start.8 = (f32[8]{0:T(128)S(1)}, f32[8]{0:T(128)}, u32[]{:S(2)}) copy-start(f32[8]{0:T(128)} %param.20) | copy-start | bytes 100
  349.8 18.4 %all-to-all-start.6 = ((f32[16,8,128]{2,1,0:T(8,128)}), f32[16,8,128]{2,1,0:T(8,128)S(1)}, u32[]{:S(2)}, u32[]{:S(2)}) async-start(f32[16,8,128]{2,1,0:T(8,128)} %spread_sums.1), calls=%async_computation.6 | async-start | bytes 131072 | tf_op jit(solution)/shard_map/all_to_all | solution.py:487
  368.2 0.6 copy-start.3
Sparse Core Ops, SparseCore 0:
  255.7 68.2 all-gather.1

commit v5 on v4

--- a/solution.py
+++ b/solution.py
@@ -22,7 +22,7 @@
 RINGS = [[2 * z + h for z in range(DEPTH)] for h in range(2)]
 STEP = 3
 TOTAL_WEIGHT = float(np.sum(np.sin((np.arange(H) + 0.5) * np.pi / H)) * np.pi / H * E * W)
-VMEM_LIMIT = 58 * 1024 * 1024
+MIB = 1 << 20
 
 
 def legendre_table(degree_count, order_count, lat_count):
@@ -139,7 +139,7 @@
         ],
         out_specs=pl.BlockSpec((groups, step, size, E), lambda j: (0, j, 0, 0)),
         out_shape=jax.ShapeDtypeStruct((groups, rows, size, E), jnp.bfloat16),
-        compiler_params=pltpu.CompilerParams(vmem_limit_bytes=VMEM_LIMIT),
+        compiler_params=pltpu.CompilerParams(vmem_limit_bytes=58 * MIB),
         cost_estimate=pl.CostEstimate(flops=flops, bytes_accessed=rows << 20, transcendentals=0),
         name="forward_transform",
     )(weights, x, gain, table)
@@ -188,7 +188,7 @@
             out_specs=[row(0), row(0)],
         ),
         out_shape=[pair, pair],
-        compiler_params=pltpu.CompilerParams(vmem_limit_bytes=VMEM_LIMIT),
+        compiler_params=pltpu.CompilerParams(vmem_limit_bytes=16 * MIB),
         cost_estimate=pl.CostEstimate(flops=1 << 30, bytes_accessed=4 << 20, transcendentals=0),
         name="shared_spectral_pass",
     )(place, moved, moved, legendre, gain, mixing)
@@ -269,7 +269,7 @@
             ],
         ),
         out_shape=jax.ShapeDtypeStruct((H, SLOTS, E), jnp.bfloat16),
-        compiler_params=pltpu.CompilerParams(vmem_limit_bytes=VMEM_LIMIT),
+        compiler_params=pltpu.CompilerParams(vmem_limit_bytes=58 * MIB),
         cost_estimate=pl.CostEstimate(flops=8 << 30, bytes_accessed=14 << 20, transcendentals=0),
         name="spectral_pass",
     )(band, moved, legendre, gain, mixing, swap)
@@ -295,7 +295,7 @@
         ],
         out_specs=pl.BlockSpec((step, W, E), lambda j: (j, 0, 0)),
         out_shape=jax.ShapeDtypeStruct((rows, W, E), jnp.bfloat16),
-        compiler_params=pltpu.CompilerParams(vmem_limit_bytes=VMEM_LIMIT),
+        compiler_params=pltpu.CompilerParams(vmem_limit_bytes=18 * MIB),
         cost_estimate=pl.CostEstimate(
             flops=flops, bytes_accessed=rows << 20, transcendentals=rows * W * E
         ),
@@ -335,7 +335,7 @@
         out_specs=pl.BlockSpec((BANDS, 8, 128), lambda j: (0, 0, 0)),
         out_shape=jax.ShapeDtypeStruct((BANDS, 8, 128), jnp.float32),
         scratch_shapes=[pltpu.VMEM((8, E), jnp.float32)],
-        compiler_params=pltpu.CompilerParams(vmem_limit_bytes=VMEM_LIMIT),
+        compiler_params=pltpu.CompilerParams(vmem_limit_bytes=12 * MIB),
         cost_estimate=pl.CostEstimate(flops=9 << 20, bytes_accessed=11 << 20, transcendentals=0),
         name="spread_sums",
     )(weights, own, control)
@@ -364,7 +364,7 @@
         ],
         out_specs=row,
         out_shape=jax.ShapeDtypeStruct((ROWS, W, E), jnp.bfloat16),
-        compiler_params=pltpu.CompilerParams(vmem_limit_bytes=VMEM_LIMIT),
+        compiler_params=pltpu.CompilerParams(vmem_limit_bytes=14 * MIB),
         cost_estimate=pl.CostEstimate(flops=9 << 20, bytes_accessed=17 << 20, transcendentals=0),
         name="rescaled",
     )(target, sums, own, control)
@@ -381,7 +381,7 @@
 def scattered(field, extra):
     member = lax.axis_index("member")
     kept = jnp.concatenate([field[:2].reshape(2 * W, E), extra])
-    for z in range(1, DEPTH):
+    for z in (1, 7, 2, 6, 3, 5, 4):
         piece = field[2 * z : min(2 * z + 2, ROWS)].reshape(-1, E)
         arrived = lax.ppermute(jnp.concatenate([piece, extra]), "member", [(0, 2 * z)])
         if 2 * z + 1 == ROWS:
@@ -394,6 +394,17 @@
     return lax.all_to_all(
         pieces, "member", split_axis=0, concat_axis=0, axis_index_groups=RINGS, tiled=True
     )
+
+
+def permuted_along_z(pieces):
+    z = lax.axis_index("member") // 2
+    result = pieces
+    for shift in (1, 7, 2, 6, 3, 5, 4):
+        block = lax.dynamic_index_in_dim(pieces, (z + shift) % DEPTH, 0, keepdims=False)
+        pairs = [(ring[a], ring[(a + shift) % DEPTH]) for ring in RINGS for a in range(DEPTH)]
+        arrived = lax.ppermute(block, "member", pairs)
+        result = lax.dynamic_update_index_in_dim(result, arrived, (z - shift) % DEPTH, 0)
+    return result
 
 
 def across(value):
@@ -444,7 +455,7 @@
     control_gain = jnp.sum(control_parts[2 * W : 2 * W + 3, :L].astype(jnp.float32), axis=0)
     control_weights = lax.dynamic_slice(jnp.pad(weights, (0, 1)), (2 * z,), (2,))
     control_fourier = forward_transform(
-        control_x, norm_gain[None, :], control_weights, rounded(shared_ahead_np), DEPTH, 2, 32 << 30
+        control_x, norm_gain[None, :], control_weights, rounded(shared_ahead_np), DEPTH, 2, 1 << 29
     )
     moved, control_fourier = lax.optimization_barrier((moved, control_fourier))
     control_fourier = exchanged_along_z(control_fourier).reshape(DEPTH, 2, BANDS, 4, E)
@@ -473,13 +484,13 @@
         concat_axis=0,
         tiled=True,
     )
-    control_spatial = jnp.pad(control_spatial, ((0, 0), (0, 1), (0, 0), (0, 0)))
-    control_spatial = control_spatial.reshape(BANDS, DEPTH, 2, 4, E).transpose(1, 2, 0, 3, 4)
-    control_spatial = exchanged_along_z(control_spatial.reshape(DEPTH, 2, BANDS * 4, E))
     control_spatial, returned = lax.optimization_barrier((control_spatial, returned))
     spatial = lax.all_to_all(
         returned.reshape(BANDS, ROWS, SLOTS, E), "band", split_axis=0, concat_axis=0, tiled=True
     )
+    control_spatial = jnp.pad(control_spatial, ((0, 0), (0, 1), (0, 0), (0, 0)))
+    control_spatial = control_spatial.reshape(BANDS, DEPTH, 2, 4, E).transpose(1, 2, 0, 3, 4)
+    control_spatial = permuted_along_z(control_spatial.reshape(DEPTH, 2, BANDS * 4, E))
     control = inverse_transform(control_spatial, control_x, rounded(shared_back_np), 2, 1 << 29)
     control = lax.all_gather(control, "member", tiled=True, axis_index_groups=RINGS)
 

time: 388 us -> 356 us (0.918)
  blocking collectives: 43.4 us -> 15.8 us
  local copies, waits for them, and re-layouts: 12.8 us -> 35.9 us
  Pallas kernels: 67.3 us -> 52.9 us
  waiting for transfers between devices: 179 us -> 165 us
  starting transfers between devices: 58.6 us -> 63.8 us
    all_to_all x1 -> x0, blocking collectives: 27.6 us -> none  [exchanged_along_z(): lax.all_to_all(pieces, 'member', split_axis=0, concat_axis=0, axis_index_...]
    unnamed x18 -> x36, local copies, waits for them, and re-layouts: 1.17 us -> 25 us
    all_to_all x1, waiting for transfers between devices: 76.6 us -> 53.6 us  [shards(): lax.all_to_all(returned.reshape(BANDS, ROWS, SLOTS, E), 'band', split_axi...]
    ppermute x0 -> x7, waiting for transfers between devices: none -> 13.3 us  [permuted_along_z(): arrived = lax.ppermute(block, 'member', pairs)]
    ppermute x0 -> x7, starting transfers between devices: none -> 9.91 us  [permuted_along_z(): arrived = lax.ppermute(block, 'member', pairs)]
    ppermute x7, waiting for transfers between devices: 58.1 us -> 49 us  [scattered(): lax.ppermute(jnp.concatenate([piece, extra]), 'member', [(0, 2 * z)])]
    all_gather x1, waiting for transfers between devices: 0.01 us -> 8.01 us  [shards(): lax.all_gather(control, 'member', tiled=True, axis_index_groups=RINGS)]
    ppermute x1, waiting for transfers between devices: 28.1 us -> 21.3 us  [across(): lax.ppermute(value, 'member', [(2 * z, 2 * z + 1) for z in range(DEPTH)])]
  transfers between devices with their start and end apart: 14 -> 21, of which waited for: 9 -> 14; matrix products, arithmetic and copies ran while one was open for 2% -> 4% of each run, Pallas kernels for 12% -> 9%
where the time goes in v5:
time: 356 us; the launch traced here: 355 us
  waiting for transfers between devices  165 us (46%)
  starting transfers between devices  63.8 us (18%)
  Pallas kernels  52.9 us (15%)
  local copies, waits for them, and re-layouts  35.9 us (10%)
  between operations  15.9 us (4%)
  blocking collectives  15.8 us (4%)
  other arithmetic  5.63 us (2%)
    all_to_all x1, waiting for transfers between devices, shards(): lax.all_to_all(returned.reshape(BANDS, ROWS, SLOTS, E), 'band', split_axi...  53.6 us
    ppermute x7, waiting for transfers between devices, scattered(): lax.ppermute(jnp.concatenate([piece, extra]), 'member', [(0, 2 * z)])  49 us
    unnamed x36, local copies, waits for them, and re-layouts  25 us
    ppermute x1, waiting for transfers between devices, across(): lax.ppermute(value, 'member', [(2 * z, 2 * z + 1) for z in range(DEPTH)])  21.3 us
    pallas_call x1, Pallas kernels, spectral_pass(): pl.pallas_call(spectral_kernel, grid_spec=pltpu.PrefetchScalarGridSpec(nu...  18.8 us
    ppermute x7, starting transfers between devices, scattered(): lax.ppermute(jnp.concatenate([piece, extra]), 'member', [(0, 2 * z)])  17 us
    all_to_all x1, blocking collectives, shards(): lax.all_to_all(control_spatial.transpose(1, 0, 2).reshape(BANDS, ROWS, 4,...  15.8 us
    ppermute x7, waiting for transfers between devices, permuted_along_z(): arrived = lax.ppermute(block, 'member', pairs)  13.3 us
  transfers between devices with their start and end apart: 21, of which 14 were waited for; matrix products, arithmetic and copies ran while one was open for 4% of the time, Pallas kernels for 9%

profile of v5, /device:TPU:1, one launch (start us, length us, event | category | flops | bytes accessed | tf_op | source)
XLA Modules:
  0.0 354.7 jit_solution(9575963371413473058)
XLA Ops:
  8.4 9.7 %forward_transform.2 = bf16[16,15,32,384]{3,2,1,0:T(8,128)(2,1)} custom-call(f32[15]{0:T(128)} %sine_multiply_fusion.weights_ref, bf16[15,480,384]{2,1,0:T(8,128)(2,1)} %bitcast.75, f32[1,384]{1,0:T(1,128)} %broadcast_in_dim.43.gain_ref, bf16[512,480]{1,0:T(8,128)(2,1)} %constant.199.table_ref), custom_call_target="tpu_custom_call" | custom-call | flops 137438953472 | bytes 15728640 | tf_op jit(solution)/shard_map/forward_transform/pallas_call | solution.py:131
  18.1 7.7 %all-to-all-start = ((bf16[16,15,32,384]{3,2,1,0:T(8,128)(2,1)}), bf16[16,15,32,384]{3,2,1,0:T(8,128)(2,1)}, u32[]{:S(2)}, u32[]{:S(2)}) async-start(bf16[16,15,32,384]{3,2,1,0:T(8,128)(2,1)} %forward_transform.2), calls=%async_computation | async-start | bytes 11796480 | tf_op jit(solution)/shard_map/all_to_all | solution.py:449
  35.5 4.6 %collective-permute-start.5 = (bf16[496,384]{1,0:T(8,128)(2,1)S(1)}, bf16[496,384]{1,0:T(8,128)(2,1)S(1)}, u32[]{:S(2)}, u32[]{:S(2)}) collective-permute-start(bf16[496,384]{1,0:T(8,128)(2,1)S(1)} %pad_maximum_fusion.7), channel_id=1, source_target_pairs={{0,224},{1,225},{2,226},{3,227},{4,228},{5,229},{6,230},{7,231},{8... | collective-permute-start | bytes 1142792 | tf_op jit(solution)/shard_map/ppermute | solution.py:386
  52.6 11.8 %collective-permute-done.1 = bf16[976,384]{1,0:T(8,128)(2,1)S(1)} collective-permute-done((bf16[976,384]{1,0:T(8,128)(2,1)}, bf16[976,384]{1,0:T(8,128)(2,1)S(1)}, u32[]{:S(2)}, u32[]{:S(2)}) %collective-permute-start.1) | collective-permute-done | bytes 749600 | tf_op jit(solution)/shard_map/ppermute | solution.py:386
  66.6 13.9 %collective-permute-done.3 = bf16[976,384]{1,0:T(8,128)(2,1)} collective-permute-done((bf16[976,384]{1,0:T(8,128)(2,1)}, bf16[976,384]{1,0:T(8,128)(2,1)}, u32[]{:S(2)}, u32[]{:S(2)}) %collective-permute-start.3) | collective-permute-done | bytes 749600 | tf_op jit(solution)/shard_map/ppermute | solution.py:386
  82.6 16.1 %collective-permute-done = bf16[976,384]{1,0:T(8,128)(2,1)} collective-permute-done((bf16[976,384]{1,0:T(8,128)(2,1)}, bf16[976,384]{1,0:T(8,128)(2,1)}, u32[]{:S(2)}, u32[]{:S(2)}) %collective-permute-start) | collective-permute-done | bytes 749600 | tf_op jit(solution)/shard_map/ppermute | solution.py:386
  101.5 21.3 %collective-permute-done.7 = bf16[976,384]{1,0:T(8,128)(2,1)S(1)} collective-permute-done((bf16[976,384]{1,0:T(8,128)(2,1)S(1)}, bf16[976,384]{1,0:T(8,128)(2,1)S(1)}, u32[]{:S(2)}, u32[]{:S(2)}) %collective-permute-start.7) | collective-permute-done | bytes 749600 | tf_op jit(solution)/shard_map/ppermute | solution.py:411
  127.1 8.9 %all-to-all-start.1 = ((bf16[8,2,64,384]{3,2,1,0:T(8,128)(2,1)}), bf16[8,2,64,384]{3,2,1,0:T(8,128)(2,1)S(1)}, u32[]{:S(2)}, u32[]{:S(2)}) async-start(bf16[8,2,64,384]{3,2,1,0:T(8,128)(2,1)} %forward_transform.3), calls=%async_computation.1 | async-start | bytes 1572864 | tf_op jit(solution)/shard_map/all_to_all | solution.py:394
  138.0 18.8 %spectral_pass.1 = bf16[240,32,384]{2,1,0:T(8,128)(2,1)} custom-call(s32[1]{0:T(128)} %bitcast.2.band_ref, bf16[240,32,384]{2,1,0:T(8,128)(2,1)} %bitcast.18.moved_ref, bf16[16,15,240,240]{3,2,1,0:T(8,128)(2,1)} %constant.201.legendre_ref, f32[240,1]{1,0:T(8,128)} %copy.23.gain_ref, bf16[768,768]{1,0:T(8,128)(2,1)} %maximum_maximum_fusion.mixing_ref, ...), custom_call_target="tpu_custom_call" | custom-call | flops 8589934592 | bytes 14680064 | tf_op jit(solution)/shard_map/spectral_pass/pallas_call | solution.py:253
  161.2 7.8 %all-to-all-start.2 = ((bf16[16,15,4,384]{3,2,1,0:T(4,128)(2,1)}), bf16[16,15,4,384]{3,2,1,0:T(4,128)(2,1)S(1)}, u32[]{:S(2)}, u32[]{:S(2)}) async-start(bf16[16,15,4,384]{3,2,1,0:T(4,128)(2,1)} %slice.58), calls=%async_computation.2 | async-start | bytes 1474560 | tf_op jit(solution)/shard_map/all_to_all | solution.py:472
  169.3 12.2 %all-to-all-done.2 = bf16[16,15,4,384]{3,2,1,0:T(4,128)(2,1)S(1)} async-done(((bf16[16,15,4,384]{3,2,1,0:T(4,128)(2,1)}), bf16[16,15,4,384]{3,2,1,0:T(4,128)(2,1)S(1)}, u32[]{:S(2)}, u32[]{:S(2)}) %all-to-all-start.2) | async-done | bytes 737312 | tf_op jit(solution)/shard_map/all_to_all | solution.py:472
  181.6 9.4 %copy-done = bf16[16,15,240,240]{3,2,1,0:T(8,128)(2,1)S(1)} copy-done((bf16[16,15,240,240]{3,2,1,0:T(8,128)(2,1)S(1)}, bf16[16,15,240,240]{3,2,1,0:T(8,128)(2,1)}, u32[]{:S(2)}) %copy-start) | copy-done | bytes 27648024
  193.7 15.8 %all_to_all.30 = bf16[16,15,4,384]{3,2,1,0:T(4,128)(2,1)S(1)} all-to-all(bf16[16,15,4,384]{3,2,1,0:T(4,128)(2,1)S(1)} %bitcast.86), channel_id=1, replica_groups=mesh['member'=16,'band'=16] {'band'}, dimensions={0} | all-to-all | bytes 1474560 | tf_op jit(solution)/shard_map/all_to_all | solution.py:480
  209.5 5.2 %all-to-all-start.4 = ((bf16[16,15,32,384]{3,2,1,0:T(8,128)(2,1)}), bf16[16,15,32,384]{3,2,1,0:T(8,128)(2,1)}, u32[]{:S(2)}, u32[]{:S(2)}) async-start(bf16[16,15,32,384]{3,2,1,0:T(8,128)(2,1)} %bitcast.79), calls=%async_computation.4 | async-start | bytes 11796480 | tf_op jit(solution)/shard_map/all_to_all | solution.py:488
  216.1 5.1 %collective-permute-done.8 = bf16[2,64,384]{2,1,0:T(8,128)(2,1)S(1)} collective-permute-done((bf16[2,64,384]{2,1,0:T(8,128)(2,1)S(1)}, bf16[2,64,384]{2,1,0:T(8,128)(2,1)S(1)}, u32[]{:S(2)}, u32[]{:S(2)}) %collective-permute-start.8) | collective-permute-done | bytes 98336 | tf_op jit(solution)/shard_map/ppermute | solution.py:405
  222.4 3.6 %collective-permute-start.14 = (bf16[2,64,384]{2,1,0:T(8,128)(2,1)S(1)}, bf16[2,64,384]{2,1,0:T(8,128)(2,1)S(1)}, u32[]{:S(2)}, u32[]{:S(2)}) collective-permute-start(bf16[2,64,384]{2,1,0:T(8,128)(2,1)S(1)} %get-tuple-element.28), channel_id=1, source_target_pairs={{0,128},{32,160},{64,192},{96,224},{128,0},{160,32},{192,64},{224,... | collective-permute-start | bytes 294920 | tf_op jit(solution)/shard_map/ppermute | solution.py:405
  231.7 8.2 %collective-permute-done.10 = bf16[2,64,384]{2,1,0:T(8,128)(2,1)S(1)} collective-permute-done((bf16[2,64,384]{2,1,0:T(8,128)(2,1)S(1)}, bf16[2,64,384]{2,1,0:T(8,128)(2,1)S(1)}, u32[]{:S(2)}, u32[]{:S(2)}) %collective-permute-start.10) | collective-permute-done | bytes 98336 | tf_op jit(solution)/shard_map/ppermute | solution.py:405
  241.9 53.6 %all-to-all-done.4.spatial_ref = bf16[16,15,32,384]{3,2,1,0:T(8,128)(2,1)} async-done(((bf16[16,15,32,384]{3,2,1,0:T(8,128)(2,1)}), bf16[16,15,32,384]{3,2,1,0:T(8,128)(2,1)}, u32[]{:S(2)}, u32[]{:S(2)}) %all-to-all-start.4) | async-done | bytes 5898272 | tf_op jit(solution)/shard_map/all_to_all | solution.py:488
  298.1 7.8 %inverse_transform.2.own_ref = bf16[15,480,384]{2,1,0:T(8,128)(2,1)S(1)} custom-call(bf16[16,15,32,384]{3,2,1,0:T(8,128)(2,1)} %all-to-all-done.4.spatial_ref, bf16[15,480,384]{2,1,0:T(8,128)(2,1)S(1)} %bitcast.78, bf16[480,512]{1,0:T(8,128)(2,1)S(1)} %copy-done.12), custom_call_target="tpu_custom_call" | custom-call | flops 274877906944 | bytes 15728640 | tf_op jit(solution)/shard_map/inverse_transform/pallas_call | solution.py:288
  308.4 8.0 %all-gather.2.cloned.1.call-done.control_ref = bf16[16,480,384]{2,1,0:T(8,128)(2,1)} async-done(((bf16[2,480,384]{2,1,0:T(8,128)(2,1)}), bf16[16,480,384]{2,1,0:T(8,128)(2,1)}) %all-gather.2.cloned.1.call-update) | async-done | bytes 5898256 | tf_op jit(solution)/shard_map/all_gather | solution.py:495
  321.6 3.7 %spread_sums.1 = f32[16,8,128]{2,1,0:T(8,128)} custom-call(f32[15]{0:T(128)S(1)} %copy-done.11, bf16[15,480,384]{2,1,0:T(8,128)(2,1)S(1)} %copy-done.4, bf16[16,480,384]{2,1,0:T(8,128)(2,1)S(1)} %copy-done.1), custom_call_target="tpu_custom_call" | custom-call | flops 9437184 | bytes 11534336 | tf_op jit(solution)/shard_map/spread_sums/pallas_call | solution.py:331
  325.4 5.9 %all-to-all-start.5 = ((f32[16,8,128]{2,1,0:T(8,128)}), f32[16,8,128]{2,1,0:T(8,128)S(1)}, u32[]{:S(2)}, u32[]{:S(2)}) async-start(f32[16,8,128]{2,1,0:T(8,128)} %spread_sums.1), calls=%async_computation.5 | async-start | bytes 131072 | tf_op jit(solution)/shard_map/all_to_all | solution.py:498
  332.6 4.5 %all-to-all-done.5.sums_ref = f32[16,8,128]{2,1,0:T(8,128)S(1)} async-done(((f32[16,8,128]{2,1,0:T(8,128)}), f32[16,8,128]{2,1,0:T(8,128)S(1)}, u32[]{:S(2)}, u32[]{:S(2)}) %all-to-all-start.5) | async-done | bytes 65568 | tf_op jit(solution)/shard_map/all_to_all | solution.py:498
  342.3 5.5 %rescaled.1 = bf16[15,480,384]{2,1,0:T(8,128)(2,1)} custom-call(f32[1]{0:T(128)} %bitcast.1.target_ref, f32[16,8,128]{2,1,0:T(8,128)S(1)} %all-to-all-done.5.sums_ref, bf16[15,480,384]{2,1,0:T(8,128)(2,1)S(1)} %copy-done.5, bf16[16,480,384]{2,1,0:T(8,128)(2,1)S(1)} %copy-done.2), custom_call_target="tpu_custom_call" | custom-call | flops 9437184 | bytes 17825792 | tf_op jit(solution)/shard_map/rescaled/pallas_call | solution.py:356
  (103 shorter events, 69.6 us)
Async XLA Ops:
  18.1 109.0 %all-to-all-start = ((bf16[16,15,32,384]{3,2,1,0:T(8,128)(2,1)}), bf16[16,15,32,384]{3,2,1,0:T(8,128)(2,1)}, u32[]{:S(2)}, u32[]{:S(2)}) async-start(bf16[16,15,32,384]{3,2,1,0:T(8,128)(2,1)} %forward_transform.2), calls=%async_computation | async-start | bytes 11796480 | tf_op jit(solution)/shard_map/all_to_all | solution.py:449
  31.6 18.8 %collective-permute-start.6 = (bf16[976,384]{1,0:T(8,128)(2,1)S(1)}, bf16[976,384]{1,0:T(8,128)(2,1)S(1)}, u32[]{:S(2)}, u32[]{:S(2)}) collective-permute-start(bf16[976,384]{1,0:T(8,128)(2,1)S(1)} %get-tuple-element.35), channel_id=1, source_target_pairs={{0,32},{1,33},{2,34},{3,35},{4,36},{5,37},{6,38},{7,39},{8,40},{9,... | collective-permute-start | bytes 2248712 | tf_op jit(solution)/shard_map/ppermute | solution.py:386
  35.5 12.7 %collective-permute-start.5 = (bf16[496,384]{1,0:T(8,128)(2,1)S(1)}, bf16[496,384]{1,0:T(8,128)(2,1)S(1)}, u32[]{:S(2)}, u32[]{:S(2)}) collective-permute-start(bf16[496,384]{1,0:T(8,128)(2,1)S(1)} %pad_maximum_fusion.7), channel_id=1, source_target_pairs={{0,224},{1,225},{2,226},{3,227},{4,228},{5,229},{6,230},{7,231},{8... | collective-permute-start | bytes 1142792 | tf_op jit(solution)/shard_map/ppermute | solution.py:386
  40.2 24.2 %collective-permute-start.1 = (bf16[976,384]{1,0:T(8,128)(2,1)}, bf16[976,384]{1,0:T(8,128)(2,1)S(1)}, u32[]{:S(2)}, u32[]{:S(2)}) collective-permute-start(bf16[976,384]{1,0:T(8,128)(2,1)} %get-tuple-element.36), channel_id=1, source_target_pairs={{0,160},{1,161},{2,162},{3,163},{4,164},{5,165},{6,166},{7,167},{8... | collective-permute-start | bytes 2248712 | tf_op jit(solution)/shard_map/ppermute | solution.py:386
  41.8 24.8 %collective-permute-start.2 = (bf16[976,384]{1,0:T(8,128)(2,1)}, bf16[976,384]{1,0:T(8,128)(2,1)S(1)}, u32[]{:S(2)}, u32[]{:S(2)}) collective-permute-start(bf16[976,384]{1,0:T(8,128)(2,1)} %get-tuple-element.37), channel_id=1, source_target_pairs={{0,96},{1,97},{2,98},{3,99},{4,100},{5,101},{6,102},{7,103},{8,104... | collective-permute-start | bytes 2248712 | tf_op jit(solution)/shard_map/ppermute | solution.py:386
  43.1 37.3 %collective-permute-start.3 = (bf16[976,384]{1,0:T(8,128)(2,1)}, bf16[976,384]{1,0:T(8,128)(2,1)}, u32[]{:S(2)}, u32[]{:S(2)}) collective-permute-start(bf16[976,384]{1,0:T(8,128)(2,1)} %get-tuple-element.38), channel_id=1, source_target_pairs={{0,192},{1,193},{2,194},{3,195},{4,196},{5,197},{6,198},{7,199},{8... | collective-permute-start | bytes 2248712 | tf_op jit(solution)/shard_map/ppermute | solution.py:386
  48.2 34.4 %collective-permute-start.4 = (bf16[976,384]{1,0:T(8,128)(2,1)}, bf16[976,384]{1,0:T(8,128)(2,1)}, u32[]{:S(2)}, u32[]{:S(2)}) collective-permute-start(bf16[976,384]{1,0:T(8,128)(2,1)} %get-tuple-element.39), channel_id=1, source_target_pairs={{0,64},{1,65},{2,66},{3,67},{4,68},{5,69},{6,70},{7,71},{8,72},{9,... | collective-permute-start | bytes 2248712 | tf_op jit(solution)/shard_map/ppermute | solution.py:386
  50.4 48.3 %collective-permute-start = (bf16[976,384]{1,0:T(8,128)(2,1)}, bf16[976,384]{1,0:T(8,128)(2,1)}, u32[]{:S(2)}, u32[]{:S(2)}) collective-permute-start(bf16[976,384]{1,0:T(8,128)(2,1)} %get-tuple-element.40), channel_id=1, source_target_pairs={{0,128},{1,129},{2,130},{3,131},{4,132},{5,133},{6,134},{7,135},{8... | collective-permute-start | bytes 2248712 | tf_op jit(solution)/shard_map/ppermute | solution.py:386
  66.6 32.1 %copy-start.14 = (bf16[976,384]{1,0:T(8,128)(2,1)}, bf16[976,384]{1,0:T(8,128)(2,1)S(1)}, u32[]{:S(2)}) copy-start(bf16[976,384]{1,0:T(8,128)(2,1)S(1)} %collective-permute-done.2) | copy-start | bytes 2248708
  99.5 23.3 %collective-permute-start.7 = (bf16[976,384]{1,0:T(8,128)(2,1)S(1)}, bf16[976,384]{1,0:T(8,128)(2,1)S(1)}, u32[]{:S(2)}, u32[]{:S(2)}) collective-permute-start(bf16[976,384]{1,0:T(8,128)(2,1)S(1)} %fusion.6), channel_id=1, source_target_pairs={{0,16},{32,48},{64,80},{96,112},{128,144},{160,176},{192,208},{224... | collective-permute-start | bytes 2248712 | tf_op jit(solution)/shard_map/ppermute | solution.py:411
  127.1 32.5 %all-to-all-start.1 = ((bf16[8,2,64,384]{3,2,1,0:T(8,128)(2,1)}), bf16[8,2,64,384]{3,2,1,0:T(8,128)(2,1)S(1)}, u32[]{:S(2)}, u32[]{:S(2)}) async-start(bf16[8,2,64,384]{3,2,1,0:T(8,128)(2,1)} %forward_transform.3), calls=%async_computation.1 | async-start | bytes 1572864 | tf_op jit(solution)/shard_map/all_to_all | solution.py:394
  161.2 20.3 %all-to-all-start.2 = ((bf16[16,15,4,384]{3,2,1,0:T(4,128)(2,1)}), bf16[16,15,4,384]{3,2,1,0:T(4,128)(2,1)S(1)}, u32[]{:S(2)}, u32[]{:S(2)}) async-start(bf16[16,15,4,384]{3,2,1,0:T(4,128)(2,1)} %slice.58), calls=%async_computation.2 | async-start | bytes 1474560 | tf_op jit(solution)/shard_map/all_to_all | solution.py:472
  209.5 86.0 %all-to-all-start.4 = ((bf16[16,15,32,384]{3,2,1,0:T(8,128)(2,1)}), bf16[16,15,32,384]{3,2,1,0:T(8,128)(2,1)}, u32[]{:S(2)}, u32[]{:S(2)}) async-start(bf16[16,15,32,384]{3,2,1,0:T(8,128)(2,1)} %bitcast.79), calls=%async_computation.4 | async-start | bytes 11796480 | tf_op jit(solution)/shard_map/all_to_all | solution.py:488
  214.7 101.7 %all-gather.2.cloned.1.call-start = ((), (), s32[]{:S(2)}) async-start(), calls=%async_computation.6 | async-start | bytes 6635520 | tf_op jit(solution)/shard_map/all_gather | solution.py:495
  215.7 24.3 %copy-start.7 = (bf16[960,384]{1,0:T(8,128)(2,1)S(1)}, bf16[960,384]{1,0:T(8,128)(2,1)}, u32[]{:S(2)}) copy-start(bf16[960,384]{1,0:T(8,128)(2,1)} %slice.57) | copy-start | bytes 2211844
  215.8 5.5 %collective-permute-start.8 = (bf16[2,64,384]{2,1,0:T(8,128)(2,1)S(1)}, bf16[2,64,384]{2,1,0:T(8,128)(2,1)S(1)}, u32[]{:S(2)}, u32[]{:S(2)}) collective-permute-start(bf16[2,64,384]{2,1,0:T(8,128)(2,1)S(1)} %dynamic-slice_bitcast_fusion.6), channel_id=1, source_target_pairs={{0,32},{32,64},{64,96},{96,128},{128,160},{160,192},{192,224},{224... | collective-permute-start | bytes 294920 | tf_op jit(solution)/shard_map/ppermute | solution.py:405
  221.4 9.3 %collective-permute-start.9 = (bf16[2,64,384]{2,1,0:T(8,128)(2,1)S(1)}, bf16[2,64,384]{2,1,0:T(8,128)(2,1)S(1)}, u32[]{:S(2)}, u32[]{:S(2)}) collective-permute-start(bf16[2,64,384]{2,1,0:T(8,128)(2,1)S(1)} %get-tuple-element.33), channel_id=1, source_target_pairs={{0,224},{32,0},{64,32},{96,64},{128,96},{160,128},{192,160},{224,1... | collective-permute-start | bytes 294920 | tf_op jit(solution)/shard_map/ppermute | solution.py:405
  222.4 17.6 %collective-permute-start.14 = (bf16[2,64,384]{2,1,0:T(8,128)(2,1)S(1)}, bf16[2,64,384]{2,1,0:T(8,128)(2,1)S(1)}, u32[]{:S(2)}, u32[]{:S(2)}) collective-permute-start(bf16[2,64,384]{2,1,0:T(8,128)(2,1)S(1)} %get-tuple-element.28), channel_id=1, source_target_pairs={{0,128},{32,160},{64,192},{96,224},{128,0},{160,32},{192,64},{224,... | collective-permute-start | bytes 294920 | tf_op jit(solution)/shard_map/ppermute | solution.py:405
  226.1 13.9 %collective-permute-start.13 = (bf16[2,64,384]{2,1,0:T(8,128)(2,1)S(1)}, bf16[2,64,384]{2,1,0:T(8,128)(2,1)S(1)}, u32[]{:S(2)}, u32[]{:S(2)}) collective-permute-start(bf16[2,64,384]{2,1,0:T(8,128)(2,1)S(1)} %get-tuple-element.29), channel_id=1, source_target_pairs={{0,160},{32,192},{64,224},{96,0},{128,32},{160,64},{192,96},{224,1... | collective-permute-start | bytes 294920 | tf_op jit(solution)/shard_map/ppermute | solution.py:405
  228.1 11.9 %collective-permute-start.12 = (bf16[2,64,384]{2,1,0:T(8,128)(2,1)S(1)}, bf16[2,64,384]{2,1,0:T(8,128)(2,1)S(1)}, u32[]{:S(2)}, u32[]{:S(2)}) collective-permute-start(bf16[2,64,384]{2,1,0:T(8,128)(2,1)S(1)} %get-tuple-element.30), channel_id=1, source_target_pairs={{0,96},{32,128},{64,160},{96,192},{128,224},{160,0},{192,32},{224,... | collective-permute-start | bytes 294920 | tf_op jit(solution)/shard_map/ppermute | solution.py:405
  229.3 10.6 %collective-permute-start.11 = (bf16[2,64,384]{2,1,0:T(8,128)(2,1)S(1)}, bf16[2,64,384]{2,1,0:T(8,128)(2,1)S(1)}, u32[]{:S(2)}, u32[]{:S(2)}) collective-permute-start(bf16[2,64,384]{2,1,0:T(8,128)(2,1)S(1)} %get-tuple-element.31), channel_id=1, source_target_pairs={{0,192},{32,224},{64,0},{96,32},{128,64},{160,96},{192,128},{224,1... | collective-permute-start | bytes 294920 | tf_op jit(solution)/shard_map/ppermute | solution.py:405
  230.7 9.2 %collective-permute-start.10 = (bf16[2,64,384]{2,1,0:T(8,128)(2,1)S(1)}, bf16[2,64,384]{2,1,0:T(8,128)(2,1)S(1)}, u32[]{:S(2)}, u32[]{:S(2)}) collective-permute-start(bf16[2,64,384]{2,1,0:T(8,128)(2,1)S(1)} %get-tuple-element.32), channel_id=1, source_target_pairs={{0,64},{32,96},{64,128},{96,160},{128,192},{160,224},{192,0},{224,... | collective-permute-start | bytes 294920 | tf_op jit(solution)/shard_map/ppermute | solution.py:405
  240.1 55.4 %copy-start.12 = (bf16[480,512]{1,0:T(8,128)(2,1)S(1)}, bf16[480,512]{1,0:T(8,128)(2,1)}, u32[]{:S(2)}) copy-start(bf16[480,512]{1,0:T(8,128)(2,1)} %constant.203.table_ref) | copy-start | bytes 1474564
  325.4 11.7 %all-to-all-start.5 = ((f32[16,8,128]{2,1,0:T(8,128)}), f32[16,8,128]{2,1,0:T(8,128)S(1)}, u32[]{:S(2)}, u32[]{:S(2)}) async-start(f32[16,8,128]{2,1,0:T(8,128)} %spread_sums.1), calls=%async_computation.5 | async-start | bytes 131072 | tf_op jit(solution)/shard_map/all_to_all | solution.py:498
  (15 other events, 130.8 us)
Sparse Core Ops, SparseCore 0:
  242.0 74.2 all-gather.1

commit v6 on v5

--- a/solution.py
+++ b/solution.py
@@ -188,7 +188,7 @@
             out_specs=[row(0), row(0)],
         ),
         out_shape=[pair, pair],
-        compiler_params=pltpu.CompilerParams(vmem_limit_bytes=16 * MIB),
+        compiler_params=pltpu.CompilerParams(vmem_limit_bytes=58 * MIB),
         cost_estimate=pl.CostEstimate(flops=1 << 30, bytes_accessed=4 << 20, transcendentals=0),
         name="shared_spectral_pass",
     )(place, moved, moved, legendre, gain, mixing)
@@ -295,7 +295,7 @@
         ],
         out_specs=pl.BlockSpec((step, W, E), lambda j: (j, 0, 0)),
         out_shape=jax.ShapeDtypeStruct((rows, W, E), jnp.bfloat16),
-        compiler_params=pltpu.CompilerParams(vmem_limit_bytes=18 * MIB),
+        compiler_params=pltpu.CompilerParams(vmem_limit_bytes=58 * MIB),
         cost_estimate=pl.CostEstimate(
             flops=flops, bytes_accessed=rows << 20, transcendentals=rows * W * E
         ),
@@ -335,7 +335,7 @@
         out_specs=pl.BlockSpec((BANDS, 8, 128), lambda j: (0, 0, 0)),
         out_shape=jax.ShapeDtypeStruct((BANDS, 8, 128), jnp.float32),
         scratch_shapes=[pltpu.VMEM((8, E), jnp.float32)],
-        compiler_params=pltpu.CompilerParams(vmem_limit_bytes=12 * MIB),
+        compiler_params=pltpu.CompilerParams(vmem_limit_bytes=58 * MIB),
         cost_estimate=pl.CostEstimate(flops=9 << 20, bytes_accessed=11 << 20, transcendentals=0),
         name="spread_sums",
     )(weights, own, control)
@@ -364,7 +364,7 @@
         ],
         out_specs=row,
         out_shape=jax.ShapeDtypeStruct((ROWS, W, E), jnp.bfloat16),
-        compiler_params=pltpu.CompilerParams(vmem_limit_bytes=14 * MIB),
+        compiler_params=pltpu.CompilerParams(vmem_limit_bytes=58 * MIB),
         cost_estimate=pl.CostEstimate(flops=9 << 20, bytes_accessed=17 << 20, transcendentals=0),
         name="rescaled",
     )(target, sums, own, control)

time: 356 us -> 351 us (0.986)
  local copies, waits for them, and re-layouts: 35.9 us -> 14 us
  Pallas kernels: 52.9 us -> 67.5 us
    unnamed x36 -> x16, local copies, waits for them, and re-layouts: 25 us -> 1.54 us
    all_gather x1, waiting for transfers between devices: 8.01 us -> 12.5 us  [shards(): lax.all_gather(control, 'member', tiled=True, axis_index_groups=RINGS)]
    pallas_call x2, Pallas kernels: 9.58 us -> 14 us  [inverse_transform(): pl.pallas_call(inverse_kernel, grid=(rows // step,), in_specs=[pl.BlockSp...]
    pallas_call x1, Pallas kernels: 5.53 us -> 9.92 us  [rescaled(): pl.pallas_call(rescale_kernel, grid=(ROWS // STEP,), in_specs=[scalars, p...]
  transfers between devices with their start and end apart: 21 -> 21, of which waited for: 14 -> 14; matrix products, arithmetic and copies ran while one was open for 4% -> 4% of each run, Pallas kernels for 9% -> 10%
where the time goes in v6:
time: 351 us; the launch traced here: 350 us
  waiting for transfers between devices  166 us (47%)
  Pallas kernels  67.5 us (19%)
  starting transfers between devices  63.7 us (18%)
  blocking collectives  15.8 us (5%)
  between operations  15.7 us (4%)
  local copies, waits for them, and re-layouts  14 us (4%)
  other arithmetic  7.21 us (2%)
    all_to_all x1, waiting for transfers between devices, shards(): lax.all_to_all(returned.reshape(BANDS, ROWS, SLOTS, E), 'band', split_axi...  51.2 us
    ppermute x7, waiting for transfers between devices, scattered(): lax.ppermute(jnp.concatenate([piece, extra]), 'member', [(0, 2 * z)])  49 us
    ppermute x1, waiting for transfers between devices, across(): lax.ppermute(value, 'member', [(2 * z, 2 * z + 1) for z in range(DEPTH)])  21.3 us
    pallas_call x1, Pallas kernels, spectral_pass(): pl.pallas_call(spectral_kernel, grid_spec=pltpu.PrefetchScalarGridSpec(nu...  18.8 us
    ppermute x7, starting transfers between devices, scattered(): lax.ppermute(jnp.concatenate([piece, extra]), 'member', [(0, 2 * z)])  17 us
    all_to_all x1, blocking collectives, shards(): lax.all_to_all(control_spatial.transpose(1, 0, 2).reshape(BANDS, ROWS, 4,...  15.8 us
    pallas_call x2, Pallas kernels, inverse_transform(): pl.pallas_call(inverse_kernel, grid=(rows // step,), in_specs=[pl.BlockSp...  14 us
    ppermute x7, waiting for transfers between devices, permuted_along_z(): arrived = lax.ppermute(block, 'member', pairs)  13.3 us
  transfers between devices with their start and end apart: 21, of which 14 were waited for; matrix products, arithmetic and copies ran while one was open for 4% of the time, Pallas kernels for 10%

profile of v6, /device:TPU:1, one launch (start us, length us, event | category | flops | bytes accessed | tf_op | source)
XLA Modules:
  0.0 349.7 jit_solution(4182771816774928553)
XLA Ops:
  8.4 9.7 %forward_transform.2 = bf16[16,15,32,384]{3,2,1,0:T(8,128)(2,1)} custom-call(f32[15]{0:T(128)} %sine_multiply_fusion.weights_ref, bf16[15,480,384]{2,1,0:T(8,128)(2,1)} %bitcast.76, f32[1,384]{1,0:T(1,128)} %broadcast_in_dim.43.gain_ref, bf16[512,480]{1,0:T(8,128)(2,1)} %constant.199.table_ref), custom_call_target="tpu_custom_call" | custom-call | flops 137438953472 | bytes 15728640 | tf_op jit(solution)/shard_map/forward_transform/pallas_call | solution.py:131
  18.1 7.7 %all-to-all-start = ((bf16[16,15,32,384]{3,2,1,0:T(8,128)(2,1)}), bf16[16,15,32,384]{3,2,1,0:T(8,128)(2,1)}, u32[]{:S(2)}, u32[]{:S(2)}) async-start(bf16[16,15,32,384]{3,2,1,0:T(8,128)(2,1)} %forward_transform.2), calls=%async_computation | async-start | bytes 11796480 | tf_op jit(solution)/shard_map/all_to_all | solution.py:449
  35.5 4.6 %collective-permute-start.5 = (bf16[496,384]{1,0:T(8,128)(2,1)S(1)}, bf16[496,384]{1,0:T(8,128)(2,1)S(1)}, u32[]{:S(2)}, u32[]{:S(2)}) collective-permute-start(bf16[496,384]{1,0:T(8,128)(2,1)S(1)} %pad_maximum_fusion.7), channel_id=1, source_target_pairs={{0,224},{1,225},{2,226},{3,227},{4,228},{5,229},{6,230},{7,231},{8... | collective-permute-start | bytes 1142792 | tf_op jit(solution)/shard_map/ppermute | solution.py:386
  52.6 11.8 %collective-permute-done.1 = bf16[976,384]{1,0:T(8,128)(2,1)S(1)} collective-permute-done((bf16[976,384]{1,0:T(8,128)(2,1)}, bf16[976,384]{1,0:T(8,128)(2,1)S(1)}, u32[]{:S(2)}, u32[]{:S(2)}) %collective-permute-start.1) | collective-permute-done | bytes 749600 | tf_op jit(solution)/shard_map/ppermute | solution.py:386
  66.5 13.9 %collective-permute-done.3 = bf16[976,384]{1,0:T(8,128)(2,1)} collective-permute-done((bf16[976,384]{1,0:T(8,128)(2,1)}, bf16[976,384]{1,0:T(8,128)(2,1)}, u32[]{:S(2)}, u32[]{:S(2)}) %collective-permute-start.3) | collective-permute-done | bytes 749600 | tf_op jit(solution)/shard_map/ppermute | solution.py:386
  82.6 16.1 %collective-permute-done = bf16[976,384]{1,0:T(8,128)(2,1)} collective-permute-done((bf16[976,384]{1,0:T(8,128)(2,1)}, bf16[976,384]{1,0:T(8,128)(2,1)}, u32[]{:S(2)}, u32[]{:S(2)}) %collective-permute-start) | collective-permute-done | bytes 749600 | tf_op jit(solution)/shard_map/ppermute | solution.py:386
  101.5 21.3 %collective-permute-done.7 = bf16[976,384]{1,0:T(8,128)(2,1)S(1)} collective-permute-done((bf16[976,384]{1,0:T(8,128)(2,1)S(1)}, bf16[976,384]{1,0:T(8,128)(2,1)S(1)}, u32[]{:S(2)}, u32[]{:S(2)}) %collective-permute-start.7) | collective-permute-done | bytes 749600 | tf_op jit(solution)/shard_map/ppermute | solution.py:411
  127.0 8.9 %all-to-all-start.1 = ((bf16[8,2,64,384]{3,2,1,0:T(8,128)(2,1)}), bf16[8,2,64,384]{3,2,1,0:T(8,128)(2,1)S(1)}, u32[]{:S(2)}, u32[]{:S(2)}) async-start(bf16[8,2,64,384]{3,2,1,0:T(8,128)(2,1)} %forward_transform.3), calls=%async_computation.1 | async-start | bytes 1572864 | tf_op jit(solution)/shard_map/all_to_all | solution.py:394
  137.9 18.8 %spectral_pass.1 = bf16[240,32,384]{2,1,0:T(8,128)(2,1)} custom-call(s32[1]{0:T(128)} %bitcast.2.band_ref, bf16[240,32,384]{2,1,0:T(8,128)(2,1)} %bitcast.18.moved_ref, bf16[16,15,240,240]{3,2,1,0:T(8,128)(2,1)} %constant.201.legendre_ref, f32[240,1]{1,0:T(8,128)} %copy.23.gain_ref, bf16[768,768]{1,0:T(8,128)(2,1)} %maximum_maximum_fusion.mixing_ref, ...), custom_call_target="tpu_custom_call" | custom-call | flops 8589934592 | bytes 14680064 | tf_op jit(solution)/shard_map/spectral_pass/pallas_call | solution.py:253
  161.2 7.7 %all-to-all-start.2 = ((bf16[16,15,4,384]{3,2,1,0:T(4,128)(2,1)}), bf16[16,15,4,384]{3,2,1,0:T(4,128)(2,1)S(1)}, u32[]{:S(2)}, u32[]{:S(2)}) async-start(bf16[16,15,4,384]{3,2,1,0:T(4,128)(2,1)} %slice.58), calls=%async_computation.2 | async-start | bytes 1474560 | tf_op jit(solution)/shard_map/all_to_all | solution.py:472
  170.3 11.0 %all-to-all-done.2 = bf16[16,15,4,384]{3,2,1,0:T(4,128)(2,1)S(1)} async-done(((bf16[16,15,4,384]{3,2,1,0:T(4,128)(2,1)}), bf16[16,15,4,384]{3,2,1,0:T(4,128)(2,1)S(1)}, u32[]{:S(2)}, u32[]{:S(2)}) %all-to-all-start.2) | async-done | bytes 737312 | tf_op jit(solution)/shard_map/all_to_all | solution.py:472
  182.3 4.8 %shared_spectral_pass.1 = (bf16[2,240,384]{2,1,0:T(8,128)(2,1)}, bf16[2,240,384]{2,1,0:T(8,128)(2,1)}) custom-call(s32[2]{0:T(128)} %pad_add_fusion.place_ref, bf16[4,240,384]{2,1,0:T(8,128)(2,1)} %bitcast.74, bf16[4,240,384]{2,1,0:T(8,128)(2,1)} %bitcast.75, bf16[16,15,240,240]{3,2,1,0:T(8,128)(2,1)} %constant.201.legendre_ref, f32[240,1]{1,0:T(8,128)} %copy.26.gain_ref, ...), custom_call_target="tpu_custom_call" | custom-call | flops 1073741824 | bytes 4194304 | tf_op jit(solution)/shard_map/shared_spectral_pass/pallas_call | solution.py:173
  188.5 15.8 %all_to_all.30 = bf16[16,15,4,384]{3,2,1,0:T(4,128)(2,1)S(1)} all-to-all(bf16[16,15,4,384]{3,2,1,0:T(4,128)(2,1)S(1)} %bitcast.86), channel_id=1, replica_groups=mesh['member'=16,'band'=16] {'band'}, dimensions={0} | all-to-all | bytes 1474560 | tf_op jit(solution)/shard_map/all_to_all | solution.py:480
  204.3 5.2 %all-to-all-start.4 = ((bf16[16,15,32,384]{3,2,1,0:T(8,128)(2,1)}), bf16[16,15,32,384]{3,2,1,0:T(8,128)(2,1)}, u32[]{:S(2)}, u32[]{:S(2)}) async-start(bf16[16,15,32,384]{3,2,1,0:T(8,128)(2,1)} %bitcast.71), calls=%async_computation.4 | async-start | bytes 11796480 | tf_op jit(solution)/shard_map/all_to_all | solution.py:488
  210.9 5.1 %collective-permute-done.8 = bf16[2,64,384]{2,1,0:T(8,128)(2,1)S(1)} collective-permute-done((bf16[2,64,384]{2,1,0:T(8,128)(2,1)S(1)}, bf16[2,64,384]{2,1,0:T(8,128)(2,1)S(1)}, u32[]{:S(2)}, u32[]{:S(2)}) %collective-permute-start.8) | collective-permute-done | bytes 98336 | tf_op jit(solution)/shard_map/ppermute | solution.py:405
  217.2 3.6 %collective-permute-start.14 = (bf16[2,64,384]{2,1,0:T(8,128)(2,1)S(1)}, bf16[2,64,384]{2,1,0:T(8,128)(2,1)S(1)}, u32[]{:S(2)}, u32[]{:S(2)}) collective-permute-start(bf16[2,64,384]{2,1,0:T(8,128)(2,1)S(1)} %get-tuple-element.28), channel_id=1, source_target_pairs={{0,128},{32,160},{64,192},{96,224},{128,0},{160,32},{192,64},{224,... | collective-permute-start | bytes 294920 | tf_op jit(solution)/shard_map/ppermute | solution.py:405
  226.5 8.1 %collective-permute-done.10 = bf16[2,64,384]{2,1,0:T(8,128)(2,1)S(1)} collective-permute-done((bf16[2,64,384]{2,1,0:T(8,128)(2,1)S(1)}, bf16[2,64,384]{2,1,0:T(8,128)(2,1)S(1)}, u32[]{:S(2)}, u32[]{:S(2)}) %collective-permute-start.10) | collective-permute-done | bytes 98336 | tf_op jit(solution)/shard_map/ppermute | solution.py:405
  239.1 51.2 %all-to-all-done.4.spatial_ref = bf16[16,15,32,384]{3,2,1,0:T(8,128)(2,1)} async-done(((bf16[16,15,32,384]{3,2,1,0:T(8,128)(2,1)}), bf16[16,15,32,384]{3,2,1,0:T(8,128)(2,1)}, u32[]{:S(2)}, u32[]{:S(2)}) %all-to-all-start.4) | async-done | bytes 5898272 | tf_op jit(solution)/shard_map/all_to_all | solution.py:488
  290.3 10.7 %inverse_transform.2.own_ref = bf16[15,480,384]{2,1,0:T(8,128)(2,1)} custom-call(bf16[16,15,32,384]{3,2,1,0:T(8,128)(2,1)} %all-to-all-done.4.spatial_ref, bf16[15,480,384]{2,1,0:T(8,128)(2,1)} %bitcast.79, bf16[480,512]{1,0:T(8,128)(2,1)} %constant.203.table_ref), custom_call_target="tpu_custom_call" | custom-call | flops 274877906944 | bytes 15728640 | tf_op jit(solution)/shard_map/inverse_transform/pallas_call | solution.py:288
  301.0 12.5 %all-gather.2.cloned.1.call-done.control_ref = bf16[16,480,384]{2,1,0:T(8,128)(2,1)} async-done(((bf16[2,480,384]{2,1,0:T(8,128)(2,1)}), bf16[16,480,384]{2,1,0:T(8,128)(2,1)}) %all-gather.2.cloned.1.call-update) | async-done | bytes 5898256 | tf_op jit(solution)/shard_map/all_gather | solution.py:495
  313.5 7.0 %spread_sums.1 = f32[16,8,128]{2,1,0:T(8,128)} custom-call(f32[15]{0:T(128)} %sine_multiply_fusion.weights_ref, bf16[15,480,384]{2,1,0:T(8,128)(2,1)} %inverse_transform.2.own_ref, bf16[16,480,384]{2,1,0:T(8,128)(2,1)} %all-gather.2.cloned.1.call-done.control_ref), custom_call_target="tpu_custom_call" | custom-call | flops 9437184 | bytes 11534336 | tf_op jit(solution)/shard_map/spread_sums/pallas_call | solution.py:331
  320.5 5.9 %all-to-all-start.5 = ((f32[16,8,128]{2,1,0:T(8,128)}), f32[16,8,128]{2,1,0:T(8,128)S(1)}, u32[]{:S(2)}, u32[]{:S(2)}) async-start(f32[16,8,128]{2,1,0:T(8,128)} %spread_sums.1), calls=%async_computation.5 | async-start | bytes 131072 | tf_op jit(solution)/shard_map/all_to_all | solution.py:498
  327.6 4.6 %all-to-all-done.5.sums_ref = f32[16,8,128]{2,1,0:T(8,128)S(1)} async-done(((f32[16,8,128]{2,1,0:T(8,128)}), f32[16,8,128]{2,1,0:T(8,128)S(1)}, u32[]{:S(2)}, u32[]{:S(2)}) %all-to-all-start.5) | async-done | bytes 65568 | tf_op jit(solution)/shard_map/all_to_all | solution.py:498
  332.9 9.9 %rescaled.1 = bf16[15,480,384]{2,1,0:T(8,128)(2,1)} custom-call(f32[1]{0:T(128)} %bitcast.1.target_ref, f32[16,8,128]{2,1,0:T(8,128)} %copy-done.4, bf16[15,480,384]{2,1,0:T(8,128)(2,1)} %inverse_transform.2.own_ref, bf16[16,480,384]{2,1,0:T(8,128)(2,1)} %all-gather.2.cloned.1.call-done.control_ref), custom_call_target="tpu_custom_call" | custom-call | flops 9437184 | bytes 17825792 | tf_op jit(solution)/shard_map/rescaled/pallas_call | solution.py:356
  (83 shorter events, 57.8 us)
Async XLA Ops:
  18.1 109.0 %all-to-all-start = ((bf16[16,15,32,384]{3,2,1,0:T(8,128)(2,1)}), bf16[16,15,32,384]{3,2,1,0:T(8,128)(2,1)}, u32[]{:S(2)}, u32[]{:S(2)}) async-start(bf16[16,15,32,384]{3,2,1,0:T(8,128)(2,1)} %forward_transform.2), calls=%async_computation | async-start | bytes 11796480 | tf_op jit(solution)/shard_map/all_to_all | solution.py:449
  31.5 18.9 %collective-permute-start.6 = (bf16[976,384]{1,0:T(8,128)(2,1)S(1)}, bf16[976,384]{1,0:T(8,128)(2,1)S(1)}, u32[]{:S(2)}, u32[]{:S(2)}) collective-permute-start(bf16[976,384]{1,0:T(8,128)(2,1)S(1)} %get-tuple-element.35), channel_id=1, source_target_pairs={{0,32},{1,33},{2,34},{3,35},{4,36},{5,37},{6,38},{7,39},{8,40},{9,... | collective-permute-start | bytes 2248712 | tf_op jit(solution)/shard_map/ppermute | solution.py:386
  35.5 12.7 %collective-permute-start.5 = (bf16[496,384]{1,0:T(8,128)(2,1)S(1)}, bf16[496,384]{1,0:T(8,128)(2,1)S(1)}, u32[]{:S(2)}, u32[]{:S(2)}) collective-permute-start(bf16[496,384]{1,0:T(8,128)(2,1)S(1)} %pad_maximum_fusion.7), channel_id=1, source_target_pairs={{0,224},{1,225},{2,226},{3,227},{4,228},{5,229},{6,230},{7,231},{8... | collective-permute-start | bytes 1142792 | tf_op jit(solution)/shard_map/ppermute | solution.py:386
  40.2 24.2 %collective-permute-start.1 = (bf16[976,384]{1,0:T(8,128)(2,1)}, bf16[976,384]{1,0:T(8,128)(2,1)S(1)}, u32[]{:S(2)}, u32[]{:S(2)}) collective-permute-start(bf16[976,384]{1,0:T(8,128)(2,1)} %get-tuple-element.36), channel_id=1, source_target_pairs={{0,160},{1,161},{2,162},{3,163},{4,164},{5,165},{6,166},{7,167},{8... | collective-permute-start | bytes 2248712 | tf_op jit(solution)/shard_map/ppermute | solution.py:386
  41.8 24.8 %collective-permute-start.2 = (bf16[976,384]{1,0:T(8,128)(2,1)}, bf16[976,384]{1,0:T(8,128)(2,1)S(1)}, u32[]{:S(2)}, u32[]{:S(2)}) collective-permute-start(bf16[976,384]{1,0:T(8,128)(2,1)} %get-tuple-element.37), channel_id=1, source_target_pairs={{0,96},{1,97},{2,98},{3,99},{4,100},{5,101},{6,102},{7,103},{8,104... | collective-permute-start | bytes 2248712 | tf_op jit(solution)/shard_map/ppermute | solution.py:386
  43.1 37.4 %collective-permute-start.3 = (bf16[976,384]{1,0:T(8,128)(2,1)}, bf16[976,384]{1,0:T(8,128)(2,1)}, u32[]{:S(2)}, u32[]{:S(2)}) collective-permute-start(bf16[976,384]{1,0:T(8,128)(2,1)} %get-tuple-element.38), channel_id=1, source_target_pairs={{0,192},{1,193},{2,194},{3,195},{4,196},{5,197},{6,198},{7,199},{8... | collective-permute-start | bytes 2248712 | tf_op jit(solution)/shard_map/ppermute | solution.py:386
  48.2 34.4 %collective-permute-start.4 = (bf16[976,384]{1,0:T(8,128)(2,1)}, bf16[976,384]{1,0:T(8,128)(2,1)}, u32[]{:S(2)}, u32[]{:S(2)}) collective-permute-start(bf16[976,384]{1,0:T(8,128)(2,1)} %get-tuple-element.39), channel_id=1, source_target_pairs={{0,64},{1,65},{2,66},{3,67},{4,68},{5,69},{6,70},{7,71},{8,72},{9,... | collective-permute-start | bytes 2248712 | tf_op jit(solution)/shard_map/ppermute | solution.py:386
  50.4 48.3 %collective-permute-start = (bf16[976,384]{1,0:T(8,128)(2,1)}, bf16[976,384]{1,0:T(8,128)(2,1)}, u32[]{:S(2)}, u32[]{:S(2)}) collective-permute-start(bf16[976,384]{1,0:T(8,128)(2,1)} %get-tuple-element.40), channel_id=1, source_target_pairs={{0,128},{1,129},{2,130},{3,131},{4,132},{5,133},{6,134},{7,135},{8... | collective-permute-start | bytes 2248712 | tf_op jit(solution)/shard_map/ppermute | solution.py:386
  66.5 32.1 %copy-start.2 = (bf16[976,384]{1,0:T(8,128)(2,1)}, bf16[976,384]{1,0:T(8,128)(2,1)S(1)}, u32[]{:S(2)}) copy-start(bf16[976,384]{1,0:T(8,128)(2,1)S(1)} %collective-permute-done.2) | copy-start | bytes 2248708
  99.5 23.3 %collective-permute-start.7 = (bf16[976,384]{1,0:T(8,128)(2,1)S(1)}, bf16[976,384]{1,0:T(8,128)(2,1)S(1)}, u32[]{:S(2)}, u32[]{:S(2)}) collective-permute-start(bf16[976,384]{1,0:T(8,128)(2,1)S(1)} %fusion.6), channel_id=1, source_target_pairs={{0,16},{32,48},{64,80},{96,112},{128,144},{160,176},{192,208},{224... | collective-permute-start | bytes 2248712 | tf_op jit(solution)/shard_map/ppermute | solution.py:411
  123.8 12.9 %copy-start.1 = (bf16[384,384]{1,0:T(8,128)(2,1)S(1)}, bf16[384,384]{1,0:T(8,128)(2,1)}, u32[]{:S(2)}) copy-start(bf16[384,384]{1,0:T(8,128)(2,1)} %param.17) | copy-start | bytes 884740
  127.0 32.5 %all-to-all-start.1 = ((bf16[8,2,64,384]{3,2,1,0:T(8,128)(2,1)}), bf16[8,2,64,384]{3,2,1,0:T(8,128)(2,1)S(1)}, u32[]{:S(2)}, u32[]{:S(2)}) async-start(bf16[8,2,64,384]{3,2,1,0:T(8,128)(2,1)} %forward_transform.3), calls=%async_computation.1 | async-start | bytes 1572864 | tf_op jit(solution)/shard_map/all_to_all | solution.py:394
  161.2 20.1 %all-to-all-start.2 = ((bf16[16,15,4,384]{3,2,1,0:T(4,128)(2,1)}), bf16[16,15,4,384]{3,2,1,0:T(4,128)(2,1)S(1)}, u32[]{:S(2)}, u32[]{:S(2)}) async-start(bf16[16,15,4,384]{3,2,1,0:T(4,128)(2,1)} %slice.58), calls=%async_computation.2 | async-start | bytes 1474560 | tf_op jit(solution)/shard_map/all_to_all | solution.py:472
  204.3 86.0 %all-to-all-start.4 = ((bf16[16,15,32,384]{3,2,1,0:T(8,128)(2,1)}), bf16[16,15,32,384]{3,2,1,0:T(8,128)(2,1)}, u32[]{:S(2)}, u32[]{:S(2)}) async-start(bf16[16,15,32,384]{3,2,1,0:T(8,128)(2,1)} %bitcast.71), calls=%async_computation.4 | async-start | bytes 11796480 | tf_op jit(solution)/shard_map/all_to_all | solution.py:488
  209.5 104.0 %all-gather.2.cloned.1.call-start = ((), (), s32[]{:S(2)}) async-start(), calls=%async_computation.6 | async-start | bytes 6635520 | tf_op jit(solution)/shard_map/all_gather | solution.py:495
  210.5 5.5 %collective-permute-start.8 = (bf16[2,64,384]{2,1,0:T(8,128)(2,1)S(1)}, bf16[2,64,384]{2,1,0:T(8,128)(2,1)S(1)}, u32[]{:S(2)}, u32[]{:S(2)}) collective-permute-start(bf16[2,64,384]{2,1,0:T(8,128)(2,1)S(1)} %dynamic-slice_bitcast_fusion.6), channel_id=1, source_target_pairs={{0,32},{32,64},{64,96},{96,128},{128,160},{160,192},{192,224},{224... | collective-permute-start | bytes 294920 | tf_op jit(solution)/shard_map/ppermute | solution.py:405
  216.2 9.4 %collective-permute-start.9 = (bf16[2,64,384]{2,1,0:T(8,128)(2,1)S(1)}, bf16[2,64,384]{2,1,0:T(8,128)(2,1)S(1)}, u32[]{:S(2)}, u32[]{:S(2)}) collective-permute-start(bf16[2,64,384]{2,1,0:T(8,128)(2,1)S(1)} %get-tuple-element.33), channel_id=1, source_target_pairs={{0,224},{32,0},{64,32},{96,64},{128,96},{160,128},{192,160},{224,1... | collective-permute-start | bytes 294920 | tf_op jit(solution)/shard_map/ppermute | solution.py:405
  217.2 17.6 %collective-permute-start.14 = (bf16[2,64,384]{2,1,0:T(8,128)(2,1)S(1)}, bf16[2,64,384]{2,1,0:T(8,128)(2,1)S(1)}, u32[]{:S(2)}, u32[]{:S(2)}) collective-permute-start(bf16[2,64,384]{2,1,0:T(8,128)(2,1)S(1)} %get-tuple-element.28), channel_id=1, source_target_pairs={{0,128},{32,160},{64,192},{96,224},{128,0},{160,32},{192,64},{224,... | collective-permute-start | bytes 294920 | tf_op jit(solution)/shard_map/ppermute | solution.py:405
  220.9 13.9 %collective-permute-start.13 = (bf16[2,64,384]{2,1,0:T(8,128)(2,1)S(1)}, bf16[2,64,384]{2,1,0:T(8,128)(2,1)S(1)}, u32[]{:S(2)}, u32[]{:S(2)}) collective-permute-start(bf16[2,64,384]{2,1,0:T(8,128)(2,1)S(1)} %get-tuple-element.29), channel_id=1, source_target_pairs={{0,160},{32,192},{64,224},{96,0},{128,32},{160,64},{192,96},{224,1... | collective-permute-start | bytes 294920 | tf_op jit(solution)/shard_map/ppermute | solution.py:405
  222.9 11.9 %collective-permute-start.12 = (bf16[2,64,384]{2,1,0:T(8,128)(2,1)S(1)}, bf16[2,64,384]{2,1,0:T(8,128)(2,1)S(1)}, u32[]{:S(2)}, u32[]{:S(2)}) collective-permute-start(bf16[2,64,384]{2,1,0:T(8,128)(2,1)S(1)} %get-tuple-element.30), channel_id=1, source_target_pairs={{0,96},{32,128},{64,160},{96,192},{128,224},{160,0},{192,32},{224,... | collective-permute-start | bytes 294920 | tf_op jit(solution)/shard_map/ppermute | solution.py:405
  224.1 10.5 %collective-permute-start.11 = (bf16[2,64,384]{2,1,0:T(8,128)(2,1)S(1)}, bf16[2,64,384]{2,1,0:T(8,128)(2,1)S(1)}, u32[]{:S(2)}, u32[]{:S(2)}) collective-permute-start(bf16[2,64,384]{2,1,0:T(8,128)(2,1)S(1)} %get-tuple-element.31), channel_id=1, source_target_pairs={{0,192},{32,224},{64,0},{96,32},{128,64},{160,96},{192,128},{224,1... | collective-permute-start | bytes 294920 | tf_op jit(solution)/shard_map/ppermute | solution.py:405
  225.5 9.1 %collective-permute-start.10 = (bf16[2,64,384]{2,1,0:T(8,128)(2,1)S(1)}, bf16[2,64,384]{2,1,0:T(8,128)(2,1)S(1)}, u32[]{:S(2)}, u32[]{:S(2)}) collective-permute-start(bf16[2,64,384]{2,1,0:T(8,128)(2,1)S(1)} %get-tuple-element.32), channel_id=1, source_target_pairs={{0,64},{32,96},{64,128},{96,160},{128,192},{160,224},{192,0},{224,... | collective-permute-start | bytes 294920 | tf_op jit(solution)/shard_map/ppermute | solution.py:405
  301.0 25.4 %copy-start.7 = (f32[8]{0:T(128)S(1)}, f32[8]{0:T(128)}, u32[]{:S(2)}) copy-start(f32[8]{0:T(128)} %param.20) | copy-start | bytes 100
  320.5 11.7 %all-to-all-start.5 = ((f32[16,8,128]{2,1,0:T(8,128)}), f32[16,8,128]{2,1,0:T(8,128)S(1)}, u32[]{:S(2)}, u32[]{:S(2)}) async-start(f32[16,8,128]{2,1,0:T(8,128)} %spread_sums.1), calls=%async_computation.5 | async-start | bytes 131072 | tf_op jit(solution)/shard_map/all_to_all | solution.py:498
  (5 other events, 21.9 us)
Sparse Core Ops, SparseCore 0:
  239.2 74.3 all-gather.1

commit v7 on v6

--- a/solution.py
+++ b/solution.py
@@ -19,6 +19,8 @@
 OWN = M // BANDS
 SLOTS = 32
 DEPTH = 8
+SHIFT = 3
+BOTH_WAYS = (1, 7, 2, 6, 3, 5, 4)
 RINGS = [[2 * z + h for z in range(DEPTH)] for h in range(2)]
 STEP = 3
 TOTAL_WEIGHT = float(np.sum(np.sin((np.arange(H) + 0.5) * np.pi / H)) * np.pi / H * E * W)
@@ -303,11 +305,16 @@
     )(spatial, x, table)
 
 
-def spread_kernel(weights_ref, own_ref, control_ref, out_ref, total):
+def control_rows(t):
+    return pl.BlockSpec((1, W, E), lambda j: ((STEP * j + t + 16 - 2 * SHIFT) % 16, 0, 0))
+
+
+def spread_kernel(weights_ref, own_ref, *refs):
+    *control_refs, out_ref, total = refs
     step = pl.program_id(0)
     partial = 0.0
     for j in range(STEP):
-        difference = own_ref[j].astype(jnp.float32) - control_ref[j].astype(jnp.float32)
+        difference = own_ref[j].astype(jnp.float32) - control_refs[j][0].astype(jnp.float32)
         squares = jnp.sum((difference * difference).reshape(W // 8, 8, E), axis=0)
         partial = partial + squares * weights_ref[step * STEP + j]
 
@@ -331,21 +338,22 @@
     return pl.pallas_call(
         spread_kernel,
         grid=(ROWS // STEP,),
-        in_specs=[scalars, row, row],
+        in_specs=[scalars, row] + [control_rows(t) for t in range(STEP)],
         out_specs=pl.BlockSpec((BANDS, 8, 128), lambda j: (0, 0, 0)),
         out_shape=jax.ShapeDtypeStruct((BANDS, 8, 128), jnp.float32),
         scratch_shapes=[pltpu.VMEM((8, E), jnp.float32)],
         compiler_params=pltpu.CompilerParams(vmem_limit_bytes=58 * MIB),
         cost_estimate=pl.CostEstimate(flops=9 << 20, bytes_accessed=11 << 20, transcendentals=0),
         name="spread_sums",
-    )(weights, own, control)
-
-
-def rescale_kernel(target_ref, sums_ref, own_ref, control_ref, out_ref):
+    )(weights, own, *[control] * STEP)
+
+
+def rescale_kernel(target_ref, sums_ref, own_ref, *refs):
+    *control_refs, out_ref = refs
     total = jnp.sum(jnp.sum(sums_ref[...], axis=0), axis=(0, 1), keepdims=True)
     scale = target_ref[0] / jnp.sqrt(total * (1.0 / TOTAL_WEIGHT) + 1e-06)
     for j in range(STEP):
-        control = control_ref[j].astype(jnp.float32)
+        control = control_refs[j][0].astype(jnp.float32)
         difference = own_ref[j].astype(jnp.float32) - control
         out_ref[j] = (control + scale * difference).astype(jnp.bfloat16)
 
@@ -360,14 +368,14 @@
             scalars,
             pl.BlockSpec((BANDS, 8, 128), lambda j: (0, 0, 0)),
             row,
-            row,
-        ],
+        ]
+        + [control_rows(t) for t in range(STEP)],
         out_specs=row,
         out_shape=jax.ShapeDtypeStruct((ROWS, W, E), jnp.bfloat16),
         compiler_params=pltpu.CompilerParams(vmem_limit_bytes=58 * MIB),
         cost_estimate=pl.CostEstimate(flops=9 << 20, bytes_accessed=17 << 20, transcendentals=0),
         name="rescaled",
-    )(target, sums, own, control)
+    )(target, sums, own, *[control] * STEP)
 
 
 def in_three(value):
@@ -380,11 +388,16 @@
 
 def scattered(field, extra):
     member = lax.axis_index("member")
-    kept = jnp.concatenate([field[:2].reshape(2 * W, E), extra])
-    for z in (1, 7, 2, 6, 3, 5, 4):
-        piece = field[2 * z : min(2 * z + 2, ROWS)].reshape(-1, E)
-        arrived = lax.ppermute(jnp.concatenate([piece, extra]), "member", [(0, 2 * z)])
-        if 2 * z + 1 == ROWS:
+
+    def piece(z):
+        first = 2 * ((z + SHIFT) % DEPTH)
+        rows = field[first : min(first + 2, ROWS)].reshape(-1, E)
+        return jnp.concatenate([rows, extra])
+
+    kept = piece(0)
+    for z in BOTH_WAYS:
+        arrived = lax.ppermute(piece(z), "member", [(0, 2 * z)])
+        if arrived.shape != kept.shape:
             arrived = jnp.concatenate([arrived[:W], arrived])
         kept = jnp.where(member == 2 * z, arrived, kept)
     return kept
@@ -399,7 +412,7 @@
 def permuted_along_z(pieces):
     z = lax.axis_index("member") // 2
     result = pieces
-    for shift in (1, 7, 2, 6, 3, 5, 4):
+    for shift in BOTH_WAYS:
         block = lax.dynamic_index_in_dim(pieces, (z + shift) % DEPTH, 0, keepdims=False)
         pairs = [(ring[a], ring[(a + shift) % DEPTH]) for ring in RINGS for a in range(DEPTH)]
         arrived = lax.ppermute(block, "member", pairs)
@@ -408,8 +421,33 @@
 
 
 def across(value):
-    arrived = lax.ppermute(value, "member", [(2 * z, 2 * z + 1) for z in range(DEPTH)])
+    half = BANDS // 2
+    pairs = [
+        (2 * z * BANDS + b, (2 * z + 1) * BANDS + (b + half) % BANDS)
+        for z in range(DEPTH)
+        for b in range(BANDS)
+    ]
+    arrived = lax.ppermute(value, ("member", "band"), pairs)
     return jnp.where(lax.axis_index("member") % 2 == 1, arrived, value)
+
+
+def home_again(value):
+    half = BANDS // 2
+    pairs = [
+        ((2 * z + 1) * BANDS + b, (2 * z + 1) * BANDS + (b + half) % BANDS)
+        for z in range(DEPTH)
+        for b in range(BANDS)
+    ]
+    arrived = lax.ppermute(value, ("member", "band"), pairs)
+    return jnp.where(lax.axis_index("member") % 2 == 1, arrived, value)
+
+
+def turned(value, first):
+    return jnp.concatenate([value[first:], value[:first]])
+
+
+def latitude_weights(rows):
+    return jnp.sin((rows.astype(jnp.float32) + 0.5) * (math.pi / H)) * (math.pi / H)
 
 
 def shards(
@@ -427,8 +465,7 @@
     legendre_np = legendre_table(L, M, H).reshape(OWN, BANDS, L, H).transpose(1, 0, 2, 3)
     x = jnp.transpose(copy_fields[0], (0, 2, 1))
 
-    global_rows = band_index * ROWS + jnp.arange(ROWS, dtype=jnp.int32)
-    weights = jnp.sin((global_rows.astype(jnp.float32) + 0.5) * (math.pi / H)) * (math.pi / H)
+    weights = latitude_weights(band_index * ROWS + jnp.arange(ROWS, dtype=jnp.int32))
     bank_rows = filter_bank.shape[0]
     draw_onehot = (jnp.arange(bank_rows, dtype=jnp.int32) == perturbation_draw_numbers[0]).astype(
         jnp.float32
@@ -444,6 +481,8 @@
         [jnp.concatenate([mix_real, mix_imag], 1), jnp.concatenate([-mix_imag, mix_real], 1)], 0
     )
     z = member // 2
+    crossed = member % 2 == 1
+    control_band = jnp.where(crossed, (band_index + BANDS // 2) % BANDS, band_index)
 
     fourier = forward_transform(x, norm_gain[None, :], weights, rounded(ahead_np), BANDS, STEP, 1 << 37)
     moved = lax.all_to_all(fourier, "band", split_axis=0, concat_axis=0, tiled=True)
@@ -453,12 +492,14 @@
     )
     control_x = control_parts[: 2 * W].reshape(2, W, E)
     control_gain = jnp.sum(control_parts[2 * W : 2 * W + 3, :L].astype(jnp.float32), axis=0)
-    control_weights = lax.dynamic_slice(jnp.pad(weights, (0, 1)), (2 * z,), (2,))
+    control_first = control_band * ROWS + 2 * ((z + SHIFT) % DEPTH)
+    control_weights = latitude_weights(control_first + jnp.arange(2, dtype=jnp.int32))
     control_fourier = forward_transform(
         control_x, norm_gain[None, :], control_weights, rounded(shared_ahead_np), DEPTH, 2, 1 << 29
     )
     moved, control_fourier = lax.optimization_barrier((moved, control_fourier))
     control_fourier = exchanged_along_z(control_fourier).reshape(DEPTH, 2, BANDS, 4, E)
+    control_fourier = turned(control_fourier, DEPTH - SHIFT)
     control_fourier = control_fourier.transpose(2, 0, 1, 3, 4).reshape(BANDS, 16, 4, E)[:, :ROWS]
     returned = spectral_pass(
         band_index[None],
@@ -470,6 +511,8 @@
     )
     returned, control_fourier = lax.optimization_barrier((returned, control_fourier))
     control_moved = lax.all_to_all(control_fourier, "band", split_axis=0, concat_axis=0, tiled=True)
+    control_moved = jnp.where(crossed, turned(control_moved, BANDS // 2), control_moved)
+    control_x, control_moved = lax.optimization_barrier((home_again(control_x), control_moved))
     control_spatial = shared_spectral_pass(
         place,
         control_moved.reshape(H, 4, E).transpose(1, 0, 2),
@@ -490,7 +533,8 @@
     )
     control_spatial = jnp.pad(control_spatial, ((0, 0), (0, 1), (0, 0), (0, 0)))
     control_spatial = control_spatial.reshape(BANDS, DEPTH, 2, 4, E).transpose(1, 2, 0, 3, 4)
-    control_spatial = permuted_along_z(control_spatial.reshape(DEPTH, 2, BANDS * 4, E))
+    control_spatial = turned(control_spatial.reshape(DEPTH, 2, BANDS * 4, E), SHIFT)
+    control_spatial = permuted_along_z(control_spatial)
     control = inverse_transform(control_spatial, control_x, rounded(shared_back_np), 2, 1 << 29)
     control = lax.all_gather(control, "member", tiled=True, axis_index_groups=RINGS)
 

time: 351 us -> 339 us (0.966)
  waiting for transfers between devices: 166 us -> 146 us
  starting transfers between devices: 63.7 us -> 68.5 us
    ppermute x8 -> x9, waiting for transfers between devices: 70.3 us -> 54.8 us  [the longest x7 40.9 us: scattered(): arrived = lax.ppermute(piece(z), 'member', [(0, 2 * z)])]
    all_to_all x1, waiting for transfers between devices: 51.2 us -> 47.5 us  [shards(): lax.all_to_all(returned.reshape(BANDS, ROWS, SLOTS, E), 'band', split_axi...]
    ppermute x8 -> x9, starting transfers between devices: 18.3 us -> 21 us  [the longest x7 18.1 us: scattered(): arrived = lax.ppermute(piece(z), 'member', [(0, 2 * z)])]
  transfers between devices with their start and end apart: 21 -> 22, of which waited for: 14 -> 12; matrix products, arithmetic and copies ran while one was open for 4% -> 5% of each run, Pallas kernels for 10% -> 11%
where the time goes in v7:
time: 339 us; the launch traced here: 337 us
  waiting for transfers between devices  146 us (43%)
  starting transfers between devices  68.5 us (20%)
  Pallas kernels  67.2 us (20%)
  blocking collectives  15.8 us (5%)
  between operations  15.7 us (5%)
  local copies, waits for them, and re-layouts  14.2 us (4%)
  other arithmetic  9.82 us (3%)
    all_to_all x1, waiting for transfers between devices, shards(): lax.all_to_all(returned.reshape(BANDS, ROWS, SLOTS, E), 'band', split_axi...  47.5 us
    ppermute x7, waiting for transfers between devices, scattered(): arrived = lax.ppermute(piece(z), 'member', [(0, 2 * z)])  40.9 us
    pallas_call x1, Pallas kernels, spectral_pass(): pl.pallas_call(spectral_kernel, grid_spec=pltpu.PrefetchScalarGridSpec(nu...  18.8 us
    ppermute x7, starting transfers between devices, scattered(): arrived = lax.ppermute(piece(z), 'member', [(0, 2 * z)])  18.1 us
    all_to_all x1, blocking collectives, shards(): lax.all_to_all(control_spatial.transpose(1, 0, 2).reshape(BANDS, ROWS, 4,...  15.8 us
    all_gather x1, waiting for transfers between devices, shards(): lax.all_gather(control, 'member', tiled=True, axis_index_groups=RINGS)  15.2 us
    ppermute x7, waiting for transfers between devices, permuted_along_z(): arrived = lax.ppermute(block, 'member', pairs)  14.1 us
    pallas_call x2, Pallas kernels, inverse_transform(): pl.pallas_call(inverse_kernel, grid=(rows // step,), in_specs=[pl.BlockSp...  14 us
  transfers between devices with their start and end apart: 22, of which 12 were waited for; matrix products, arithmetic and copies ran while one was open for 5% of the time, Pallas kernels for 11%

profile of v7, /device:TPU:1, one launch (start us, length us, event | category | flops | bytes accessed | tf_op | source)
XLA Modules:
  0.0 337.5 jit_solution(793662075679888702)
XLA Ops:
  8.4 9.7 %forward_transform.2 = bf16[16,15,32,384]{3,2,1,0:T(8,128)(2,1)} custom-call(f32[15]{0:T(128)} %sine_multiply_fusion.1.weights_ref, bf16[15,480,384]{2,1,0:T(8,128)(2,1)} %bitcast.80, f32[1,384]{1,0:T(1,128)} %broadcast_in_dim.43.gain_ref, bf16[512,480]{1,0:T(8,128)(2,1)} %constant.211.table_ref), custom_call_target="tpu_custom_call" | custom-call | flops 137438953472 | bytes 15728640 | tf_op jit(solution)/shard_map/forward_transform/pallas_call | solution.py:133
  18.1 7.7 %all-to-all-start = ((bf16[16,15,32,384]{3,2,1,0:T(8,128)(2,1)}), bf16[16,15,32,384]{3,2,1,0:T(8,128)(2,1)}, u32[]{:S(2)}, u32[]{:S(2)}) async-start(bf16[16,15,32,384]{3,2,1,0:T(8,128)(2,1)} %forward_transform.2), calls=%async_computation | async-start | bytes 11796480 | tf_op jit(solution)/shard_map/all_to_all | solution.py:488
  35.5 6.0 %collective-permute-start = (bf16[496,384]{1,0:T(8,128)(2,1)S(1)}, bf16[496,384]{1,0:T(8,128)(2,1)S(1)}, u32[]{:S(2)}, u32[]{:S(2)}) collective-permute-start(bf16[496,384]{1,0:T(8,128)(2,1)S(1)} %pad_maximum_fusion.7), channel_id=1, source_target_pairs={{0,128},{1,129},{2,130},{3,131},{4,132},{5,133},{6,134},{7,135},{8... | collective-permute-start | bytes 1142792 | tf_op jit(solution)/shard_map/ppermute | solution.py:399
  46.4 12.2 %collective-permute-done = bf16[496,384]{1,0:T(8,128)(2,1)S(1)} collective-permute-done((bf16[496,384]{1,0:T(8,128)(2,1)S(1)}, bf16[496,384]{1,0:T(8,128)(2,1)S(1)}, u32[]{:S(2)}, u32[]{:S(2)}) %collective-permute-start) | collective-permute-done | bytes 380960 | tf_op jit(solution)/shard_map/ppermute | solution.py:399
  63.0 11.8 %collective-permute-done.2 = bf16[976,384]{1,0:T(8,128)(2,1)S(1)} collective-permute-done((bf16[976,384]{1,0:T(8,128)(2,1)}, bf16[976,384]{1,0:T(8,128)(2,1)S(1)}, u32[]{:S(2)}, u32[]{:S(2)}) %collective-permute-start.2) | collective-permute-done | bytes 749600 | tf_op jit(solution)/shard_map/ppermute | solution.py:399
  74.7 16.1 %collective-permute-done.4 = bf16[976,384]{1,0:T(8,128)(2,1)} collective-permute-done((bf16[976,384]{1,0:T(8,128)(2,1)}, bf16[976,384]{1,0:T(8,128)(2,1)}, u32[]{:S(2)}, u32[]{:S(2)}) %collective-permute-start.4) | collective-permute-done | bytes 749600 | tf_op jit(solution)/shard_map/ppermute | solution.py:399
  94.5 13.8 %collective-permute-done.7 = bf16[976,384]{1,0:T(8,128)(2,1)S(1)} collective-permute-done((bf16[976,384]{1,0:T(8,128)(2,1)S(1)}, bf16[976,384]{1,0:T(8,128)(2,1)S(1)}, u32[]{:S(2)}, u32[]{:S(2)}) %collective-permute-start.7) | collective-permute-done | bytes 749600 | tf_op jit(solution)/shard_map/ppermute | solution.py:430
  112.6 7.7 %all-to-all-start.1 = ((bf16[8,2,64,384]{3,2,1,0:T(8,128)(2,1)}), bf16[8,2,64,384]{3,2,1,0:T(8,128)(2,1)S(1)}, u32[]{:S(2)}, u32[]{:S(2)}) async-start(bf16[8,2,64,384]{3,2,1,0:T(8,128)(2,1)} %forward_transform.3), calls=%async_computation.1 | async-start | bytes 1572864 | tf_op jit(solution)/shard_map/all_to_all | solution.py:407
  123.9 18.8 %spectral_pass.1 = bf16[240,32,384]{2,1,0:T(8,128)(2,1)} custom-call(s32[1]{0:T(128)} %bitcast.2.band_ref, bf16[240,32,384]{2,1,0:T(8,128)(2,1)} %bitcast.18.moved_ref, bf16[16,15,240,240]{3,2,1,0:T(8,128)(2,1)} %constant.213.legendre_ref, f32[240,1]{1,0:T(8,128)} %copy.23.gain_ref, bf16[768,768]{1,0:T(8,128)(2,1)} %maximum_maximum_fusion.mixing_ref, ...), custom_call_target="tpu_custom_call" | custom-call | flops 8589934592 | bytes 14680064 | tf_op jit(solution)/shard_map/spectral_pass/pallas_call | solution.py:255
  145.0 8.4 %all-to-all-start.2 = ((bf16[16,15,4,384]{3,2,1,0:T(4,128)(2,1)}), bf16[16,15,4,384]{3,2,1,0:T(4,128)(2,1)S(1)}, u32[]{:S(2)}, u32[]{:S(2)}) async-start(bf16[16,15,4,384]{3,2,1,0:T(4,128)(2,1)} %slice.100), calls=%async_computation.2 | async-start | bytes 1474560 | tf_op jit(solution)/shard_map/all_to_all | solution.py:513
  155.8 10.1 %all-to-all-done.2 = bf16[16,15,4,384]{3,2,1,0:T(4,128)(2,1)S(1)} async-done(((bf16[16,15,4,384]{3,2,1,0:T(4,128)(2,1)}), bf16[16,15,4,384]{3,2,1,0:T(4,128)(2,1)S(1)}, u32[]{:S(2)}, u32[]{:S(2)}) %all-to-all-start.2) | async-done | bytes 737312 | tf_op jit(solution)/shard_map/all_to_all | solution.py:513
  167.7 4.8 %shared_spectral_pass.1 = (bf16[2,240,384]{2,1,0:T(8,128)(2,1)}, bf16[2,240,384]{2,1,0:T(8,128)(2,1)}) custom-call(s32[2]{0:T(128)} %pad_add_fusion.place_ref, bf16[4,240,384]{2,1,0:T(8,128)(2,1)} %bitcast.78, bf16[4,240,384]{2,1,0:T(8,128)(2,1)} %bitcast.79, bf16[16,15,240,240]{3,2,1,0:T(8,128)(2,1)} %constant.213.legendre_ref, f32[240,1]{1,0:T(8,128)} %copy.26.gain_ref, ...), custom_call_target="tpu_custom_call" | custom-call | flops 1073741824 | bytes 4194304 | tf_op jit(solution)/shard_map/shared_spectral_pass/pallas_call | solution.py:175
  174.0 15.8 %all_to_all.30 = bf16[16,15,4,384]{3,2,1,0:T(4,128)(2,1)S(1)} all-to-all(bf16[16,15,4,384]{3,2,1,0:T(4,128)(2,1)S(1)} %bitcast.90), channel_id=1, replica_groups=mesh['member'=16,'band'=16] {'band'}, dimensions={0} | all-to-all | bytes 1474560 | tf_op jit(solution)/shard_map/all_to_all | solution.py:523
  189.8 5.2 %all-to-all-start.4 = ((bf16[16,15,32,384]{3,2,1,0:T(8,128)(2,1)}), bf16[16,15,32,384]{3,2,1,0:T(8,128)(2,1)}, u32[]{:S(2)}, u32[]{:S(2)}) async-start(bf16[16,15,32,384]{3,2,1,0:T(8,128)(2,1)} %bitcast.74), calls=%async_computation.4 | async-start | bytes 11796480 | tf_op jit(solution)/shard_map/all_to_all | solution.py:531
  197.9 4.2 %collective-permute-done.9 = bf16[2,64,384]{2,1,0:T(8,128)(2,1)S(1)} collective-permute-done((bf16[2,64,384]{2,1,0:T(8,128)(2,1)S(1)}, bf16[2,64,384]{2,1,0:T(8,128)(2,1)S(1)}, u32[]{:S(2)}, u32[]{:S(2)}) %collective-permute-start.9) | collective-permute-done | bytes 98336 | tf_op jit(solution)/shard_map/ppermute | solution.py:418
  204.2 4.1 %collective-permute-start.15 = (bf16[2,64,384]{2,1,0:T(8,128)(2,1)S(1)}, bf16[2,64,384]{2,1,0:T(8,128)(2,1)S(1)}, u32[]{:S(2)}, u32[]{:S(2)}) collective-permute-start(bf16[2,64,384]{2,1,0:T(8,128)(2,1)S(1)} %get-tuple-element.32), channel_id=1, source_target_pairs={{0,128},{32,160},{64,192},{96,224},{128,0},{160,32},{192,64},{224,... | collective-permute-start | bytes 294920 | tf_op jit(solution)/shard_map/ppermute | solution.py:418
  214.0 8.9 %collective-permute-done.11 = bf16[2,64,384]{2,1,0:T(8,128)(2,1)S(1)} collective-permute-done((bf16[2,64,384]{2,1,0:T(8,128)(2,1)S(1)}, bf16[2,64,384]{2,1,0:T(8,128)(2,1)S(1)}, u32[]{:S(2)}, u32[]{:S(2)}) %collective-permute-start.11) | collective-permute-done | bytes 98336 | tf_op jit(solution)/shard_map/ppermute | solution.py:418
  228.2 47.5 %all-to-all-done.4.spatial_ref = bf16[16,15,32,384]{3,2,1,0:T(8,128)(2,1)} async-done(((bf16[16,15,32,384]{3,2,1,0:T(8,128)(2,1)}), bf16[16,15,32,384]{3,2,1,0:T(8,128)(2,1)}, u32[]{:S(2)}, u32[]{:S(2)}) %all-to-all-start.4) | async-done | bytes 5898272 | tf_op jit(solution)/shard_map/all_to_all | solution.py:531
  275.8 10.7 %inverse_transform.2.own_ref = bf16[15,480,384]{2,1,0:T(8,128)(2,1)} custom-call(bf16[16,15,32,384]{3,2,1,0:T(8,128)(2,1)} %all-to-all-done.4.spatial_ref, bf16[15,480,384]{2,1,0:T(8,128)(2,1)} %bitcast.83, bf16[480,512]{1,0:T(8,128)(2,1)} %constant.215.table_ref), custom_call_target="tpu_custom_call" | custom-call | flops 274877906944 | bytes 15728640 | tf_op jit(solution)/shard_map/inverse_transform/pallas_call | solution.py:290
  286.5 15.2 %all-gather.2.cloned.1.call-done.refs_0_.refs_1_.refs_2_ = bf16[16,480,384]{2,1,0:T(8,128)(2,1)} async-done(((bf16[2,480,384]{2,1,0:T(8,128)(2,1)}), bf16[16,480,384]{2,1,0:T(8,128)(2,1)}) %all-gather.2.cloned.1.call-update) | async-done | bytes 5898256 | tf_op jit(solution)/shard_map/all_gather | solution.py:539
  301.6 6.9 %spread_sums.1 = f32[16,8,128]{2,1,0:T(8,128)} custom-call(f32[15]{0:T(128)} %sine_multiply_fusion.1.weights_ref, bf16[15,480,384]{2,1,0:T(8,128)(2,1)} %inverse_transform.2.own_ref, bf16[16,480,384]{2,1,0:T(8,128)(2,1)} %all-gather.2.cloned.1.call-done.refs_0_.refs_1_.refs_2_, bf16[16,480,384]{2,1,0:T(8,128)(2,1)} %all-gather.2.cloned.1.call-done.refs_0_.refs_1_.refs_2_, ...), custom_call_target="tpu_custom_call" | custom-call | flops 9437184 | bytes 11534336 | tf_op jit(solution)/shard_map/spread_sums/pallas_call | solution.py:338
  308.5 5.9 %all-to-all-start.5 = ((f32[16,8,128]{2,1,0:T(8,128)}), f32[16,8,128]{2,1,0:T(8,128)S(1)}, u32[]{:S(2)}, u32[]{:S(2)}) async-start(f32[16,8,128]{2,1,0:T(8,128)} %spread_sums.1), calls=%async_computation.5 | async-start | bytes 131072 | tf_op jit(solution)/shard_map/all_to_all | solution.py:542
  315.7 4.6 %all-to-all-done.5.sums_ref = f32[16,8,128]{2,1,0:T(8,128)S(1)} async-done(((f32[16,8,128]{2,1,0:T(8,128)}), f32[16,8,128]{2,1,0:T(8,128)S(1)}, u32[]{:S(2)}, u32[]{:S(2)}) %all-to-all-start.5) | async-done | bytes 65568 | tf_op jit(solution)/shard_map/all_to_all | solution.py:542
  320.9 9.8 %rescaled.1 = bf16[15,480,384]{2,1,0:T(8,128)(2,1)} custom-call(f32[1]{0:T(128)} %bitcast.1.target_ref, f32[16,8,128]{2,1,0:T(8,128)} %copy-done.5, bf16[15,480,384]{2,1,0:T(8,128)(2,1)} %inverse_transform.2.own_ref, bf16[16,480,384]{2,1,0:T(8,128)(2,1)} %all-gather.2.cloned.1.call-done.refs_0_.refs_1_.refs_2_, ...), custom_call_target="tpu_custom_call" | custom-call | flops 9437184 | bytes 17825792 | tf_op jit(solution)/shard_map/rescaled/pallas_call | solution.py:364
  (97 shorter events, 55.9 us)
Async XLA Ops:
  18.1 94.5 %all-to-all-start = ((bf16[16,15,32,384]{3,2,1,0:T(8,128)(2,1)}), bf16[16,15,32,384]{3,2,1,0:T(8,128)(2,1)}, u32[]{:S(2)}, u32[]{:S(2)}) async-start(bf16[16,15,32,384]{3,2,1,0:T(8,128)(2,1)} %forward_transform.2), calls=%async_computation | async-start | bytes 11796480 | tf_op jit(solution)/shard_map/all_to_all | solution.py:488
  31.5 29.2 %collective-permute-start.6 = (bf16[976,384]{1,0:T(8,128)(2,1)S(1)}, bf16[976,384]{1,0:T(8,128)(2,1)S(1)}, u32[]{:S(2)}, u32[]{:S(2)}) collective-permute-start(bf16[976,384]{1,0:T(8,128)(2,1)S(1)} %get-tuple-element.41), channel_id=1, source_target_pairs={{0,32},{1,33},{2,34},{3,35},{4,36},{5,37},{6,38},{7,39},{8,40},{9,... | collective-permute-start | bytes 2248712 | tf_op jit(solution)/shard_map/ppermute | solution.py:399
  35.5 23.0 %collective-permute-start = (bf16[496,384]{1,0:T(8,128)(2,1)S(1)}, bf16[496,384]{1,0:T(8,128)(2,1)S(1)}, u32[]{:S(2)}, u32[]{:S(2)}) collective-permute-start(bf16[496,384]{1,0:T(8,128)(2,1)S(1)} %pad_maximum_fusion.7), channel_id=1, source_target_pairs={{0,128},{1,129},{2,130},{3,131},{4,132},{5,133},{6,134},{7,135},{8... | collective-permute-start | bytes 1142792 | tf_op jit(solution)/shard_map/ppermute | solution.py:399
  41.5 33.2 %collective-permute-start.2 = (bf16[976,384]{1,0:T(8,128)(2,1)}, bf16[976,384]{1,0:T(8,128)(2,1)S(1)}, u32[]{:S(2)}, u32[]{:S(2)}) collective-permute-start(bf16[976,384]{1,0:T(8,128)(2,1)} %get-tuple-element.42), channel_id=1, source_target_pairs={{0,96},{1,97},{2,98},{3,99},{4,100},{5,101},{6,102},{7,103},{8,104... | collective-permute-start | bytes 2248712 | tf_op jit(solution)/shard_map/ppermute | solution.py:399
  42.8 31.9 %collective-permute-start.3 = (bf16[976,384]{1,0:T(8,128)(2,1)}, bf16[976,384]{1,0:T(8,128)(2,1)S(1)}, u32[]{:S(2)}, u32[]{:S(2)}) collective-permute-start(bf16[976,384]{1,0:T(8,128)(2,1)} %get-tuple-element.43), channel_id=1, source_target_pairs={{0,192},{1,193},{2,194},{3,195},{4,196},{5,197},{6,198},{7,199},{8... | collective-permute-start | bytes 2248712 | tf_op jit(solution)/shard_map/ppermute | solution.py:399
  44.2 46.6 %collective-permute-start.4 = (bf16[976,384]{1,0:T(8,128)(2,1)}, bf16[976,384]{1,0:T(8,128)(2,1)}, u32[]{:S(2)}, u32[]{:S(2)}) collective-permute-start(bf16[976,384]{1,0:T(8,128)(2,1)} %get-tuple-element.44), channel_id=1, source_target_pairs={{0,64},{1,65},{2,66},{3,67},{4,68},{5,69},{6,70},{7,71},{8,72},{9,... | collective-permute-start | bytes 2248712 | tf_op jit(solution)/shard_map/ppermute | solution.py:399
  58.5 32.2 %collective-permute-start.5 = (bf16[976,384]{1,0:T(8,128)(2,1)}, bf16[976,384]{1,0:T(8,128)(2,1)}, u32[]{:S(2)}, u32[]{:S(2)}) collective-permute-start(bf16[976,384]{1,0:T(8,128)(2,1)} %get-tuple-element.45), channel_id=1, source_target_pairs={{0,224},{1,225},{2,226},{3,227},{4,228},{5,229},{6,230},{7,231},{8... | collective-permute-start | bytes 2248712 | tf_op jit(solution)/shard_map/ppermute | solution.py:399
  60.7 31.0 %collective-permute-start.1 = (bf16[976,384]{1,0:T(8,128)(2,1)}, bf16[976,384]{1,0:T(8,128)(2,1)}, u32[]{:S(2)}, u32[]{:S(2)}) collective-permute-start(bf16[976,384]{1,0:T(8,128)(2,1)} %get-tuple-element.46), channel_id=1, source_target_pairs={{0,160},{1,161},{2,162},{3,163},{4,164},{5,165},{6,166},{7,167},{8... | collective-permute-start | bytes 2248712 | tf_op jit(solution)/shard_map/ppermute | solution.py:399
  74.7 17.0 %copy-start.3 = (bf16[976,384]{1,0:T(8,128)(2,1)}, bf16[976,384]{1,0:T(8,128)(2,1)S(1)}, u32[]{:S(2)}) copy-start(bf16[976,384]{1,0:T(8,128)(2,1)S(1)} %collective-permute-done.3) | copy-start | bytes 2248708
  92.5 15.8 %collective-permute-start.7 = (bf16[976,384]{1,0:T(8,128)(2,1)S(1)}, bf16[976,384]{1,0:T(8,128)(2,1)S(1)}, u32[]{:S(2)}, u32[]{:S(2)}) collective-permute-start(bf16[976,384]{1,0:T(8,128)(2,1)S(1)} %fusion.6), channel_id=1, source_target_pairs={{0,24},{1,25},{2,26},{3,27},{4,28},{5,29},{6,30},{7,31},{8,16},{9,... | collective-permute-start | bytes 2248712 | tf_op jit(solution)/shard_map/ppermute | solution.py:430
  112.6 30.1 %all-to-all-start.1 = ((bf16[8,2,64,384]{3,2,1,0:T(8,128)(2,1)}), bf16[8,2,64,384]{3,2,1,0:T(8,128)(2,1)S(1)}, u32[]{:S(2)}, u32[]{:S(2)}) async-start(bf16[8,2,64,384]{3,2,1,0:T(8,128)(2,1)} %forward_transform.3), calls=%async_computation.1 | async-start | bytes 1572864 | tf_op jit(solution)/shard_map/all_to_all | solution.py:407
  122.3 32.5 %collective-permute-start.8 = (bf16[2,480,384]{2,1,0:T(8,128)(2,1)S(1)}, bf16[2,480,384]{2,1,0:T(8,128)(2,1)}, u32[]{:S(2)}, u32[]{:S(2)}) collective-permute-start(bf16[2,480,384]{2,1,0:T(8,128)(2,1)S(1)} %bitcast.76), channel_id=1, source_target_pairs={{16,24},{17,25},{18,26},{19,27},{20,28},{21,29},{22,30},{23,31},{2... | collective-permute-start | bytes 2211848 | tf_op jit(solution)/shard_map/ppermute | solution.py:441
  145.0 20.9 %all-to-all-start.2 = ((bf16[16,15,4,384]{3,2,1,0:T(4,128)(2,1)}), bf16[16,15,4,384]{3,2,1,0:T(4,128)(2,1)S(1)}, u32[]{:S(2)}, u32[]{:S(2)}) async-start(bf16[16,15,4,384]{3,2,1,0:T(4,128)(2,1)} %slice.100), calls=%async_computation.2 | async-start | bytes 1474560 | tf_op jit(solution)/shard_map/all_to_all | solution.py:513
  189.8 86.0 %all-to-all-start.4 = ((bf16[16,15,32,384]{3,2,1,0:T(8,128)(2,1)}), bf16[16,15,32,384]{3,2,1,0:T(8,128)(2,1)}, u32[]{:S(2)}, u32[]{:S(2)}) async-start(bf16[16,15,32,384]{3,2,1,0:T(8,128)(2,1)} %bitcast.74), calls=%async_computation.4 | async-start | bytes 11796480 | tf_op jit(solution)/shard_map/all_to_all | solution.py:531
  195.0 106.7 %all-gather.2.cloned.1.call-start = ((), (), s32[]{:S(2)}) async-start(), calls=%async_computation.6 | async-start | bytes 6635520 | tf_op jit(solution)/shard_map/all_gather | solution.py:539
  196.7 5.5 %collective-permute-start.9 = (bf16[2,64,384]{2,1,0:T(8,128)(2,1)S(1)}, bf16[2,64,384]{2,1,0:T(8,128)(2,1)S(1)}, u32[]{:S(2)}, u32[]{:S(2)}) collective-permute-start(bf16[2,64,384]{2,1,0:T(8,128)(2,1)S(1)} %dynamic-slice_bitcast_fusion.6), channel_id=1, source_target_pairs={{0,32},{32,64},{64,96},{96,128},{128,160},{160,192},{192,224},{224... | collective-permute-start | bytes 294920 | tf_op jit(solution)/shard_map/ppermute | solution.py:418
  202.3 10.7 %collective-permute-start.10 = (bf16[2,64,384]{2,1,0:T(8,128)(2,1)S(1)}, bf16[2,64,384]{2,1,0:T(8,128)(2,1)S(1)}, u32[]{:S(2)}, u32[]{:S(2)}) collective-permute-start(bf16[2,64,384]{2,1,0:T(8,128)(2,1)S(1)} %get-tuple-element.37), channel_id=1, source_target_pairs={{0,224},{32,0},{64,32},{96,64},{128,96},{160,128},{192,160},{224,1... | collective-permute-start | bytes 294920 | tf_op jit(solution)/shard_map/ppermute | solution.py:418
  204.2 19.7 %collective-permute-start.15 = (bf16[2,64,384]{2,1,0:T(8,128)(2,1)S(1)}, bf16[2,64,384]{2,1,0:T(8,128)(2,1)S(1)}, u32[]{:S(2)}, u32[]{:S(2)}) collective-permute-start(bf16[2,64,384]{2,1,0:T(8,128)(2,1)S(1)} %get-tuple-element.32), channel_id=1, source_target_pairs={{0,128},{32,160},{64,192},{96,224},{128,0},{160,32},{192,64},{224,... | collective-permute-start | bytes 294920 | tf_op jit(solution)/shard_map/ppermute | solution.py:418
  208.3 15.6 %collective-permute-start.14 = (bf16[2,64,384]{2,1,0:T(8,128)(2,1)S(1)}, bf16[2,64,384]{2,1,0:T(8,128)(2,1)S(1)}, u32[]{:S(2)}, u32[]{:S(2)}) collective-permute-start(bf16[2,64,384]{2,1,0:T(8,128)(2,1)S(1)} %get-tuple-element.33), channel_id=1, source_target_pairs={{0,160},{32,192},{64,224},{96,0},{128,32},{160,64},{192,96},{224,1... | collective-permute-start | bytes 294920 | tf_op jit(solution)/shard_map/ppermute | solution.py:418
  208.8 15.1 %collective-permute-start.13 = (bf16[2,64,384]{2,1,0:T(8,128)(2,1)S(1)}, bf16[2,64,384]{2,1,0:T(8,128)(2,1)S(1)}, u32[]{:S(2)}, u32[]{:S(2)}) collective-permute-start(bf16[2,64,384]{2,1,0:T(8,128)(2,1)S(1)} %get-tuple-element.34), channel_id=1, source_target_pairs={{0,96},{32,128},{64,160},{96,192},{128,224},{160,0},{192,32},{224,... | collective-permute-start | bytes 294920 | tf_op jit(solution)/shard_map/ppermute | solution.py:418
  211.6 12.3 %collective-permute-start.12 = (bf16[2,64,384]{2,1,0:T(8,128)(2,1)S(1)}, bf16[2,64,384]{2,1,0:T(8,128)(2,1)S(1)}, u32[]{:S(2)}, u32[]{:S(2)}) collective-permute-start(bf16[2,64,384]{2,1,0:T(8,128)(2,1)S(1)} %get-tuple-element.35), channel_id=1, source_target_pairs={{0,192},{32,224},{64,0},{96,32},{128,64},{160,96},{192,128},{224,1... | collective-permute-start | bytes 294920 | tf_op jit(solution)/shard_map/ppermute | solution.py:418
  213.0 9.9 %collective-permute-start.11 = (bf16[2,64,384]{2,1,0:T(8,128)(2,1)S(1)}, bf16[2,64,384]{2,1,0:T(8,128)(2,1)S(1)}, u32[]{:S(2)}, u32[]{:S(2)}) collective-permute-start(bf16[2,64,384]{2,1,0:T(8,128)(2,1)S(1)} %get-tuple-element.36), channel_id=1, source_target_pairs={{0,64},{32,96},{64,128},{96,160},{128,192},{160,224},{192,0},{224,... | collective-permute-start | bytes 294920 | tf_op jit(solution)/shard_map/ppermute | solution.py:418
  286.5 27.9 %copy-start.7 = (f32[8]{0:T(128)S(1)}, f32[8]{0:T(128)}, u32[]{:S(2)}) copy-start(f32[8]{0:T(128)} %param.20) | copy-start | bytes 100
  308.5 11.7 %all-to-all-start.5 = ((f32[16,8,128]{2,1,0:T(8,128)}), f32[16,8,128]{2,1,0:T(8,128)S(1)}, u32[]{:S(2)}, u32[]{:S(2)}) async-start(f32[16,8,128]{2,1,0:T(8,128)} %spread_sums.1), calls=%async_computation.5 | async-start | bytes 131072 | tf_op jit(solution)/shard_map/all_to_all | solution.py:542
  (6 other events, 32.2 us)
Sparse Core Ops, SparseCore 0:
  228.3 73.2 all-gather.1

commit v8 on v7

--- a/solution.py
+++ b/solution.py
@@ -24,6 +24,7 @@
 RINGS = [[2 * z + h for z in range(DEPTH)] for h in range(2)]
 STEP = 3
 TOTAL_WEIGHT = float(np.sum(np.sin((np.arange(H) + 0.5) * np.pi / H)) * np.pi / H * E * W)
+HALF = W // 2
 MIB = 1 << 20
 
 
@@ -305,17 +306,25 @@
     )(spatial, x, table)
 
 
-def control_rows(t):
-    return pl.BlockSpec((1, W, E), lambda j: ((STEP * j + t + 16 - 2 * SHIFT) % 16, 0, 0))
+def control_rows():
+    half = lambda t: pl.BlockSpec((1, HALF, E), lambda j: ((STEP * j + t + 16 - 2 * SHIFT) % 16, 0, 0))
+    return [half(t) for t in range(STEP)] * 2
+
+
+def halves(control_refs):
+    for part in range(2):
+        for j in range(STEP):
+            where = slice(part * HALF, part * HALF + HALF)
+            yield j, where, control_refs[part * STEP + j][0].astype(jnp.float32)
 
 
 def spread_kernel(weights_ref, own_ref, *refs):
     *control_refs, out_ref, total = refs
     step = pl.program_id(0)
     partial = 0.0
-    for j in range(STEP):
-        difference = own_ref[j].astype(jnp.float32) - control_refs[j][0].astype(jnp.float32)
-        squares = jnp.sum((difference * difference).reshape(W // 8, 8, E), axis=0)
+    for j, where, control in halves(control_refs):
+        difference = own_ref[j, where].astype(jnp.float32) - control
+        squares = jnp.sum((difference * difference).reshape(HALF // 8, 8, E), axis=0)
         partial = partial + squares * weights_ref[step * STEP + j]
 
     @pl.when(step == 0)
@@ -332,33 +341,32 @@
         out_ref[...] = jnp.broadcast_to(lanes[None], out_ref.shape)
 
 
-def spread_sums(weights, own, control):
+def spread_sums(weights, own, near, far):
     row = pl.BlockSpec((STEP, W, E), lambda j: (j, 0, 0))
     scalars = pl.BlockSpec(memory_space=pltpu.SMEM)
     return pl.pallas_call(
         spread_kernel,
         grid=(ROWS // STEP,),
-        in_specs=[scalars, row] + [control_rows(t) for t in range(STEP)],
+        in_specs=[scalars, row] + control_rows(),
         out_specs=pl.BlockSpec((BANDS, 8, 128), lambda j: (0, 0, 0)),
         out_shape=jax.ShapeDtypeStruct((BANDS, 8, 128), jnp.float32),
         scratch_shapes=[pltpu.VMEM((8, E), jnp.float32)],
         compiler_params=pltpu.CompilerParams(vmem_limit_bytes=58 * MIB),
         cost_estimate=pl.CostEstimate(flops=9 << 20, bytes_accessed=11 << 20, transcendentals=0),
         name="spread_sums",
-    )(weights, own, *[control] * STEP)
+    )(weights, own, *[near] * STEP, *[far] * STEP)
 
 
 def rescale_kernel(target_ref, sums_ref, own_ref, *refs):
     *control_refs, out_ref = refs
     total = jnp.sum(jnp.sum(sums_ref[...], axis=0), axis=(0, 1), keepdims=True)
     scale = target_ref[0] / jnp.sqrt(total * (1.0 / TOTAL_WEIGHT) + 1e-06)
-    for j in range(STEP):
-        control = control_refs[j][0].astype(jnp.float32)
-        difference = own_ref[j].astype(jnp.float32) - control
-        out_ref[j] = (control + scale * difference).astype(jnp.bfloat16)
-
-
-def rescaled(target, sums, own, control):
+    for j, where, control in halves(control_refs):
+        difference = own_ref[j, where].astype(jnp.float32) - control
+        out_ref[j, where] = (control + scale * difference).astype(jnp.bfloat16)
+
+
+def rescaled(target, sums, own, near, far):
     row = pl.BlockSpec((STEP, W, E), lambda j: (j, 0, 0))
     scalars = pl.BlockSpec(memory_space=pltpu.SMEM)
     return pl.pallas_call(
@@ -369,13 +377,13 @@
             pl.BlockSpec((BANDS, 8, 128), lambda j: (0, 0, 0)),
             row,
         ]
-        + [control_rows(t) for t in range(STEP)],
+        + control_rows(),
         out_specs=row,
         out_shape=jax.ShapeDtypeStruct((ROWS, W, E), jnp.bfloat16),
         compiler_params=pltpu.CompilerParams(vmem_limit_bytes=58 * MIB),
         cost_estimate=pl.CostEstimate(flops=9 << 20, bytes_accessed=17 << 20, transcendentals=0),
         name="rescaled",
-    )(target, sums, own, *[control] * STEP)
+    )(target, sums, own, *[near] * STEP, *[far] * STEP)
 
 
 def in_three(value):
@@ -417,6 +425,21 @@
         pairs = [(ring[a], ring[(a + shift) % DEPTH]) for ring in RINGS for a in range(DEPTH)]
         arrived = lax.ppermute(block, "member", pairs)
         result = lax.dynamic_update_index_in_dim(result, arrived, (z - shift) % DEPTH, 0)
+    return result
+
+
+def around_the_ring(piece):
+    z = lax.axis_index("member") // 2
+    up = [(ring[a], ring[(a + 1) % DEPTH]) for ring in RINGS for a in range(DEPTH)]
+    down = [(b, a) for a, b in up]
+    result = jnp.zeros((2 * DEPTH,) + piece.shape[1:], piece.dtype)
+    result = lax.dynamic_update_slice_in_dim(result, piece, 2 * z, 0)
+    first, second = piece[:1], piece[1:]
+    for step in range(1, DEPTH):
+        first = lax.ppermute(first, "member", up)
+        second = lax.ppermute(second, "member", down)
+        result = lax.dynamic_update_slice_in_dim(result, first, 2 * ((z - step) % DEPTH), 0)
+        result = lax.dynamic_update_slice_in_dim(result, second, 2 * ((z + step) % DEPTH) + 1, 0)
     return result
 
 
@@ -536,11 +559,13 @@
     control_spatial = turned(control_spatial.reshape(DEPTH, 2, BANDS * 4, E), SHIFT)
     control_spatial = permuted_along_z(control_spatial)
     control = inverse_transform(control_spatial, control_x, rounded(shared_back_np), 2, 1 << 29)
-    control = lax.all_gather(control, "member", tiled=True, axis_index_groups=RINGS)
+    near = lax.all_gather(control[:, :HALF], "member", tiled=True, axis_index_groups=RINGS)
+    far = around_the_ring(control[:, HALF:])
+    spatial, far = lax.optimization_barrier((spatial, far))
 
     forecast = inverse_transform(spatial, x, rounded(back_np), STEP, 1 << 38)
     sums = lax.all_to_all(
-        spread_sums(weights, forecast, control),
+        spread_sums(weights, forecast, near, far),
         "band",
         split_axis=0,
         concat_axis=0,
@@ -553,7 +578,7 @@
             0.0,
         )
     )
-    bred = rescaled(jnp.where(member > 0, target, 0.0)[None], sums, forecast, control)
+    bred = rescaled(jnp.where(member > 0, target, 0.0)[None], sums, forecast, near, far)
     return jnp.transpose(bred, (0, 2, 1))[None]
 
 

time: 339 us -> 358 us (1.056); the launches traced: 337 us -> 352 us
  starting transfers between devices: 68.5 us -> 102 us
  waiting for transfers between devices: 146 us -> 122 us
    all_to_all x1, waiting for transfers between devices: 47.5 us -> 0.01 us  [shards(): lax.all_to_all(returned.reshape(BANDS, ROWS, SLOTS, E), 'band', split_axi...]
    ppermute x0 -> x14, waiting for transfers between devices: none -> 35.9 us  [the longest x7 28.9 us: around_the_ring(): first = lax.ppermute(first, 'member', up)]
    ppermute x0 -> x14, starting transfers between devices: none -> 26 us  [the longest x7 17.6 us: around_the_ring(): second = lax.ppermute(second, 'member', down)]
    all_gather x1, waiting for transfers between devices: 15.2 us -> 0.02 us  [shards(): lax.all_gather(control[:, :HALF], 'member', tiled=True, axis_index_groups...]
    all_to_all x1, starting transfers between devices: 5.88 us -> 14.5 us  [shards(): lax.all_to_all(spread_sums(weights, forecast, near, far), 'band', split_a...]
    ppermute x7, waiting for transfers between devices: 40.9 us -> 47.1 us  [scattered(): arrived = lax.ppermute(piece(z), 'member', [(0, 2 * z)])]
    ppermute x7, waiting for transfers between devices: 14.1 us -> 9.51 us  [permuted_along_z(): arrived = lax.ppermute(block, 'member', pairs)]
  transfers between devices with their start and end apart: 22 -> 36, of which waited for: 12 -> 24; matrix products, arithmetic and copies ran while one was open for 5% -> 6% of each run, Pallas kernels for 11% -> 11%
where the time goes in v8:
time: 358 us; the launch traced here: 352 us
  waiting for transfers between devices  122 us (34%)
  starting transfers between devices  102 us (28%)
  Pallas kernels  68.4 us (19%)
  local copies, waits for them, and re-layouts  17.5 us (5%)
  between operations  16.4 us (5%)
  blocking collectives  15.8 us (4%)
  other arithmetic  9.88 us (3%)
    ppermute x7, waiting for transfers between devices, scattered(): arrived = lax.ppermute(piece(z), 'member', [(0, 2 * z)])  47.1 us
    ppermute x7, waiting for transfers between devices, around_the_ring(): first = lax.ppermute(first, 'member', up)  28.9 us
    pallas_call x1, Pallas kernels, spectral_pass(): pl.pallas_call(spectral_kernel, grid_spec=pltpu.PrefetchScalarGridSpec(nu...  18.8 us
    ppermute x7, starting transfers between devices, scattered(): arrived = lax.ppermute(piece(z), 'member', [(0, 2 * z)])  18.2 us
    ppermute x7, starting transfers between devices, around_the_ring(): second = lax.ppermute(second, 'member', down)  17.6 us
    all_to_all x1, blocking collectives, shards(): lax.all_to_all(control_spatial.transpose(1, 0, 2).reshape(BANDS, ROWS, 4,...  15.8 us
    ppermute x7, starting transfers between devices, permuted_along_z(): arrived = lax.ppermute(block, 'member', pairs)  15.5 us
    pallas_call x2, Pallas kernels, inverse_transform(): pl.pallas_call(inverse_kernel, grid=(rows // step,), in_specs=[pl.BlockSp...  15 us
  transfers between devices with their start and end apart: 36, of which 24 were waited for; matrix products, arithmetic and copies ran while one was open for 6% of the time, Pallas kernels for 11%

profile of v8, /device:TPU:1, one launch (start us, length us, event | category | flops | bytes accessed | tf_op | source)
XLA Modules:
  0.0 351.7 jit_solution(16048189140883844388)
XLA Ops:
  8.4 9.7 %forward_transform.2 = bf16[16,15,32,384]{3,2,1,0:T(8,128)(2,1)} custom-call(f32[15]{0:T(128)} %sine_multiply_fusion.1.weights_ref, bf16[15,480,384]{2,1,0:T(8,128)(2,1)} %bitcast.80, f32[1,384]{1,0:T(1,128)} %broadcast_in_dim.46.gain_ref, bf16[512,480]{1,0:T(8,128)(2,1)} %constant.250.table_ref), custom_call_target="tpu_custom_call" | custom-call | flops 137438953472 | bytes 15728640 | tf_op jit(solution)/shard_map/forward_transform/pallas_call | solution.py:134
  18.0 7.7 %all-to-all-start = ((bf16[16,15,32,384]{3,2,1,0:T(8,128)(2,1)}), bf16[16,15,32,384]{3,2,1,0:T(8,128)(2,1)}, u32[]{:S(2)}, u32[]{:S(2)}) async-start(bf16[16,15,32,384]{3,2,1,0:T(8,128)(2,1)} %forward_transform.2), calls=%async_computation | async-start | bytes 11796480 | tf_op jit(solution)/shard_map/all_to_all | solution.py:511
  31.5 7.7 %collective-permute-start.1 = (bf16[976,384]{1,0:T(8,128)(2,1)S(1)}, bf16[976,384]{1,0:T(8,128)(2,1)S(1)}, u32[]{:S(2)}, u32[]{:S(2)}) collective-permute-start(bf16[976,384]{1,0:T(8,128)(2,1)S(1)} %get-tuple-element.54), channel_id=1, source_target_pairs={{0,160},{1,161},{2,162},{3,163},{4,164},{5,165},{6,166},{7,167},{8... | collective-permute-start | bytes 2248712 | tf_op jit(solution)/shard_map/ppermute | solution.py:407
  57.3 8.5 %collective-permute-done.2 = bf16[976,384]{1,0:T(8,128)(2,1)S(1)} collective-permute-done((bf16[976,384]{1,0:T(8,128)(2,1)}, bf16[976,384]{1,0:T(8,128)(2,1)S(1)}, u32[]{:S(2)}, u32[]{:S(2)}) %collective-permute-start.2) | collective-permute-done | bytes 749600 | tf_op jit(solution)/shard_map/ppermute | solution.py:407
  65.8 5.5 %collective-permute-done.3 = bf16[976,384]{1,0:T(8,128)(2,1)S(1)} collective-permute-done((bf16[976,384]{1,0:T(8,128)(2,1)}, bf16[976,384]{1,0:T(8,128)(2,1)S(1)}, u32[]{:S(2)}, u32[]{:S(2)}) %collective-permute-start.3) | collective-permute-done | bytes 749600 | tf_op jit(solution)/shard_map/ppermute | solution.py:407
  71.3 10.6 %collective-permute-done.4 = bf16[976,384]{1,0:T(8,128)(2,1)} collective-permute-done((bf16[976,384]{1,0:T(8,128)(2,1)}, bf16[976,384]{1,0:T(8,128)(2,1)}, u32[]{:S(2)}, u32[]{:S(2)}) %collective-permute-start.4) | collective-permute-done | bytes 749600 | tf_op jit(solution)/shard_map/ppermute | solution.py:407
  81.9 5.5 %collective-permute-done.5 = bf16[976,384]{1,0:T(8,128)(2,1)} collective-permute-done((bf16[976,384]{1,0:T(8,128)(2,1)}, bf16[976,384]{1,0:T(8,128)(2,1)}, u32[]{:S(2)}, u32[]{:S(2)}) %collective-permute-start.5) | collective-permute-done | bytes 749600 | tf_op jit(solution)/shard_map/ppermute | solution.py:407
  87.4 10.6 %collective-permute-done.6 = bf16[976,384]{1,0:T(8,128)(2,1)} collective-permute-done((bf16[976,384]{1,0:T(8,128)(2,1)}, bf16[976,384]{1,0:T(8,128)(2,1)}, u32[]{:S(2)}, u32[]{:S(2)}) %collective-permute-start.6) | collective-permute-done | bytes 749600 | tf_op jit(solution)/shard_map/ppermute | solution.py:407
  100.7 14.7 %collective-permute-done.7 = bf16[976,384]{1,0:T(8,128)(2,1)S(1)} collective-permute-done((bf16[976,384]{1,0:T(8,128)(2,1)S(1)}, bf16[976,384]{1,0:T(8,128)(2,1)S(1)}, u32[]{:S(2)}, u32[]{:S(2)}) %collective-permute-start.7) | collective-permute-done | bytes 749600 | tf_op jit(solution)/shard_map/ppermute | solution.py:453
  128.0 18.8 %spectral_pass.1 = bf16[240,32,384]{2,1,0:T(8,128)(2,1)} custom-call(s32[1]{0:T(128)} %bitcast.2.band_ref, bf16[240,32,384]{2,1,0:T(8,128)(2,1)} %bitcast.18.moved_ref, bf16[16,15,240,240]{3,2,1,0:T(8,128)(2,1)} %constant.252.legendre_ref, f32[240,1]{1,0:T(8,128)} %copy.23.gain_ref, bf16[768,768]{1,0:T(8,128)(2,1)} %maximum_maximum_fusion.mixing_ref, ...), custom_call_target="tpu_custom_call" | custom-call | flops 8589934592 | bytes 14680064 | tf_op jit(solution)/shard_map/spectral_pass/pallas_call | solution.py:256
  149.2 7.0 %all-to-all-start.2 = ((bf16[16,15,4,384]{3,2,1,0:T(4,128)(2,1)}), bf16[16,15,4,384]{3,2,1,0:T(4,128)(2,1)S(1)}, u32[]{:S(2)}, u32[]{:S(2)}) async-start(bf16[16,15,4,384]{3,2,1,0:T(4,128)(2,1)} %slice.118), calls=%async_computation.2 | async-start | bytes 1474560 | tf_op jit(solution)/shard_map/all_to_all | solution.py:536
  158.6 10.0 %all-to-all-done.2 = bf16[16,15,4,384]{3,2,1,0:T(4,128)(2,1)S(1)} async-done(((bf16[16,15,4,384]{3,2,1,0:T(4,128)(2,1)}), bf16[16,15,4,384]{3,2,1,0:T(4,128)(2,1)S(1)}, u32[]{:S(2)}, u32[]{:S(2)}) %all-to-all-start.2) | async-done | bytes 737312 | tf_op jit(solution)/shard_map/all_to_all | solution.py:536
  170.4 4.8 %shared_spectral_pass.1 = (bf16[2,240,384]{2,1,0:T(8,128)(2,1)}, bf16[2,240,384]{2,1,0:T(8,128)(2,1)}) custom-call(s32[2]{0:T(128)} %pad_add_fusion.place_ref, bf16[4,240,384]{2,1,0:T(8,128)(2,1)} %bitcast.78, bf16[4,240,384]{2,1,0:T(8,128)(2,1)} %bitcast.79, bf16[16,15,240,240]{3,2,1,0:T(8,128)(2,1)} %constant.252.legendre_ref, f32[240,1]{1,0:T(8,128)} %copy.26.gain_ref, ...), custom_call_target="tpu_custom_call" | custom-call | flops 1073741824 | bytes 4194304 | tf_op jit(solution)/shard_map/shared_spectral_pass/pallas_call | solution.py:176
  176.7 15.8 %all_to_all.30 = bf16[16,15,4,384]{3,2,1,0:T(4,128)(2,1)S(1)} all-to-all(bf16[16,15,4,384]{3,2,1,0:T(4,128)(2,1)S(1)} %bitcast.90), channel_id=1, replica_groups=mesh['member'=16,'band'=16] {'band'}, dimensions={0} | all-to-all | bytes 1474560 | tf_op jit(solution)/shard_map/all_to_all | solution.py:546
  192.5 5.2 %all-to-all-start.4 = ((bf16[16,15,32,384]{3,2,1,0:T(8,128)(2,1)}), bf16[16,15,32,384]{3,2,1,0:T(8,128)(2,1)}, u32[]{:S(2)}, u32[]{:S(2)}) async-start(bf16[16,15,32,384]{3,2,1,0:T(8,128)(2,1)} %bitcast.74), calls=%async_computation.4 | async-start | bytes 11796480 | tf_op jit(solution)/shard_map/all_to_all | solution.py:554
  231.3 5.3 %collective-permute-start.16 = (bf16[1,240,384]{2,1,0:T(8,128)(2,1)}, bf16[1,240,384]{2,1,0:T(8,128)(2,1)S(1)}, u32[]{:S(2)}, u32[]{:S(2)}) collective-permute-start(bf16[1,240,384]{2,1,0:T(8,128)(2,1)} %get-tuple-element.46), channel_id=1, source_target_pairs={{0,32},{32,64},{64,96},{96,128},{128,160},{160,192},{192,224},{224... | collective-permute-start | bytes 552968 | tf_op jit(solution)/shard_map/ppermute | solution.py:439
  256.6 4.8 %collective-permute-done.22 = bf16[1,240,384]{2,1,0:T(8,128)(2,1)S(1)} collective-permute-done((bf16[1,240,384]{2,1,0:T(8,128)(2,1)S(1)}, bf16[1,240,384]{2,1,0:T(8,128)(2,1)S(1)}, u32[]{:S(2)}, u32[]{:S(2)}) %collective-permute-start.22) | collective-permute-done | bytes 184352 | tf_op jit(solution)/shard_map/ppermute | solution.py:439
  267.1 5.2 %collective-permute-done.24 = bf16[1,240,384]{2,1,0:T(8,128)(2,1)S(1)} collective-permute-done((bf16[1,240,384]{2,1,0:T(8,128)(2,1)S(1)}, bf16[1,240,384]{2,1,0:T(8,128)(2,1)S(1)}, u32[]{:S(2)}, u32[]{:S(2)}) %collective-permute-start.24) | collective-permute-done | bytes 184352 | tf_op jit(solution)/shard_map/ppermute | solution.py:439
  277.9 5.5 %collective-permute-done.26 = bf16[1,240,384]{2,1,0:T(8,128)(2,1)S(1)} collective-permute-done((bf16[1,240,384]{2,1,0:T(8,128)(2,1)S(1)}, bf16[1,240,384]{2,1,0:T(8,128)(2,1)S(1)}, u32[]{:S(2)}, u32[]{:S(2)}) %collective-permute-start.26) | collective-permute-done | bytes 184352 | tf_op jit(solution)/shard_map/ppermute | solution.py:439
  288.1 6.7 %collective-permute-done.28 = bf16[1,240,384]{2,1,0:T(8,128)(2,1)S(1)} collective-permute-done((bf16[1,240,384]{2,1,0:T(8,128)(2,1)S(1)}, bf16[1,240,384]{2,1,0:T(8,128)(2,1)S(1)}, u32[]{:S(2)}, u32[]{:S(2)}) %collective-permute-start.28) | collective-permute-done | bytes 184352 | tf_op jit(solution)/shard_map/ppermute | solution.py:439
  294.9 11.7 %inverse_transform.3.own_ref = bf16[15,480,384]{2,1,0:T(8,128)(2,1)} custom-call(bf16[16,15,32,384]{3,2,1,0:T(8,128)(2,1)} %all-to-all-done.4.spatial_ref, bf16[15,480,384]{2,1,0:T(8,128)(2,1)} %bitcast.83, bf16[480,512]{1,0:T(8,128)(2,1)} %constant.255.table_ref), custom_call_target="tpu_custom_call" | custom-call | flops 274877906944 | bytes 15728640 | tf_op jit(solution)/shard_map/inverse_transform/pallas_call | solution.py:291
  306.7 6.9 %spread_sums.1 = f32[16,8,128]{2,1,0:T(8,128)} custom-call(f32[15]{0:T(128)} %sine_multiply_fusion.1.weights_ref, bf16[15,480,384]{2,1,0:T(8,128)(2,1)} %inverse_transform.3.own_ref, bf16[16,240,384]{2,1,0:T(8,128)(2,1)} %all-gather.2.cloned.1.call-done.refs_0_.refs_1_.refs_2_, bf16[16,240,384]{2,1,0:T(8,128)(2,1)} %all-gather.2.cloned.1.call-done.refs_0_.refs_1_.refs_2_, ...), custom_call_target="tpu_custom_call" | custom-call | flops 9437184 | bytes 11534336 | tf_op jit(solution)/shard_map/spread_sums/pallas_call | solution.py:347
  313.5 14.5 %all-to-all-start.5 = ((f32[16,8,128]{2,1,0:T(8,128)}), f32[16,8,128]{2,1,0:T(8,128)S(1)}, u32[]{:S(2)}, u32[]{:S(2)}) async-start(f32[16,8,128]{2,1,0:T(8,128)} %spread_sums.1), calls=%async_computation.5 | async-start | bytes 131072 | tf_op jit(solution)/shard_map/all_to_all | solution.py:567
  334.5 10.0 %rescaled.1 = bf16[15,480,384]{2,1,0:T(8,128)(2,1)} custom-call(f32[1]{0:T(128)} %bitcast.1.target_ref, f32[16,8,128]{2,1,0:T(8,128)} %copy-done.7, bf16[15,480,384]{2,1,0:T(8,128)(2,1)} %inverse_transform.3.own_ref, bf16[16,240,384]{2,1,0:T(8,128)(2,1)} %all-gather.2.cloned.1.call-done.refs_0_.refs_1_.refs_2_, ...), custom_call_target="tpu_custom_call" | custom-call | flops 9437184 | bytes 17825792 | tf_op jit(solution)/shard_map/rescaled/pallas_call | solution.py:372
  (146 shorter events, 123.0 us)
Async XLA Ops:
  18.0 101.8 %all-to-all-start = ((bf16[16,15,32,384]{3,2,1,0:T(8,128)(2,1)}), bf16[16,15,32,384]{3,2,1,0:T(8,128)(2,1)}, u32[]{:S(2)}, u32[]{:S(2)}) async-start(bf16[16,15,32,384]{3,2,1,0:T(8,128)(2,1)} %forward_transform.2), calls=%async_computation | async-start | bytes 11796480 | tf_op jit(solution)/shard_map/all_to_all | solution.py:511
  31.5 23.7 %collective-permute-start.1 = (bf16[976,384]{1,0:T(8,128)(2,1)S(1)}, bf16[976,384]{1,0:T(8,128)(2,1)S(1)}, u32[]{:S(2)}, u32[]{:S(2)}) collective-permute-start(bf16[976,384]{1,0:T(8,128)(2,1)S(1)} %get-tuple-element.54), channel_id=1, source_target_pairs={{0,160},{1,161},{2,162},{3,163},{4,164},{5,165},{6,166},{7,167},{8... | collective-permute-start | bytes 2248712 | tf_op jit(solution)/shard_map/ppermute | solution.py:407
  41.6 24.2 %collective-permute-start.2 = (bf16[976,384]{1,0:T(8,128)(2,1)}, bf16[976,384]{1,0:T(8,128)(2,1)S(1)}, u32[]{:S(2)}, u32[]{:S(2)}) collective-permute-start(bf16[976,384]{1,0:T(8,128)(2,1)} %get-tuple-element.50), channel_id=1, source_target_pairs={{0,96},{1,97},{2,98},{3,99},{4,100},{5,101},{6,102},{7,103},{8,104... | collective-permute-start | bytes 2248712 | tf_op jit(solution)/shard_map/ppermute | solution.py:407
  42.9 28.4 %collective-permute-start.3 = (bf16[976,384]{1,0:T(8,128)(2,1)}, bf16[976,384]{1,0:T(8,128)(2,1)S(1)}, u32[]{:S(2)}, u32[]{:S(2)}) collective-permute-start(bf16[976,384]{1,0:T(8,128)(2,1)} %get-tuple-element.51), channel_id=1, source_target_pairs={{0,192},{1,193},{2,194},{3,195},{4,196},{5,197},{6,198},{7,199},{8... | collective-permute-start | bytes 2248712 | tf_op jit(solution)/shard_map/ppermute | solution.py:407
  44.3 37.6 %collective-permute-start.4 = (bf16[976,384]{1,0:T(8,128)(2,1)}, bf16[976,384]{1,0:T(8,128)(2,1)}, u32[]{:S(2)}, u32[]{:S(2)}) collective-permute-start(bf16[976,384]{1,0:T(8,128)(2,1)} %get-tuple-element.52), channel_id=1, source_target_pairs={{0,64},{1,65},{2,66},{3,67},{4,68},{5,69},{6,70},{7,71},{8,72},{9,... | collective-permute-start | bytes 2248712 | tf_op jit(solution)/shard_map/ppermute | solution.py:407
  49.7 37.7 %collective-permute-start.5 = (bf16[976,384]{1,0:T(8,128)(2,1)}, bf16[976,384]{1,0:T(8,128)(2,1)}, u32[]{:S(2)}, u32[]{:S(2)}) collective-permute-start(bf16[976,384]{1,0:T(8,128)(2,1)} %get-tuple-element.53), channel_id=1, source_target_pairs={{0,224},{1,225},{2,226},{3,227},{4,228},{5,229},{6,230},{7,231},{8... | collective-permute-start | bytes 2248712 | tf_op jit(solution)/shard_map/ppermute | solution.py:407
  55.1 42.8 %collective-permute-start.6 = (bf16[976,384]{1,0:T(8,128)(2,1)}, bf16[976,384]{1,0:T(8,128)(2,1)}, u32[]{:S(2)}, u32[]{:S(2)}) collective-permute-start(bf16[976,384]{1,0:T(8,128)(2,1)} %get-tuple-element.49), channel_id=1, source_target_pairs={{0,32},{1,33},{2,34},{3,35},{4,36},{5,37},{6,38},{7,39},{8,40},{9,... | collective-permute-start | bytes 2248712 | tf_op jit(solution)/shard_map/ppermute | solution.py:407
  98.8 16.7 %collective-permute-start.7 = (bf16[976,384]{1,0:T(8,128)(2,1)S(1)}, bf16[976,384]{1,0:T(8,128)(2,1)S(1)}, u32[]{:S(2)}, u32[]{:S(2)}) collective-permute-start(bf16[976,384]{1,0:T(8,128)(2,1)S(1)} %fusion.6), channel_id=1, source_target_pairs={{0,24},{1,25},{2,26},{3,27},{4,28},{5,29},{6,30},{7,31},{8,16},{9,... | collective-permute-start | bytes 2248712 | tf_op jit(solution)/shard_map/ppermute | solution.py:453
  119.8 27.0 %all-to-all-start.1 = ((bf16[8,2,64,384]{3,2,1,0:T(8,128)(2,1)}), bf16[8,2,64,384]{3,2,1,0:T(8,128)(2,1)S(1)}, u32[]{:S(2)}, u32[]{:S(2)}) async-start(bf16[8,2,64,384]{3,2,1,0:T(8,128)(2,1)} %forward_transform.3), calls=%async_computation.1 | async-start | bytes 1572864 | tf_op jit(solution)/shard_map/all_to_all | solution.py:415
  126.4 31.2 %collective-permute-start.8 = (bf16[2,480,384]{2,1,0:T(8,128)(2,1)S(1)}, bf16[2,480,384]{2,1,0:T(8,128)(2,1)}, u32[]{:S(2)}, u32[]{:S(2)}) collective-permute-start(bf16[2,480,384]{2,1,0:T(8,128)(2,1)S(1)} %bitcast.76), channel_id=1, source_target_pairs={{16,24},{17,25},{18,26},{19,27},{20,28},{21,29},{22,30},{23,31},{2... | collective-permute-start | bytes 2211848 | tf_op jit(solution)/shard_map/ppermute | solution.py:464
  149.2 19.4 %all-to-all-start.2 = ((bf16[16,15,4,384]{3,2,1,0:T(4,128)(2,1)}), bf16[16,15,4,384]{3,2,1,0:T(4,128)(2,1)S(1)}, u32[]{:S(2)}, u32[]{:S(2)}) async-start(bf16[16,15,4,384]{3,2,1,0:T(4,128)(2,1)} %slice.118), calls=%async_computation.2 | async-start | bytes 1474560 | tf_op jit(solution)/shard_map/all_to_all | solution.py:536
  192.5 102.5 %all-to-all-start.4 = ((bf16[16,15,32,384]{3,2,1,0:T(8,128)(2,1)}), bf16[16,15,32,384]{3,2,1,0:T(8,128)(2,1)}, u32[]{:S(2)}, u32[]{:S(2)}) async-start(bf16[16,15,32,384]{3,2,1,0:T(8,128)(2,1)} %bitcast.74), calls=%async_computation.4 | async-start | bytes 11796480 | tf_op jit(solution)/shard_map/all_to_all | solution.py:554
  197.7 109.0 %all-gather.2.cloned.1.call-start = ((), (), s32[]{:S(2)}) async-start(), calls=%async_computation.6 | async-start | bytes 3317760 | tf_op jit(solution)/shard_map/all_gather | solution.py:562
  207.5 12.3 %collective-permute-start.11 = (bf16[2,64,384]{2,1,0:T(8,128)(2,1)S(1)}, bf16[2,64,384]{2,1,0:T(8,128)(2,1)S(1)}, u32[]{:S(2)}, u32[]{:S(2)}) collective-permute-start(bf16[2,64,384]{2,1,0:T(8,128)(2,1)S(1)} %get-tuple-element.40), channel_id=1, source_target_pairs={{0,64},{32,96},{64,128},{96,160},{128,192},{160,224},{192,0},{224,... | collective-permute-start | bytes 294920 | tf_op jit(solution)/shard_map/ppermute | solution.py:426
  207.8 12.1 %collective-permute-start.12 = (bf16[2,64,384]{2,1,0:T(8,128)(2,1)S(1)}, bf16[2,64,384]{2,1,0:T(8,128)(2,1)S(1)}, u32[]{:S(2)}, u32[]{:S(2)}) collective-permute-start(bf16[2,64,384]{2,1,0:T(8,128)(2,1)S(1)} %get-tuple-element.39), channel_id=1, source_target_pairs={{0,192},{32,224},{64,0},{96,32},{128,64},{160,96},{192,128},{224,1... | collective-permute-start | bytes 294920 | tf_op jit(solution)/shard_map/ppermute | solution.py:426
  211.2 10.4 %collective-permute-start.13 = (bf16[2,64,384]{2,1,0:T(8,128)(2,1)S(1)}, bf16[2,64,384]{2,1,0:T(8,128)(2,1)S(1)}, u32[]{:S(2)}, u32[]{:S(2)}) collective-permute-start(bf16[2,64,384]{2,1,0:T(8,128)(2,1)S(1)} %get-tuple-element.38), channel_id=1, source_target_pairs={{0,96},{32,128},{64,160},{96,192},{128,224},{160,0},{192,32},{224,... | collective-permute-start | bytes 294920 | tf_op jit(solution)/shard_map/ppermute | solution.py:426
  253.0 10.5 %collective-permute-start.23 = (bf16[1,240,384]{2,1,0:T(8,128)(2,1)S(1)}, bf16[1,240,384]{2,1,0:T(8,128)(2,1)S(1)}, u32[]{:S(2)}, u32[]{:S(2)}) collective-permute-start(bf16[1,240,384]{2,1,0:T(8,128)(2,1)S(1)} %collective-permute-done.21), channel_id=1, source_target_pairs={{32,0},{64,32},{96,64},{128,96},{160,128},{192,160},{224,192},{0,2... | collective-permute-start | bytes 552968 | tf_op jit(solution)/shard_map/ppermute | solution.py:440
  261.3 10.9 %collective-permute-start.24 = (bf16[1,240,384]{2,1,0:T(8,128)(2,1)S(1)}, bf16[1,240,384]{2,1,0:T(8,128)(2,1)S(1)}, u32[]{:S(2)}, u32[]{:S(2)}) collective-permute-start(bf16[1,240,384]{2,1,0:T(8,128)(2,1)S(1)} %collective-permute-done.22), channel_id=1, source_target_pairs={{0,32},{32,64},{64,96},{96,128},{128,160},{160,192},{192,224},{224... | collective-permute-start | bytes 552968 | tf_op jit(solution)/shard_map/ppermute | solution.py:439
  263.5 10.8 %collective-permute-start.25 = (bf16[1,240,384]{2,1,0:T(8,128)(2,1)S(1)}, bf16[1,240,384]{2,1,0:T(8,128)(2,1)S(1)}, u32[]{:S(2)}, u32[]{:S(2)}) collective-permute-start(bf16[1,240,384]{2,1,0:T(8,128)(2,1)S(1)} %collective-permute-done.23), channel_id=1, source_target_pairs={{32,0},{64,32},{96,64},{128,96},{160,128},{192,160},{224,192},{0,2... | collective-permute-start | bytes 552968 | tf_op jit(solution)/shard_map/ppermute | solution.py:440
  272.2 11.2 %collective-permute-start.26 = (bf16[1,240,384]{2,1,0:T(8,128)(2,1)S(1)}, bf16[1,240,384]{2,1,0:T(8,128)(2,1)S(1)}, u32[]{:S(2)}, u32[]{:S(2)}) collective-permute-start(bf16[1,240,384]{2,1,0:T(8,128)(2,1)S(1)} %collective-permute-done.24), channel_id=1, source_target_pairs={{0,32},{32,64},{64,96},{96,128},{128,160},{160,192},{192,224},{224... | collective-permute-start | bytes 552968 | tf_op jit(solution)/shard_map/ppermute | solution.py:439
  274.3 10.2 %collective-permute-start.27 = (bf16[1,240,384]{2,1,0:T(8,128)(2,1)S(1)}, bf16[1,240,384]{2,1,0:T(8,128)(2,1)S(1)}, u32[]{:S(2)}, u32[]{:S(2)}) collective-permute-start(bf16[1,240,384]{2,1,0:T(8,128)(2,1)S(1)} %collective-permute-done.25), channel_id=1, source_target_pairs={{32,0},{64,32},{96,64},{128,96},{160,128},{192,160},{224,192},{0,2... | collective-permute-start | bytes 552968 | tf_op jit(solution)/shard_map/ppermute | solution.py:440
  283.4 11.4 %collective-permute-start.28 = (bf16[1,240,384]{2,1,0:T(8,128)(2,1)S(1)}, bf16[1,240,384]{2,1,0:T(8,128)(2,1)S(1)}, u32[]{:S(2)}, u32[]{:S(2)}) collective-permute-start(bf16[1,240,384]{2,1,0:T(8,128)(2,1)S(1)} %collective-permute-done.26), channel_id=1, source_target_pairs={{0,32},{32,64},{64,96},{96,128},{128,160},{160,192},{192,224},{224... | collective-permute-start | bytes 552968 | tf_op jit(solution)/shard_map/ppermute | solution.py:439
  284.5 10.4 %collective-permute-start.29 = (bf16[1,240,384]{2,1,0:T(8,128)(2,1)S(1)}, bf16[1,240,384]{2,1,0:T(8,128)(2,1)S(1)}, u32[]{:S(2)}, u32[]{:S(2)}) collective-permute-start(bf16[1,240,384]{2,1,0:T(8,128)(2,1)S(1)} %collective-permute-done.27), channel_id=1, source_target_pairs={{32,0},{64,32},{96,64},{128,96},{160,128},{192,160},{224,192},{0,2... | collective-permute-start | bytes 552968 | tf_op jit(solution)/shard_map/ppermute | solution.py:440
  313.5 20.3 %all-to-all-start.5 = ((f32[16,8,128]{2,1,0:T(8,128)}), f32[16,8,128]{2,1,0:T(8,128)S(1)}, u32[]{:S(2)}, u32[]{:S(2)}) async-start(f32[16,8,128]{2,1,0:T(8,128)} %spread_sums.1), calls=%async_computation.5 | async-start | bytes 131072 | tf_op jit(solution)/shard_map/all_to_all | solution.py:567
  (22 other events, 195.5 us)
Sparse Core Ops, SparseCore 0:
  237.8 59.2 all-gather.1

commit v9 on v7

--- a/solution.py
+++ b/solution.py
@@ -22,7 +22,7 @@
 SHIFT = 3
 BOTH_WAYS = (1, 7, 2, 6, 3, 5, 4)
 RINGS = [[2 * z + h for z in range(DEPTH)] for h in range(2)]
-STEP = 3
+STEP = 5
 TOTAL_WEIGHT = float(np.sum(np.sin((np.arange(H) + 0.5) * np.pi / H)) * np.pi / H * E * W)
 MIB = 1 << 20
 
@@ -121,7 +121,7 @@
         x = x_ref[j].astype(jnp.float32)
         centred = x - jnp.mean(x, axis=1, keepdims=True)
         variance = jnp.mean(jnp.square(centred), axis=1, keepdims=True)
-        normed = (centred * lax.rsqrt(variance + 1e-05) * gain_ref[...]).astype(jnp.bfloat16)
+        normed = (centred * lax.rsqrt(variance + 1e-05) * gain_ref[...][None, :]).astype(jnp.bfloat16)
         sums = jnp.dot(table_ref[...], normed, preferred_element_type=jnp.float32)
         sums = (sums * weights_ref[pl.program_id(0) * rows + j]).astype(jnp.bfloat16)
         out_ref[:, j] = sums.reshape(out_ref.shape[0], out_ref.shape[2], E)
@@ -136,7 +136,7 @@
         in_specs=[
             pl.BlockSpec(memory_space=pltpu.SMEM),
             pl.BlockSpec((step, W, E), lambda j: (j, 0, 0)),
-            pl.BlockSpec((1, E), lambda j: (0, 0)),
+            pl.BlockSpec((E,), lambda j: (0,)),
             pl.BlockSpec((BANDS * SLOTS, W), lambda j: (0, 0)),
         ],
         out_specs=pl.BlockSpec((groups, step, size, E), lambda j: (0, j, 0, 0)),
@@ -484,7 +484,7 @@
     crossed = member % 2 == 1
     control_band = jnp.where(crossed, (band_index + BANDS // 2) % BANDS, band_index)
 
-    fourier = forward_transform(x, norm_gain[None, :], weights, rounded(ahead_np), BANDS, STEP, 1 << 37)
+    fourier = forward_transform(x, norm_gain, weights, rounded(ahead_np), BANDS, STEP, 1 << 37)
     moved = lax.all_to_all(fourier, "band", split_axis=0, concat_axis=0, tiled=True)
 
     control_parts = across(
@@ -495,7 +495,7 @@
     control_first = control_band * ROWS + 2 * ((z + SHIFT) % DEPTH)
     control_weights = latitude_weights(control_first + jnp.arange(2, dtype=jnp.int32))
     control_fourier = forward_transform(
-        control_x, norm_gain[None, :], control_weights, rounded(shared_ahead_np), DEPTH, 2, 1 << 29
+        control_x, norm_gain, control_weights, rounded(shared_ahead_np), DEPTH, 2, 1 << 29
     )
     moved, control_fourier = lax.optimization_barrier((moved, control_fourier))
     control_fourier = exchanged_along_z(control_fourier).reshape(DEPTH, 2, BANDS, 4, E)

time: 339 us -> 336 us (level)
  no operation moved by 1% of the time
where the time goes in v9:
time: 336 us; the launch traced here: 335 us
  waiting for transfers between devices  147 us (44%)
  starting transfers between devices  68.5 us (20%)
  Pallas kernels  65.2 us (19%)
  blocking collectives  15.8 us (5%)
  between operations  15.7 us (5%)
  local copies, waits for them, and re-layouts  12.9 us (4%)
  other arithmetic  9.91 us (3%)
    all_to_all x1, waiting for transfers between devices, shards(): lax.all_to_all(returned.reshape(BANDS, ROWS, SLOTS, E), 'band', split_axi...  47.5 us
    ppermute x7, waiting for transfers between devices, scattered(): arrived = lax.ppermute(piece(z), 'member', [(0, 2 * z)])  40.9 us
    pallas_call x1, Pallas kernels, spectral_pass(): pl.pallas_call(spectral_kernel, grid_spec=pltpu.PrefetchScalarGridSpec(nu...  18.8 us
    ppermute x7, starting transfers between devices, scattered(): arrived = lax.ppermute(piece(z), 'member', [(0, 2 * z)])  18.1 us
    all_to_all x1, blocking collectives, shards(): lax.all_to_all(control_spatial.transpose(1, 0, 2).reshape(BANDS, ROWS, 4,...  15.8 us
    all_gather x1, waiting for transfers between devices, shards(): lax.all_gather(control, 'member', tiled=True, axis_index_groups=RINGS)  15.6 us
    ppermute x7, waiting for transfers between devices, permuted_along_z(): arrived = lax.ppermute(block, 'member', pairs)  14.1 us
    ppermute x1, waiting for transfers between devices, across(): arrived = lax.ppermute(value, ('member', 'band'), pairs)  13.8 us
  transfers between devices with their start and end apart: 22, of which 12 were waited for; matrix products, arithmetic and copies ran while one was open for 5% of the time, Pallas kernels for 11%

profile of v9, /device:TPU:1, one launch (start us, length us, event | category | flops | bytes accessed | tf_op | source)
XLA Modules:
  0.0 334.7 jit_solution(4427992741618172332)
XLA Ops:
  7.2 8.9 %forward_transform.2 = bf16[16,15,32,384]{3,2,1,0:T(8,128)(2,1)} custom-call(f32[15]{0:T(128)} %sine_multiply_fusion.1.weights_ref, bf16[15,480,384]{2,1,0:T(8,128)(2,1)} %bitcast.80, f32[384]{0:T(512)} %gain_ref.3, bf16[512,480]{1,0:T(8,128)(2,1)} %constant.211.table_ref), custom_call_target="tpu_custom_call" | custom-call | flops 137438953472 | bytes 15728640 | tf_op jit(solution)/shard_map/forward_transform/pallas_call | solution.py:133
  16.1 7.7 %all-to-all-start = ((bf16[16,15,32,384]{3,2,1,0:T(8,128)(2,1)}), bf16[16,15,32,384]{3,2,1,0:T(8,128)(2,1)}, u32[]{:S(2)}, u32[]{:S(2)}) async-start(bf16[16,15,32,384]{3,2,1,0:T(8,128)(2,1)} %forward_transform.2), calls=%async_computation | async-start | bytes 11796480 | tf_op jit(solution)/shard_map/all_to_all | solution.py:488
  33.5 6.0 %collective-permute-start = (bf16[496,384]{1,0:T(8,128)(2,1)S(1)}, bf16[496,384]{1,0:T(8,128)(2,1)S(1)}, u32[]{:S(2)}, u32[]{:S(2)}) collective-permute-start(bf16[496,384]{1,0:T(8,128)(2,1)S(1)} %pad_maximum_fusion.7), channel_id=1, source_target_pairs={{0,128},{1,129},{2,130},{3,131},{4,132},{5,133},{6,134},{7,135},{8... | collective-permute-start | bytes 1142792 | tf_op jit(solution)/shard_map/ppermute | solution.py:399
  44.4 12.2 %collective-permute-done = bf16[496,384]{1,0:T(8,128)(2,1)S(1)} collective-permute-done((bf16[496,384]{1,0:T(8,128)(2,1)S(1)}, bf16[496,384]{1,0:T(8,128)(2,1)S(1)}, u32[]{:S(2)}, u32[]{:S(2)}) %collective-permute-start) | collective-permute-done | bytes 380960 | tf_op jit(solution)/shard_map/ppermute | solution.py:399
  61.0 11.8 %collective-permute-done.2 = bf16[976,384]{1,0:T(8,128)(2,1)S(1)} collective-permute-done((bf16[976,384]{1,0:T(8,128)(2,1)}, bf16[976,384]{1,0:T(8,128)(2,1)S(1)}, u32[]{:S(2)}, u32[]{:S(2)}) %collective-permute-start.2) | collective-permute-done | bytes 749600 | tf_op jit(solution)/shard_map/ppermute | solution.py:399
  72.7 16.1 %collective-permute-done.4 = bf16[976,384]{1,0:T(8,128)(2,1)} collective-permute-done((bf16[976,384]{1,0:T(8,128)(2,1)}, bf16[976,384]{1,0:T(8,128)(2,1)}, u32[]{:S(2)}, u32[]{:S(2)}) %collective-permute-start.4) | collective-permute-done | bytes 749600 | tf_op jit(solution)/shard_map/ppermute | solution.py:399
  92.5 13.8 %collective-permute-done.7 = bf16[976,384]{1,0:T(8,128)(2,1)S(1)} collective-permute-done((bf16[976,384]{1,0:T(8,128)(2,1)S(1)}, bf16[976,384]{1,0:T(8,128)(2,1)S(1)}, u32[]{:S(2)}, u32[]{:S(2)}) %collective-permute-start.7) | collective-permute-done | bytes 749600 | tf_op jit(solution)/shard_map/ppermute | solution.py:430
  110.7 7.7 %all-to-all-start.1 = ((bf16[8,2,64,384]{3,2,1,0:T(8,128)(2,1)}), bf16[8,2,64,384]{3,2,1,0:T(8,128)(2,1)S(1)}, u32[]{:S(2)}, u32[]{:S(2)}) async-start(bf16[8,2,64,384]{3,2,1,0:T(8,128)(2,1)} %forward_transform.3), calls=%async_computation.1 | async-start | bytes 1572864 | tf_op jit(solution)/shard_map/all_to_all | solution.py:407
  121.9 18.8 %spectral_pass.1 = bf16[240,32,384]{2,1,0:T(8,128)(2,1)} custom-call(s32[1]{0:T(128)} %bitcast.2.band_ref, bf16[240,32,384]{2,1,0:T(8,128)(2,1)} %bitcast.18.moved_ref, bf16[16,15,240,240]{3,2,1,0:T(8,128)(2,1)} %constant.213.legendre_ref, f32[240,1]{1,0:T(8,128)} %copy.23.gain_ref, bf16[768,768]{1,0:T(8,128)(2,1)} %maximum_maximum_fusion.mixing_ref, ...), custom_call_target="tpu_custom_call" | custom-call | flops 8589934592 | bytes 14680064 | tf_op jit(solution)/shard_map/spectral_pass/pallas_call | solution.py:255
  143.1 8.4 %all-to-all-start.2 = ((bf16[16,15,4,384]{3,2,1,0:T(4,128)(2,1)}), bf16[16,15,4,384]{3,2,1,0:T(4,128)(2,1)S(1)}, u32[]{:S(2)}, u32[]{:S(2)}) async-start(bf16[16,15,4,384]{3,2,1,0:T(4,128)(2,1)} %slice.100), calls=%async_computation.2 | async-start | bytes 1474560 | tf_op jit(solution)/shard_map/all_to_all | solution.py:513
  153.9 10.0 %all-to-all-done.2 = bf16[16,15,4,384]{3,2,1,0:T(4,128)(2,1)S(1)} async-done(((bf16[16,15,4,384]{3,2,1,0:T(4,128)(2,1)}), bf16[16,15,4,384]{3,2,1,0:T(4,128)(2,1)S(1)}, u32[]{:S(2)}, u32[]{:S(2)}) %all-to-all-start.2) | async-done | bytes 737312 | tf_op jit(solution)/shard_map/all_to_all | solution.py:513
  165.7 4.8 %shared_spectral_pass.1 = (bf16[2,240,384]{2,1,0:T(8,128)(2,1)}, bf16[2,240,384]{2,1,0:T(8,128)(2,1)}) custom-call(s32[2]{0:T(128)} %pad_add_fusion.place_ref, bf16[4,240,384]{2,1,0:T(8,128)(2,1)} %bitcast.78, bf16[4,240,384]{2,1,0:T(8,128)(2,1)} %bitcast.79, bf16[16,15,240,240]{3,2,1,0:T(8,128)(2,1)} %constant.213.legendre_ref, f32[240,1]{1,0:T(8,128)} %copy.26.gain_ref, ...), custom_call_target="tpu_custom_call" | custom-call | flops 1073741824 | bytes 4194304 | tf_op jit(solution)/shard_map/shared_spectral_pass/pallas_call | solution.py:175
  172.0 15.8 %all_to_all.30 = bf16[16,15,4,384]{3,2,1,0:T(4,128)(2,1)S(1)} all-to-all(bf16[16,15,4,384]{3,2,1,0:T(4,128)(2,1)S(1)} %bitcast.90), channel_id=1, replica_groups=mesh['member'=16,'band'=16] {'band'}, dimensions={0} | all-to-all | bytes 1474560 | tf_op jit(solution)/shard_map/all_to_all | solution.py:523
  187.8 5.2 %all-to-all-start.4 = ((bf16[16,15,32,384]{3,2,1,0:T(8,128)(2,1)}), bf16[16,15,32,384]{3,2,1,0:T(8,128)(2,1)}, u32[]{:S(2)}, u32[]{:S(2)}) async-start(bf16[16,15,32,384]{3,2,1,0:T(8,128)(2,1)} %bitcast.74), calls=%async_computation.4 | async-start | bytes 11796480 | tf_op jit(solution)/shard_map/all_to_all | solution.py:531
  196.0 4.2 %collective-permute-done.9 = bf16[2,64,384]{2,1,0:T(8,128)(2,1)S(1)} collective-permute-done((bf16[2,64,384]{2,1,0:T(8,128)(2,1)S(1)}, bf16[2,64,384]{2,1,0:T(8,128)(2,1)S(1)}, u32[]{:S(2)}, u32[]{:S(2)}) %collective-permute-start.9) | collective-permute-done | bytes 98336 | tf_op jit(solution)/shard_map/ppermute | solution.py:418
  202.3 4.1 %collective-permute-start.15 = (bf16[2,64,384]{2,1,0:T(8,128)(2,1)S(1)}, bf16[2,64,384]{2,1,0:T(8,128)(2,1)S(1)}, u32[]{:S(2)}, u32[]{:S(2)}) collective-permute-start(bf16[2,64,384]{2,1,0:T(8,128)(2,1)S(1)} %get-tuple-element.32), channel_id=1, source_target_pairs={{0,128},{32,160},{64,192},{96,224},{128,0},{160,32},{192,64},{224,... | collective-permute-start | bytes 294920 | tf_op jit(solution)/shard_map/ppermute | solution.py:418
  212.0 8.9 %collective-permute-done.11 = bf16[2,64,384]{2,1,0:T(8,128)(2,1)S(1)} collective-permute-done((bf16[2,64,384]{2,1,0:T(8,128)(2,1)S(1)}, bf16[2,64,384]{2,1,0:T(8,128)(2,1)S(1)}, u32[]{:S(2)}, u32[]{:S(2)}) %collective-permute-start.11) | collective-permute-done | bytes 98336 | tf_op jit(solution)/shard_map/ppermute | solution.py:418
  226.3 47.5 %all-to-all-done.4.spatial_ref = bf16[16,15,32,384]{3,2,1,0:T(8,128)(2,1)} async-done(((bf16[16,15,32,384]{3,2,1,0:T(8,128)(2,1)}), bf16[16,15,32,384]{3,2,1,0:T(8,128)(2,1)}, u32[]{:S(2)}, u32[]{:S(2)}) %all-to-all-start.4) | async-done | bytes 5898272 | tf_op jit(solution)/shard_map/all_to_all | solution.py:531
  273.8 10.3 %inverse_transform.2.own_ref = bf16[15,480,384]{2,1,0:T(8,128)(2,1)} custom-call(bf16[16,15,32,384]{3,2,1,0:T(8,128)(2,1)} %all-to-all-done.4.spatial_ref, bf16[15,480,384]{2,1,0:T(8,128)(2,1)} %bitcast.83, bf16[480,512]{1,0:T(8,128)(2,1)} %constant.215.table_ref), custom_call_target="tpu_custom_call" | custom-call | flops 274877906944 | bytes 15728640 | tf_op jit(solution)/shard_map/inverse_transform/pallas_call | solution.py:290
  284.1 15.6 %all-gather.2.cloned.1.call-done.refs_0_.refs_1_.refs_2_.refs_3_.refs_4_ = bf16[16,480,384]{2,1,0:T(8,128)(2,1)} async-done(((bf16[2,480,384]{2,1,0:T(8,128)(2,1)}), bf16[16,480,384]{2,1,0:T(8,128)(2,1)}) %all-gather.2.cloned.1.call-update) | async-done | bytes 5898256 | tf_op jit(solution)/shard_map/all_gather | solution.py:539
  299.7 6.3 %spread_sums.1 = f32[16,8,128]{2,1,0:T(8,128)} custom-call(f32[15]{0:T(128)} %sine_multiply_fusion.1.weights_ref, bf16[15,480,384]{2,1,0:T(8,128)(2,1)} %inverse_transform.2.own_ref, bf16[16,480,384]{2,1,0:T(8,128)(2,1)} %all-gather.2.cloned.1.call-done.refs_0_.refs_1_.refs_2_.refs_3_.refs_4_, ...), custom_call_target="tpu_custom_call" | custom-call | flops 9437184 | bytes 11534336 | tf_op jit(solution)/shard_map/spread_sums/pallas_call | solution.py:338
  306.0 5.9 %all-to-all-start.5 = ((f32[16,8,128]{2,1,0:T(8,128)}), f32[16,8,128]{2,1,0:T(8,128)S(1)}, u32[]{:S(2)}, u32[]{:S(2)}) async-start(f32[16,8,128]{2,1,0:T(8,128)} %spread_sums.1), calls=%async_computation.5 | async-start | bytes 131072 | tf_op jit(solution)/shard_map/all_to_all | solution.py:542
  313.1 4.6 %all-to-all-done.5.sums_ref = f32[16,8,128]{2,1,0:T(8,128)S(1)} async-done(((f32[16,8,128]{2,1,0:T(8,128)}), f32[16,8,128]{2,1,0:T(8,128)S(1)}, u32[]{:S(2)}, u32[]{:S(2)}) %all-to-all-start.5) | async-done | bytes 65568 | tf_op jit(solution)/shard_map/all_to_all | solution.py:542
  318.3 9.5 %rescaled.1 = bf16[15,480,384]{2,1,0:T(8,128)(2,1)} custom-call(f32[1]{0:T(128)} %bitcast.1.target_ref, f32[16,8,128]{2,1,0:T(8,128)} %copy-done.5, bf16[15,480,384]{2,1,0:T(8,128)(2,1)} %inverse_transform.2.own_ref, bf16[16,480,384]{2,1,0:T(8,128)(2,1)} %all-gather.2.cloned.1.call-done.refs_0_.refs_1_.refs_2_.refs_3_.refs_4_, ...), custom_call_target="tpu_custom_call" | custom-call | flops 9437184 | bytes 17825792 | tf_op jit(solution)/shard_map/rescaled/pallas_call | solution.py:364
  (96 shorter events, 54.9 us)
Async XLA Ops:
  16.1 94.6 %all-to-all-start = ((bf16[16,15,32,384]{3,2,1,0:T(8,128)(2,1)}), bf16[16,15,32,384]{3,2,1,0:T(8,128)(2,1)}, u32[]{:S(2)}, u32[]{:S(2)}) async-start(bf16[16,15,32,384]{3,2,1,0:T(8,128)(2,1)} %forward_transform.2), calls=%async_computation | async-start | bytes 11796480 | tf_op jit(solution)/shard_map/all_to_all | solution.py:488
  29.5 29.2 %collective-permute-start.6 = (bf16[976,384]{1,0:T(8,128)(2,1)S(1)}, bf16[976,384]{1,0:T(8,128)(2,1)S(1)}, u32[]{:S(2)}, u32[]{:S(2)}) collective-permute-start(bf16[976,384]{1,0:T(8,128)(2,1)S(1)} %get-tuple-element.41), channel_id=1, source_target_pairs={{0,32},{1,33},{2,34},{3,35},{4,36},{5,37},{6,38},{7,39},{8,40},{9,... | collective-permute-start | bytes 2248712 | tf_op jit(solution)/shard_map/ppermute | solution.py:399
  33.5 23.0 %collective-permute-start = (bf16[496,384]{1,0:T(8,128)(2,1)S(1)}, bf16[496,384]{1,0:T(8,128)(2,1)S(1)}, u32[]{:S(2)}, u32[]{:S(2)}) collective-permute-start(bf16[496,384]{1,0:T(8,128)(2,1)S(1)} %pad_maximum_fusion.7), channel_id=1, source_target_pairs={{0,128},{1,129},{2,130},{3,131},{4,132},{5,133},{6,134},{7,135},{8... | collective-permute-start | bytes 1142792 | tf_op jit(solution)/shard_map/ppermute | solution.py:399
  39.5 33.2 %collective-permute-start.2 = (bf16[976,384]{1,0:T(8,128)(2,1)}, bf16[976,384]{1,0:T(8,128)(2,1)S(1)}, u32[]{:S(2)}, u32[]{:S(2)}) collective-permute-start(bf16[976,384]{1,0:T(8,128)(2,1)} %get-tuple-element.42), channel_id=1, source_target_pairs={{0,96},{1,97},{2,98},{3,99},{4,100},{5,101},{6,102},{7,103},{8,104... | collective-permute-start | bytes 2248712 | tf_op jit(solution)/shard_map/ppermute | solution.py:399
  40.9 31.9 %collective-permute-start.3 = (bf16[976,384]{1,0:T(8,128)(2,1)}, bf16[976,384]{1,0:T(8,128)(2,1)S(1)}, u32[]{:S(2)}, u32[]{:S(2)}) collective-permute-start(bf16[976,384]{1,0:T(8,128)(2,1)} %get-tuple-element.43), channel_id=1, source_target_pairs={{0,192},{1,193},{2,194},{3,195},{4,196},{5,197},{6,198},{7,199},{8... | collective-permute-start | bytes 2248712 | tf_op jit(solution)/shard_map/ppermute | solution.py:399
  42.2 46.6 %collective-permute-start.4 = (bf16[976,384]{1,0:T(8,128)(2,1)}, bf16[976,384]{1,0:T(8,128)(2,1)}, u32[]{:S(2)}, u32[]{:S(2)}) collective-permute-start(bf16[976,384]{1,0:T(8,128)(2,1)} %get-tuple-element.44), channel_id=1, source_target_pairs={{0,64},{1,65},{2,66},{3,67},{4,68},{5,69},{6,70},{7,71},{8,72},{9,... | collective-permute-start | bytes 2248712 | tf_op jit(solution)/shard_map/ppermute | solution.py:399
  56.6 32.2 %collective-permute-start.5 = (bf16[976,384]{1,0:T(8,128)(2,1)}, bf16[976,384]{1,0:T(8,128)(2,1)}, u32[]{:S(2)}, u32[]{:S(2)}) collective-permute-start(bf16[976,384]{1,0:T(8,128)(2,1)} %get-tuple-element.45), channel_id=1, source_target_pairs={{0,224},{1,225},{2,226},{3,227},{4,228},{5,229},{6,230},{7,231},{8... | collective-permute-start | bytes 2248712 | tf_op jit(solution)/shard_map/ppermute | solution.py:399
  58.7 31.0 %collective-permute-start.1 = (bf16[976,384]{1,0:T(8,128)(2,1)}, bf16[976,384]{1,0:T(8,128)(2,1)}, u32[]{:S(2)}, u32[]{:S(2)}) collective-permute-start(bf16[976,384]{1,0:T(8,128)(2,1)} %get-tuple-element.46), channel_id=1, source_target_pairs={{0,160},{1,161},{2,162},{3,163},{4,164},{5,165},{6,166},{7,167},{8... | collective-permute-start | bytes 2248712 | tf_op jit(solution)/shard_map/ppermute | solution.py:399
  72.7 17.0 %copy-start.3 = (bf16[976,384]{1,0:T(8,128)(2,1)}, bf16[976,384]{1,0:T(8,128)(2,1)S(1)}, u32[]{:S(2)}) copy-start(bf16[976,384]{1,0:T(8,128)(2,1)S(1)} %collective-permute-done.3) | copy-start | bytes 2248708
  90.5 15.8 %collective-permute-start.7 = (bf16[976,384]{1,0:T(8,128)(2,1)S(1)}, bf16[976,384]{1,0:T(8,128)(2,1)S(1)}, u32[]{:S(2)}, u32[]{:S(2)}) collective-permute-start(bf16[976,384]{1,0:T(8,128)(2,1)S(1)} %fusion.6), channel_id=1, source_target_pairs={{0,24},{1,25},{2,26},{3,27},{4,28},{5,29},{6,30},{7,31},{8,16},{9,... | collective-permute-start | bytes 2248712 | tf_op jit(solution)/shard_map/ppermute | solution.py:430
  110.7 30.1 %all-to-all-start.1 = ((bf16[8,2,64,384]{3,2,1,0:T(8,128)(2,1)}), bf16[8,2,64,384]{3,2,1,0:T(8,128)(2,1)S(1)}, u32[]{:S(2)}, u32[]{:S(2)}) async-start(bf16[8,2,64,384]{3,2,1,0:T(8,128)(2,1)} %forward_transform.3), calls=%async_computation.1 | async-start | bytes 1572864 | tf_op jit(solution)/shard_map/all_to_all | solution.py:407
  120.4 32.6 %collective-permute-start.8 = (bf16[2,480,384]{2,1,0:T(8,128)(2,1)S(1)}, bf16[2,480,384]{2,1,0:T(8,128)(2,1)}, u32[]{:S(2)}, u32[]{:S(2)}) collective-permute-start(bf16[2,480,384]{2,1,0:T(8,128)(2,1)S(1)} %bitcast.76), channel_id=1, source_target_pairs={{16,24},{17,25},{18,26},{19,27},{20,28},{21,29},{22,30},{23,31},{2... | collective-permute-start | bytes 2211848 | tf_op jit(solution)/shard_map/ppermute | solution.py:441
  143.1 20.9 %all-to-all-start.2 = ((bf16[16,15,4,384]{3,2,1,0:T(4,128)(2,1)}), bf16[16,15,4,384]{3,2,1,0:T(4,128)(2,1)S(1)}, u32[]{:S(2)}, u32[]{:S(2)}) async-start(bf16[16,15,4,384]{3,2,1,0:T(4,128)(2,1)} %slice.100), calls=%async_computation.2 | async-start | bytes 1474560 | tf_op jit(solution)/shard_map/all_to_all | solution.py:513
  187.8 86.0 %all-to-all-start.4 = ((bf16[16,15,32,384]{3,2,1,0:T(8,128)(2,1)}), bf16[16,15,32,384]{3,2,1,0:T(8,128)(2,1)}, u32[]{:S(2)}, u32[]{:S(2)}) async-start(bf16[16,15,32,384]{3,2,1,0:T(8,128)(2,1)} %bitcast.74), calls=%async_computation.4 | async-start | bytes 11796480 | tf_op jit(solution)/shard_map/all_to_all | solution.py:531
  193.0 106.7 %all-gather.2.cloned.1.call-start = ((), (), s32[]{:S(2)}) async-start(), calls=%async_computation.6 | async-start | bytes 6635520 | tf_op jit(solution)/shard_map/all_gather | solution.py:539
  194.7 5.5 %collective-permute-start.9 = (bf16[2,64,384]{2,1,0:T(8,128)(2,1)S(1)}, bf16[2,64,384]{2,1,0:T(8,128)(2,1)S(1)}, u32[]{:S(2)}, u32[]{:S(2)}) collective-permute-start(bf16[2,64,384]{2,1,0:T(8,128)(2,1)S(1)} %dynamic-slice_bitcast_fusion.6), channel_id=1, source_target_pairs={{0,32},{32,64},{64,96},{96,128},{128,160},{160,192},{192,224},{224... | collective-permute-start | bytes 294920 | tf_op jit(solution)/shard_map/ppermute | solution.py:418
  200.3 10.7 %collective-permute-start.10 = (bf16[2,64,384]{2,1,0:T(8,128)(2,1)S(1)}, bf16[2,64,384]{2,1,0:T(8,128)(2,1)S(1)}, u32[]{:S(2)}, u32[]{:S(2)}) collective-permute-start(bf16[2,64,384]{2,1,0:T(8,128)(2,1)S(1)} %get-tuple-element.37), channel_id=1, source_target_pairs={{0,224},{32,0},{64,32},{96,64},{128,96},{160,128},{192,160},{224,1... | collective-permute-start | bytes 294920 | tf_op jit(solution)/shard_map/ppermute | solution.py:418
  202.3 19.7 %collective-permute-start.15 = (bf16[2,64,384]{2,1,0:T(8,128)(2,1)S(1)}, bf16[2,64,384]{2,1,0:T(8,128)(2,1)S(1)}, u32[]{:S(2)}, u32[]{:S(2)}) collective-permute-start(bf16[2,64,384]{2,1,0:T(8,128)(2,1)S(1)} %get-tuple-element.32), channel_id=1, source_target_pairs={{0,128},{32,160},{64,192},{96,224},{128,0},{160,32},{192,64},{224,... | collective-permute-start | bytes 294920 | tf_op jit(solution)/shard_map/ppermute | solution.py:418
  206.4 15.6 %collective-permute-start.14 = (bf16[2,64,384]{2,1,0:T(8,128)(2,1)S(1)}, bf16[2,64,384]{2,1,0:T(8,128)(2,1)S(1)}, u32[]{:S(2)}, u32[]{:S(2)}) collective-permute-start(bf16[2,64,384]{2,1,0:T(8,128)(2,1)S(1)} %get-tuple-element.33), channel_id=1, source_target_pairs={{0,160},{32,192},{64,224},{96,0},{128,32},{160,64},{192,96},{224,1... | collective-permute-start | bytes 294920 | tf_op jit(solution)/shard_map/ppermute | solution.py:418
  206.8 15.1 %collective-permute-start.13 = (bf16[2,64,384]{2,1,0:T(8,128)(2,1)S(1)}, bf16[2,64,384]{2,1,0:T(8,128)(2,1)S(1)}, u32[]{:S(2)}, u32[]{:S(2)}) collective-permute-start(bf16[2,64,384]{2,1,0:T(8,128)(2,1)S(1)} %get-tuple-element.34), channel_id=1, source_target_pairs={{0,96},{32,128},{64,160},{96,192},{128,224},{160,0},{192,32},{224,... | collective-permute-start | bytes 294920 | tf_op jit(solution)/shard_map/ppermute | solution.py:418
  209.6 12.3 %collective-permute-start.12 = (bf16[2,64,384]{2,1,0:T(8,128)(2,1)S(1)}, bf16[2,64,384]{2,1,0:T(8,128)(2,1)S(1)}, u32[]{:S(2)}, u32[]{:S(2)}) collective-permute-start(bf16[2,64,384]{2,1,0:T(8,128)(2,1)S(1)} %get-tuple-element.35), channel_id=1, source_target_pairs={{0,192},{32,224},{64,0},{96,32},{128,64},{160,96},{192,128},{224,1... | collective-permute-start | bytes 294920 | tf_op jit(solution)/shard_map/ppermute | solution.py:418
  211.0 9.9 %collective-permute-start.11 = (bf16[2,64,384]{2,1,0:T(8,128)(2,1)S(1)}, bf16[2,64,384]{2,1,0:T(8,128)(2,1)S(1)}, u32[]{:S(2)}, u32[]{:S(2)}) collective-permute-start(bf16[2,64,384]{2,1,0:T(8,128)(2,1)S(1)} %get-tuple-element.36), channel_id=1, source_target_pairs={{0,64},{32,96},{64,128},{96,160},{128,192},{160,224},{192,0},{224,... | collective-permute-start | bytes 294920 | tf_op jit(solution)/shard_map/ppermute | solution.py:418
  284.1 27.8 %copy-start.7 = (f32[8]{0:T(128)S(1)}, f32[8]{0:T(128)}, u32[]{:S(2)}) copy-start(f32[8]{0:T(128)} %param.20) | copy-start | bytes 100
  306.0 11.7 %all-to-all-start.5 = ((f32[16,8,128]{2,1,0:T(8,128)}), f32[16,8,128]{2,1,0:T(8,128)S(1)}, u32[]{:S(2)}, u32[]{:S(2)}) async-start(f32[16,8,128]{2,1,0:T(8,128)} %spread_sums.1), calls=%async_computation.5 | async-start | bytes 131072 | tf_op jit(solution)/shard_map/all_to_all | solution.py:542
  (6 other events, 32.1 us)
Sparse Core Ops, SparseCore 0:
  226.4 73.2 all-gather.1
